TPU v7x, 32 devices: a whole 2x2x4 slice. The times are simulated.
32 devices in a mesh: groups: 2 (over x), gx: 16 (over z, y, core).
Axes of the slice: x: 2, y: 2, z: 4, core: 2. Of those that a mesh axis runs over, the one named last changes fastest.
Arguments:
- hidden: bfloat16 [256, 18432], P('groups', 'gx'), parts along dimension 0, may hold values from -28 to 28, as said below
- w_qkv: bfloat16 [147456, 2688], P('gx'), may hold values from -0.046875 to 0.046875
- w_out: bfloat16 [147456, 2304], P('gx'), may hold values from -0.046875 to 0.046875
- segment_ids: int32 [256], P('groups'), parts along dimension 0, may hold values from 0 to 3, as said below
- end_positions: int32 [8], P('groups'), parts along dimension 0, may hold values from 0 to 127, as said below
- owners: int32 [8], P('groups'), parts along dimension 0, may hold values from 0 to 15, as said below
Outputs:
- mixed: bfloat16 [256, 18432], P('groups', 'gx'), parts along dimension 0
- reward_rows: bfloat16 [64, 18432], P(('groups', 'gx')), parts along dimension 0
There are 2 independent parts, one for each index of `groups`. A program takes and returns all parts, laid end to end along the dimension named above; an argument that names none is the same for every part. Nothing has to cross between parts.
Inputs may be any that keep to these rules, and one draw needn't show every extreme that they name: `hidden`: activations of the span's tokens. `segment_ids`: completion numbers never fall along the span, start at 0 and end at 3, each used by one or more tokens. end_positions[c] is the last token with segment_ids equal to c. `owners`: no device owns more than 2 completions; some device owns exactly 2.
All inputs are finite; a program needn't handle non-finite values.
Results may differ from a plain program's by a relative error of at most 0.012.
Values may be sent and summed in bfloat16 or wider, within the bound.
No kernel may reach another device: no remote copies, remote signals or barrier semaphores. Data moves between devices by JAX's collectives and lax.ppermute only.
A program may use at most 192 MiB of HBM per device.

v0:
```python
import math

import jax
import jax.numpy as jnp
from jax import lax
from jax.sharding import PartitionSpec as P

HD = 192
HPG = 12
KVG = 8
SLOTS = 2


def from_partner(block, axis, distance):
    count = lax.axis_size(axis)
    route = []
    for low in range(count):
        high = low | 1 << distance
        if high != low and high < count:
            route += [(low, high), (high, low)]
    return lax.ppermute(block, axis, route)


def join_pair(mine, partner, upper_bit, axis_number):
    return jnp.where(
        upper_bit == 1,
        jnp.concatenate([partner, mine], axis_number),
        jnp.concatenate([mine, partner], axis_number),
    )


def halve_pick(current, upper_bit, axis_number):
    half_rows = current.shape[axis_number] // 2
    low_half = lax.slice_in_dim(current, 0, half_rows, axis=axis_number)
    high_half = lax.slice_in_dim(current, half_rows, 2 * half_rows, axis=axis_number)
    outgoing = jnp.where(upper_bit == 1, low_half, high_half)
    kept_half = jnp.where(upper_bit == 1, high_half, low_half)
    return (outgoing, kept_half)


def contract_last(left, right):
    return lax.dot_general(
        left, right, (((1,), (1,)), ((), ())), preferred_element_type=jnp.float32
    )


def per_device(hidden, w_qkv, w_out, segment_ids, end_positions, owners):
    devices = lax.axis_size("gx")
    blocks = devices // KVG
    group_bits = KVG.bit_length() - 1
    block_bits = blocks.bit_length() - 1
    my_index = lax.axis_index("gx")
    my_group = my_index % KVG
    my_block = my_index // KVG
    tokens = hidden.shape[0]
    query_width = HPG * HD
    block_rows = tokens // blocks
    scale = 1.0 / math.sqrt(HD)
    features = hidden
    for bit_number in range(group_bits):
        partner = from_partner(features, "gx", bit_number)
        features = join_pair(features, partner, my_group >> bit_number & 1, 1)
    partial_value = jnp.dot(features, w_qkv, preferred_element_type=jnp.float32)
    local_part = partial_value
    for level in reversed(range(block_bits)):
        outgoing, kept_half = halve_pick(local_part, my_block >> level & 1, 0)
        local_part = kept_half + from_partner(outgoing, "gx", group_bits + level)
    query_part = local_part[:, :query_width]
    pair_rows = local_part[:, query_width:].astype(jnp.bfloat16)
    for level in range(block_bits):
        partner = from_partner(pair_rows, "gx", group_bits + level)
        pair_rows = join_pair(pair_rows, partner, my_block >> level & 1, 0)
    key_block = pair_rows[:, :HD]
    value_block = pair_rows[:, HD:]
    queries = query_part.astype(jnp.bfloat16).reshape(block_rows * HPG, HD)
    start = my_block * block_rows
    my_segments = lax.dynamic_slice_in_dim(segment_ids, start, block_rows)
    row_segments = jnp.repeat(my_segments, HPG)
    row_positions = start + jnp.repeat(jnp.arange(block_rows, dtype=jnp.int32), HPG)
    positions = jnp.arange(tokens, dtype=jnp.int32)
    allowed = (row_segments[:, None] == segment_ids[None, :]) & (
        positions[None, :] <= row_positions[:, None]
    )
    scores, allowed = (contract_last(queries, key_block) * scale, allowed)
    row_max = jnp.max(jnp.where(allowed, scores, -jnp.inf), axis=1, keepdims=True)
    weights = jnp.where(allowed, jnp.exp(scores - row_max), 0.0)
    totals = jnp.sum(weights, axis=1, keepdims=True)
    mixed_heads = jnp.dot(
        weights.astype(jnp.bfloat16), value_block, preferred_element_type=jnp.float32
    )
    attended = (mixed_heads / totals).astype(jnp.bfloat16).reshape(block_rows, query_width)
    for level in range(block_bits):
        partner = from_partner(attended, "gx", group_bits + level)
        attended = join_pair(attended, partner, my_block >> level & 1, 0)
    output_part = contract_last(attended, w_out)
    for bit_number in reversed(range(group_bits)):
        outgoing, kept_half = halve_pick(output_part, my_group >> bit_number & 1, 1)
        output_part = kept_half + from_partner(outgoing, "gx", bit_number)
    mixed = output_part.astype(jnp.bfloat16)
    picker = (end_positions[:, None] == jnp.arange(tokens, dtype=jnp.int32)[None, :]).astype(
        jnp.bfloat16
    )
    end_local = jnp.dot(picker, mixed, preferred_element_type=jnp.float32).astype(jnp.bfloat16)
    end_full = lax.all_gather(end_local, "gx", axis=1, tiled=True)
    completions = owners.shape[0]
    same_owner = owners[:, None] == owners[None, :]
    earlier = jnp.arange(completions)[None, :] < jnp.arange(completions)[:, None]
    order_rank = jnp.sum((same_owner & earlier).astype(jnp.int32), axis=1)
    chooser = (
        (owners[None, :] == my_index)
        & (order_rank[None, :] == jnp.arange(SLOTS, dtype=jnp.int32)[:, None])
    ).astype(jnp.bfloat16)
    reward_rows = jnp.dot(chooser, end_full, preferred_element_type=jnp.float32).astype(
        jnp.bfloat16
    )
    return (mixed, reward_rows)


def solution(mesh):
    placed = (
        P("groups", "gx"),
        P("gx", None),
        P("gx", None),
        P("groups"),
        P("groups"),
        P("groups"),
    )
    return jax.shard_map(
        per_device,
        mesh=mesh,
        in_specs=placed,
        out_specs=(P("groups", "gx"), P(("groups", "gx"), None)),
        check_vma=False,
    )
```

profile of v0, /device:TPU:0, one launch (start us, length us, event | category | flops | bytes accessed | tf_op | source)
XLA Modules:
  0.0 250.8 jit_solution(1884915637712830596)
XLA Ops:
  0.6 0.5 collective-permute-start
  1.1 1.4 collective-permute-done
  2.6 1.3 maximum_select_fusion.3
  3.9 3.0 %collective-permute-start.1 = (bf16[128,2304]{1,0:T(8,128)(2,1)S(1)}, bf16[128,2304]{1,0:T(8,128)(2,1)S(1)}, u32[]{:S(2)}, u32[]{:S(2)}) collective-permute-start(bf16[128,2304]{1,0:T(8,128)(2,1)S(1)} %maximum_select_fusion.3), channel_id=1, source_target_pairs={{0,2},{2,0},{1,3},{3,1},{4,6},{6,4},{5,7},{7,5},{8,10},{10,8},{9,1... | collective-permute-start | bytes 1769480 | tf_op jit(solution)/shard_map/ppermute | solution.py:21
  6.8 13.6 %collective-permute-done.1 = bf16[128,2304]{1,0:T(8,128)(2,1)S(1)} collective-permute-done((bf16[128,2304]{1,0:T(8,128)(2,1)S(1)}, bf16[128,2304]{1,0:T(8,128)(2,1)S(1)}, u32[]{:S(2)}, u32[]{:S(2)}) %collective-permute-start.1) | collective-permute-done | bytes 589856 | tf_op jit(solution)/shard_map/ppermute | solution.py:21
  20.5 0.3 maximum_select_fusion.2
  20.7 1.9 collective-permute-start.2
  22.6 25.8 %collective-permute-done.2 = bf16[128,4608]{1,0:T(8,128)(2,1)} collective-permute-done((bf16[128,4608]{1,0:T(8,128)(2,1)S(1)}, bf16[128,4608]{1,0:T(8,128)(2,1)}, u32[]{:S(2)}, u32[]{:S(2)}) %collective-permute-start.2) | collective-permute-done | bytes 1179680 | tf_op jit(solution)/shard_map/ppermute | solution.py:21
  48.4 22.6 %fusion = f32[128,2688]{1,0:T(8,128)S(1)} fusion(bf16[9216,2688]{1,0:T(8,128)(2,1)} %param.7, bf16[128,4608]{1,0:T(8,128)(2,1)S(1)} %maximum_select_fusion.2, bf16[128,4608]{1,0:T(8,128)(2,1)} %collective-permute-done.2, pred[]{:T(512)S(6)} %eq.43), kind=kOutput, calls=%fused_computation.2 | convolution fusion | flops 6352404480 | bytes 53280768 | tf_op jit(solution)/shard_map/dot_general | solution.py:63
  71.0 2.6 %collective-permute-start.3 = (f32[64,2688]{1,0:T(8,128)S(1)}, f32[64,2688]{1,0:T(8,128)S(1)}, u32[]{:S(2)}, u32[]{:S(2)}) collective-permute-start(f32[64,2688]{1,0:T(8,128)S(1)} %slice_select_fusion.2), channel_id=1, source_target_pairs={{0,8},{8,0},{1,9},{9,1},{2,10},{10,2},{3,11},{11,3},{4,12},{12,4},... | collective-permute-start | bytes 2064392 | tf_op jit(solution)/shard_map/ppermute | solution.py:21
  73.6 29.2 %collective-permute-done.3 = f32[64,2688]{1,0:T(8,128)S(1)} collective-permute-done((f32[64,2688]{1,0:T(8,128)S(1)}, f32[64,2688]{1,0:T(8,128)S(1)}, u32[]{:S(2)}, u32[]{:S(2)}) %collective-permute-start.3) | collective-permute-done | bytes 688160 | tf_op jit(solution)/shard_map/ppermute | solution.py:21
  103.2 0.1 eq.88
  103.4 0.5 reshape.28
  103.9 4.6 %collective-permute-done.4 = bf16[64,384]{1,0:T(8,128)(2,1)S(1)} collective-permute-done((bf16[64,384]{1,0:T(8,128)(2,1)S(1)}, bf16[64,384]{1,0:T(8,128)(2,1)S(1)}, u32[]{:S(2)}, u32[]{:S(2)}) %collective-permute-start.4) | collective-permute-done | bytes 49184 | tf_op jit(solution)/shard_map/ppermute | solution.py:21
  108.5 0.3 select_reduce_fusion
  108.9 0.2 fusion.16
  109.0 0.4 fusion.7
  109.4 0.2 copy.9
  109.6 0.4 reshape.29
  110.0 13.8 %collective-permute-done.5 = bf16[64,2304]{1,0:T(8,128)(2,1)S(1)} collective-permute-done((bf16[64,2304]{1,0:T(8,128)(2,1)S(1)}, bf16[64,2304]{1,0:T(8,128)(2,1)S(1)}, u32[]{:S(2)}, u32[]{:S(2)}) %collective-permute-start.5) | collective-permute-done | bytes 294944 | tf_op jit(solution)/shard_map/ppermute | solution.py:21
  123.8 21.4 %fusion.8 = f32[128,9216]{1,0:T(8,128)} fusion(bf16[9216,2304]{1,0:T(8,128)(2,1)} %param.8, bf16[64,2304]{1,0:T(8,128)(2,1)S(1)} %reshape.29, bf16[64,2304]{1,0:T(8,128)(2,1)S(1)} %collective-permute-done.5, pred[]{:T(512)S(6)} %eq.44), kind=kOutput, calls=%fused_computation.22 | convolution fusion | flops 5438472192 | bytes 47775744 | tf_op jit(solution)/shard_map/dot_general | solution.py:42
  145.3 2.8 %slice_select_fusion = f32[128,4608]{1,0:T(8,128)S(1)} fusion(f32[128,9216]{1,0:T(8,128)} %fusion.8, pred[]{:T(512)S(6)} %eq.43), kind=kLoop, calls=%fused_computation.10 | loop fusion | flops 589824 | bytes 7077889 | tf_op jit(solution)/shard_map/jit(_where)/select_n | solution.py:36
  148.1 52.0 %collective-permute-done.6 = f32[128,4608]{1,0:T(8,128)S(1)} collective-permute-done((f32[128,4608]{1,0:T(8,128)S(1)}, f32[128,4608]{1,0:T(8,128)S(1)}, u32[]{:S(2)}, u32[]{:S(2)}) %collective-permute-start.6) | collective-permute-done | bytes 2359328 | tf_op jit(solution)/shard_map/ppermute | solution.py:21
  200.2 0.3 select_add_fusion
  200.5 0.1 slice_select_fusion.1
  200.7 25.8 %collective-permute-done.7 = f32[128,2304]{1,0:T(8,128)S(1)} collective-permute-done((f32[128,2304]{1,0:T(8,128)S(1)}, f32[128,2304]{1,0:T(8,128)S(1)}, u32[]{:S(2)}, u32[]{:S(2)}) %collective-permute-start.7) | collective-permute-done | bytes 1179680 | tf_op jit(solution)/shard_map/ppermute | solution.py:21
  226.5 0.2 select_add_fusion.1
  226.9 0.2 convert_reduce_fusion
  227.1 1.8 collective-permute-done.8
  229.0 0.2 convolution_convert_fusion.1
  229.2 20.8 %all_gather.3 = bf16[4,18432]{1,0:T(4,128)(2,1)S(1)} all-gather(bf16[4,1152]{1,0:T(4,128)(2,1)S(1)} %convolution_convert_fusion.1), channel_id=1, replica_groups=mesh['groups'=2,'gx'=16] {'gx'}, dimensions={1}, use_global_device_ids=true | all-gather | bytes 156672 | tf_op jit(solution)/shard_map/all_gather | solution.py:104
  250.0 0.9 convolution_convert_fusion
  (27 shorter events, 1.0 us)
Async XLA Ops:
  0.6 1.9 collective-permute-start
  3.9 16.6 %collective-permute-start.1 = (bf16[128,2304]{1,0:T(8,128)(2,1)S(1)}, bf16[128,2304]{1,0:T(8,128)(2,1)S(1)}, u32[]{:S(2)}, u32[]{:S(2)}) collective-permute-start(bf16[128,2304]{1,0:T(8,128)(2,1)S(1)} %maximum_select_fusion.3), channel_id=1, source_target_pairs={{0,2},{2,0},{1,3},{3,1},{4,6},{6,4},{5,7},{7,5},{8,10},{10,8},{9,1... | collective-permute-start | bytes 1769480 | tf_op jit(solution)/shard_map/ppermute | solution.py:21
  20.7 27.7 %collective-permute-start.2 = (bf16[128,4608]{1,0:T(8,128)(2,1)S(1)}, bf16[128,4608]{1,0:T(8,128)(2,1)}, u32[]{:S(2)}, u32[]{:S(2)}) collective-permute-start(bf16[128,4608]{1,0:T(8,128)(2,1)S(1)} %maximum_select_fusion.2), channel_id=1, source_target_pairs={{0,4},{4,0},{1,5},{5,1},{2,6},{6,2},{3,7},{7,3},{8,12},{12,8},{9,1... | collective-permute-start | bytes 3538952 | tf_op jit(solution)/shard_map/ppermute | solution.py:21
  71.0 32.1 %copy-start.2 = (s32[128]{0:T(128)S(1)}, s32[128]{0:T(128)}, u32[]{:S(2)}) copy-start(s32[128]{0:T(128)} %param.9) | copy-start | bytes 1540
  71.0 31.8 %collective-permute-start.3 = (f32[64,2688]{1,0:T(8,128)S(1)}, f32[64,2688]{1,0:T(8,128)S(1)}, u32[]{:S(2)}, u32[]{:S(2)}) collective-permute-start(f32[64,2688]{1,0:T(8,128)S(1)} %slice_select_fusion.2), channel_id=1, source_target_pairs={{0,8},{8,0},{1,9},{9,1},{2,10},{10,2},{3,11},{11,3},{4,12},{12,4},... | collective-permute-start | bytes 2064392 | tf_op jit(solution)/shard_map/ppermute | solution.py:21
  102.9 5.6 %collective-permute-start.4 = (bf16[64,384]{1,0:T(8,128)(2,1)S(1)}, bf16[64,384]{1,0:T(8,128)(2,1)S(1)}, u32[]{:S(2)}, u32[]{:S(2)}) collective-permute-start(bf16[64,384]{1,0:T(8,128)(2,1)S(1)} %slice.53), channel_id=1, source_target_pairs={{0,8},{8,0},{1,9},{9,1},{2,10},{10,2},{3,11},{11,3},{4,12},{12,4},... | collective-permute-start | bytes 147464 | tf_op jit(solution)/shard_map/ppermute | solution.py:21
  110.0 13.9 %collective-permute-start.5 = (bf16[64,2304]{1,0:T(8,128)(2,1)S(1)}, bf16[64,2304]{1,0:T(8,128)(2,1)S(1)}, u32[]{:S(2)}, u32[]{:S(2)}) collective-permute-start(bf16[64,2304]{1,0:T(8,128)(2,1)S(1)} %reshape.29), channel_id=1, source_target_pairs={{0,8},{8,0},{1,9},{9,1},{2,10},{10,2},{3,11},{11,3},{4,12},{12,4},... | collective-permute-start | bytes 884744 | tf_op jit(solution)/shard_map/ppermute | solution.py:21
  145.3 54.9 %copy-start = (f32[128,9216]{1,0:T(8,128)S(1)}, f32[128,9216]{1,0:T(8,128)}, u32[]{:S(2)}) copy-start(f32[128,9216]{1,0:T(8,128)} %fusion.8) | copy-start | bytes 14155780
  148.1 52.1 %collective-permute-start.6 = (f32[128,4608]{1,0:T(8,128)S(1)}, f32[128,4608]{1,0:T(8,128)S(1)}, u32[]{:S(2)}, u32[]{:S(2)}) collective-permute-start(f32[128,4608]{1,0:T(8,128)S(1)} %slice_select_fusion), channel_id=1, source_target_pairs={{0,4},{4,0},{1,5},{5,1},{2,6},{6,2},{3,7},{7,3},{8,12},{12,8},{9,1... | collective-permute-start | bytes 7077896 | tf_op jit(solution)/shard_map/ppermute | solution.py:21
  200.6 26.3 %copy-start.3 = (s32[4]{0:T(128)S(1)}, s32[4]{0:T(128)}, u32[]{:S(2)}) copy-start(s32[4]{0:T(128)} %param.11) | copy-start | bytes 52
  200.6 25.9 %collective-permute-start.7 = (f32[128,2304]{1,0:T(8,128)S(1)}, f32[128,2304]{1,0:T(8,128)S(1)}, u32[]{:S(2)}, u32[]{:S(2)}) collective-permute-start(f32[128,2304]{1,0:T(8,128)S(1)} %slice_select_fusion.1), channel_id=1, source_target_pairs={{0,2},{2,0},{1,3},{3,1},{4,6},{6,4},{5,7},{7,5},{8,10},{10,8},{9,1... | collective-permute-start | bytes 3538952 | tf_op jit(solution)/shard_map/ppermute | solution.py:21
  226.7 2.3 copy-start.4
  226.8 2.1 collective-permute-start.8
  229.0 21.8 %copy-start.1 = (bf16[128,1152]{1,0:T(8,128)(2,1)}, bf16[128,1152]{1,0:T(8,128)(2,1)S(1)}, u32[]{:S(2)}) copy-start(bf16[128,1152]{1,0:T(8,128)(2,1)S(1)} %add_convert_fusion.1) | copy-start | bytes 884740
where the time goes:
time: 251 us
  waiting for transfers between devices  168 us (67%)
  matrix products  45.7 us (18%)
  blocking collectives  20.8 us (8%)
  starting transfers between devices  8.25 us (3%)
  other arithmetic  5.69 us (2%)
    ppermute x9, waiting for transfers between devices, from_partner(): return lax.ppermute(block, axis, route)  168 us
    dot_general x1, matrix products, per_device(): partial_value = jnp.dot(features, w_qkv, preferred_element_type=jnp.float32)  22.6 us
    dot_general x2, matrix products, contract_last(): lax.dot_general(left, right, (((1,), (1,)), ((), ())), preferred_element_...  21.8 us
    all_gather x1, blocking collectives, per_device(): end_full = lax.all_gather(end_local, 'gx', axis=1, tiled=True)  20.8 us
    ppermute x9, starting transfers between devices, from_partner(): return lax.ppermute(block, axis, route)  8.25 us
  transfers between devices with their start and end apart: 9, of which 9 were waited for; matrix products, arithmetic and copies ran while one was open for 0% of the time, Pallas kernels for 0%

commit v1 on v0

--- a/solution.py
+++ b/solution.py
@@ -3,6 +3,8 @@
 import jax
 import jax.numpy as jnp
 from jax import lax
+from jax.experimental import pallas as pl
+from jax.experimental.pallas import tpu as pltpu
 from jax.sharding import PartitionSpec as P
 
 HD = 192
@@ -44,7 +46,7 @@
     )
 
 
-def per_device(hidden, w_qkv, w_out, segment_ids, end_positions, owners):
+def general_device(hidden, w_qkv, w_out, segment_ids, end_positions, owners):
     devices = lax.axis_size("gx")
     blocks = devices // KVG
     group_bits = KVG.bit_length() - 1
@@ -116,6 +118,262 @@
     return (mixed, reward_rows)
 
 
+CHUNKS = (4, 4, 4)
+VMEM_BYTES = 50 * 1024 * 1024
+
+
+def xor_swap(block, distance):
+    count = lax.axis_size("gx")
+    return lax.ppermute(block, "gx", [(low, low ^ distance) for low in range(count)])
+
+
+def in_vmem():
+    return pl.BlockSpec(memory_space=pltpu.VMEM)
+
+
+def project(features, distances, running, w_qkv, my_group):
+    tokens, width = features[0].shape
+    columns = w_qkv.shape[1]
+    count = len(features)
+    block_ids = jnp.stack([my_group ^ d for d in distances]).astype(jnp.int32)
+
+    def kernel(ids_ref, *refs):
+        feature_refs = refs[:count]
+        w_ref = refs[count]
+        start_ref = refs[count + 1] if running is not None else None
+        out_ref, current = refs[-2:]
+        step = pl.program_id(0)
+        for i in range(count):
+
+            @pl.when(step == i)
+            def _():
+                current[...] = feature_refs[i][...]
+
+        @pl.when(step == 0)
+        def _():
+            out_ref[...] = jnp.zeros_like(out_ref) if start_ref is None else start_ref[...]
+
+        out_ref[...] += jnp.dot(current[...], w_ref[...], preferred_element_type=jnp.float32)
+
+    whole = pl.BlockSpec((tokens, width), lambda i, ids: (0, 0))
+    total = pl.BlockSpec((tokens, columns), lambda i, ids: (0, 0))
+    operands = list(features) + [w_qkv] + ([] if running is None else [running])
+    return pl.pallas_call(
+        kernel,
+        grid_spec=pltpu.PrefetchScalarGridSpec(
+            num_scalar_prefetch=1,
+            grid=(count,),
+            in_specs=[whole] * count
+            + [pl.BlockSpec((width, columns), lambda i, ids: (ids[i], 0))]
+            + ([] if running is None else [total]),
+            out_specs=total,
+            scratch_shapes=[pltpu.VMEM((tokens, width), jnp.bfloat16)],
+        ),
+        out_shape=jax.ShapeDtypeStruct((tokens, columns), jnp.float32),
+        compiler_params=pltpu.CompilerParams(vmem_limit_bytes=VMEM_BYTES),
+        cost_estimate=pl.CostEstimate(
+            flops=2 * count * tokens * width * columns,
+            bytes_accessed=2 * count * width * columns,
+            transcendentals=0,
+        ),
+        name="project",
+    )(block_ids, *operands)
+
+
+def attend_and_mix(own_queries, partner_queries, keys, values, allowed, running, w_out, first, my_group, last, picker):
+    tokens, chunk_width = own_queries.shape
+    heads = chunk_width // HD
+    rows = w_out.shape[0] // KVG
+    block_ids = (my_group ^ jnp.arange(KVG, dtype=jnp.int32)).astype(jnp.int32)
+    scale = 1.0 / math.sqrt(HD)
+    column_block = first * HD // chunk_width
+
+    def kernel(ids_ref, own_ref, partner_ref, key_ref, value_ref, allowed_ref, w_ref, *refs):
+        refs = list(refs)
+        start_ref = refs.pop(0) if running is not None else None
+        picker_ref = refs.pop(0) if last else None
+        out_ref = refs.pop(0)
+        end_ref = refs.pop(0) if last else None
+        attended = refs.pop(0)
+        step = pl.program_id(0)
+
+        @pl.when(step == 0)
+        def _():
+            queries = (own_ref[...] + partner_ref[...].astype(jnp.float32)).astype(jnp.bfloat16)
+            mask = allowed_ref[...] > 0.0
+            for head in range(heads):
+                lanes = slice(head * HD, (head + 1) * HD)
+                scores = contract_last(queries[:, lanes], key_ref[...]) * scale
+                row_max = jnp.max(jnp.where(mask, scores, -jnp.inf), axis=1, keepdims=True)
+                weights = jnp.where(mask, jnp.exp(scores - row_max), 0.0)
+                totals = jnp.sum(weights, axis=1, keepdims=True)
+                mixed_heads = jnp.dot(
+                    weights.astype(jnp.bfloat16), value_ref[...], preferred_element_type=jnp.float32
+                )
+                attended[:, lanes] = (mixed_heads / totals).astype(jnp.bfloat16)
+
+        part = contract_last(attended[...], w_ref[...])
+        if start_ref is not None:
+            part += start_ref[step]
+        out_ref[step] = part.astype(out_ref.dtype)
+        if last:
+            end_ref[step] = jnp.dot(
+                picker_ref[...], part.astype(jnp.bfloat16), preferred_element_type=jnp.float32
+            )
+
+    def whole(shape):
+        return pl.BlockSpec(shape, lambda i, ids: (0,) * len(shape))
+
+    out_dims = (KVG, tokens, rows)
+    out_shape = [jax.ShapeDtypeStruct(out_dims, jnp.bfloat16 if last else jnp.float32)]
+    out_specs = [whole(out_dims)]
+    operands = [own_queries, partner_queries, keys, values, allowed, w_out]
+    in_specs = [whole(o.shape) for o in operands[:-1]]
+    in_specs.append(pl.BlockSpec((rows, chunk_width), lambda i, ids: (ids[i], column_block)))
+    if running is not None:
+        operands.append(running)
+        in_specs.append(whole(out_dims))
+    if last:
+        operands.append(picker)
+        in_specs.append(whole(picker.shape))
+        end_dims = (KVG, picker.shape[0], rows)
+        out_shape.append(jax.ShapeDtypeStruct(end_dims, jnp.float32))
+        out_specs.append(whole(end_dims))
+    result = pl.pallas_call(
+        kernel,
+        grid_spec=pltpu.PrefetchScalarGridSpec(
+            num_scalar_prefetch=1,
+            grid=(KVG,),
+            in_specs=in_specs,
+            out_specs=out_specs,
+            scratch_shapes=[pltpu.VMEM((tokens, chunk_width), jnp.bfloat16)],
+        ),
+        out_shape=out_shape,
+        compiler_params=pltpu.CompilerParams(vmem_limit_bytes=VMEM_BYTES),
+        cost_estimate=pl.CostEstimate(
+            flops=2 * KVG * tokens * rows * chunk_width,
+            bytes_accessed=2 * KVG * rows * chunk_width,
+            transcendentals=heads * tokens * tokens,
+        ),
+        name="attend_and_mix",
+    )(block_ids, *operands)
+    return result if last else result[0]
+
+
+def swap_blocks(blocks, distance):
+    return [blocks[j ^ distance] for j in range(len(blocks))]
+
+
+def natural_order(blocks, my_group):
+    distance = 1
+    while distance < len(blocks):
+        bit = my_group // distance % 2 == 1
+        swapped = swap_blocks(blocks, distance)
+        blocks = [jnp.where(bit, other, own) for own, other in zip(blocks, swapped)]
+        distance *= 2
+    return jnp.concatenate(blocks, axis=-1)
+
+
+def pair_device(hidden, w_qkv, w_out, segment_ids, end_positions, owners):
+    my_index = lax.axis_index("gx")
+    my_group = my_index % KVG
+    my_block = my_index // KVG
+    tokens = hidden.shape[0]
+    query_width = HPG * HD
+    positions = jnp.arange(tokens, dtype=jnp.int32)
+    allowed = (
+        (segment_ids[:, None] == segment_ids[None, :]) & (positions[None, :] <= positions[:, None])
+    ).astype(jnp.float32)
+    completions = owners.shape[0]
+    end_rows = -(-completions // 8) * 8
+    picker = (
+        jnp.pad(end_positions, (0, end_rows - completions), constant_values=-1)[:, None] == positions[None, :]
+    ).astype(jnp.bfloat16)
+
+    features = {0: hidden}
+    for distance in range(2, KVG, 2):
+        features[distance] = xor_swap(hidden, distance)
+    for distance in range(0, KVG, 2):
+        features[distance + 1] = xor_swap(features[distance], 1)
+    early, late = (0, 1), tuple(range(2, KVG))
+    partial = project([features[d] for d in early], early, None, w_qkv, my_group)
+    partial = project([features[d] for d in late], late, partial, w_qkv, my_group)
+
+    rounded = partial.astype(jnp.bfloat16)
+    lanes = []
+    low = 0
+    for heads in CHUNKS:
+        lanes.append((low, low + heads * HD))
+        low += heads * HD
+    partner_kv = xor_swap(rounded[:, query_width:], KVG)
+    partner_queries = [xor_swap(rounded[:, low:high], KVG) for low, high in lanes]
+    pair = (partial[:, query_width:] + partner_kv.astype(jnp.float32)).astype(jnp.bfloat16)
+    keys, values = pair[:, :HD], pair[:, HD:]
+    running = None
+    for number, (low, high) in enumerate(lanes):
+        last = number == len(lanes) - 1
+        running = attend_and_mix(
+            partial[:, low:high],
+            partner_queries[number],
+            keys,
+            values,
+            allowed,
+            running,
+            w_out,
+            low // HD,
+            my_group,
+            last,
+            picker,
+        )
+    parts, end_parts = running
+
+    end_parts = end_parts[:, :completions].astype(jnp.bfloat16)
+    near = [end_parts[j].astype(jnp.float32) for j in range(0, KVG, 2)]
+    far = xor_swap(end_parts[1::2], 1).astype(jnp.float32)
+    near = [(mine + far[i]) for i, mine in enumerate(near)]
+    message = jnp.stack(near).astype(jnp.bfloat16)
+    ends = list(near)
+    for distance in range(2, KVG, 2):
+        arrived = xor_swap(message, distance).astype(jnp.float32)
+        arrived = swap_blocks([arrived[i] for i in range(KVG // 2)], distance // 2)
+        ends = [a + b for a, b in zip(ends, arrived)]
+    ends = jnp.stack(ends).astype(jnp.bfloat16)
+    both = jnp.stack([ends, xor_swap(ends, KVG)])
+    both_far = xor_swap(both, 1)
+    halves = []
+    for half in range(2):
+        blocks = []
+        for i in range(KVG // 2):
+            blocks += [both[half, i], both_far[half, i]]
+        halves.append(natural_order(blocks, my_group))
+    end_full = jnp.concatenate(
+        [jnp.where(my_block == 0, halves[0], halves[1]), jnp.where(my_block == 0, halves[1], halves[0])], axis=-1
+    )
+    same_owner = owners[:, None] == owners[None, :]
+    earlier = jnp.arange(completions)[None, :] < jnp.arange(completions)[:, None]
+    order_rank = jnp.sum((same_owner & earlier).astype(jnp.int32), axis=1)
+    chooser = (
+        (owners[None, :] == my_index)
+        & (order_rank[None, :] == jnp.arange(SLOTS, dtype=jnp.int32)[:, None])
+    ).astype(jnp.bfloat16)
+    reward_rows = jnp.dot(chooser, end_full, preferred_element_type=jnp.float32).astype(jnp.bfloat16)
+
+    arrived = xor_swap(parts[1::2], 1)
+    near = parts[0::2].astype(jnp.float32) + arrived.astype(jnp.float32)
+    mixed = near[0]
+    for distance in range(2, KVG, 2):
+        mixed += xor_swap(near[distance // 2].astype(jnp.bfloat16), distance).astype(jnp.float32)
+    return (mixed.astype(jnp.bfloat16), reward_rows)
+
+
+def per_device(hidden, w_qkv, w_out, segment_ids, end_positions, owners):
+    tokens, width = hidden.shape
+    blocks = lax.axis_size("gx") // KVG
+    if blocks == 2 and width % 128 == 0 and tokens % 16 == 0 and tokens <= 128:
+        return pair_device(hidden, w_qkv, w_out, segment_ids, end_positions, owners)
+    return general_device(hidden, w_qkv, w_out, segment_ids, end_positions, owners)
+
+
 def solution(mesh):
     placed = (
         P("groups", "gx"),

time: 251 us -> 153 us (0.61)
  waiting for transfers between devices: 168 us -> 60.7 us
  Pallas kernels: 0 us -> 63.1 us
  matrix products: 45.7 us -> 0.86 us
  blocking collectives: 20.8 us -> 0 us
  starting transfers between devices: 8.25 us -> 20.5 us
  other arithmetic: 5.69 us -> 3.18 us
    ppermute x9 -> x21, waiting for transfers between devices: 168 us -> 60.7 us  [xor_swap(): lax.ppermute(block, 'gx', [(low, low ^ distance) for low in range(count)])]
    pallas_call x0 -> x5, Pallas kernels: none -> 63.1 us  [the longest x3 41.6 us: attend_and_mix(): pl.pallas_call(kernel, grid_spec=pltpu.PrefetchScalarGridSpec(num_scalar_...]
    dot_general x6 -> x1, matrix products: 45.7 us -> 0.86 us  [pair_device(): jnp.dot(chooser, end_full, preferred_element_type=jnp.float32)]
    all_gather x1 -> x0, blocking collectives: 20.8 us -> none  [per_device(): end_full = lax.all_gather(end_local, 'gx', axis=1, tiled=True)]
    ppermute x9 -> x21, starting transfers between devices: 8.25 us -> 20.5 us  [xor_swap(): lax.ppermute(block, 'gx', [(low, low ^ distance) for low in range(count)])]
    select_n x7 -> x1, other arithmetic: 4.61 us -> 0.06 us  [pair_device(): jnp.where(my_block == 0, halves[0], halves[1])]
  transfers between devices with their start and end apart: 9 -> 21, of which waited for: 9 -> 15; matrix products, arithmetic and copies ran while one was open for 0% -> 2% of each run, Pallas kernels for 0% -> 23%
where the time goes in v1:
time: 153 us; the launch traced here: 152 us
  Pallas kernels  63.1 us (41%)
  waiting for transfers between devices  60.7 us (40%)
  starting transfers between devices  20.5 us (13%)
  local copies, waits for them, and re-layouts  3.22 us (2%)
  other arithmetic  3.18 us (2%)
    ppermute x21, waiting for transfers between devices, xor_swap(): lax.ppermute(block, 'gx', [(low, low ^ distance) for low in range(count)])  60.7 us
    pallas_call x3, Pallas kernels, attend_and_mix(): pl.pallas_call(kernel, grid_spec=pltpu.PrefetchScalarGridSpec(num_scalar_...  41.6 us
    pallas_call x2, Pallas kernels, project(): pl.pallas_call(kernel, grid_spec=pltpu.PrefetchScalarGridSpec(num_scalar_...  21.5 us
    ppermute x21, starting transfers between devices, xor_swap(): lax.ppermute(block, 'gx', [(low, low ^ distance) for low in range(count)])  20.5 us
  transfers between devices with their start and end apart: 21, of which 15 were waited for; matrix products, arithmetic and copies ran while one was open for 2% of the time, Pallas kernels for 23%

profile of v1, /device:TPU:0, one launch (start us, length us, event | category | flops | bytes accessed | tf_op | source)
XLA Modules:
  0.0 152.4 jit_solution(1643939188858550339)
XLA Ops:
  0.6 3.0 %collective-permute-start = (bf16[128,1152]{1,0:T(8,128)(2,1)}, bf16[128,1152]{1,0:T(8,128)(2,1)S(1)}, u32[]{:S(2)}, u32[]{:S(2)}) collective-permute-start(bf16[128,1152]{1,0:T(8,128)(2,1)} %refs_0_.1), channel_id=1, source_target_pairs={{0,2},{1,3},{2,0},{3,1},{4,6},{5,7},{6,4},{7,5},{8,10},{9,11},{10,... | collective-permute-start | bytes 884744 | tf_op jit(solution)/shard_map/ppermute | solution.py:127
  3.7 1.6 %collective-permute-start.2 = (bf16[128,1152]{1,0:T(8,128)(2,1)}, bf16[128,1152]{1,0:T(8,128)(2,1)S(1)}, u32[]{:S(2)}, u32[]{:S(2)}) collective-permute-start(bf16[128,1152]{1,0:T(8,128)(2,1)} %refs_0_.1), channel_id=1, source_target_pairs={{0,4},{1,5},{2,6},{3,7},{4,0},{5,1},{6,2},{7,3},{8,12},{9,13},{10,... | collective-permute-start | bytes 884744 | tf_op jit(solution)/shard_map/ppermute | solution.py:127
  6.8 4.1 %collective-permute-done.refs_0_ = bf16[128,1152]{1,0:T(8,128)(2,1)S(1)} collective-permute-done((bf16[128,1152]{1,0:T(8,128)(2,1)}, bf16[128,1152]{1,0:T(8,128)(2,1)S(1)}, u32[]{:S(2)}, u32[]{:S(2)}) %collective-permute-start) | collective-permute-done | bytes 294944 | tf_op jit(solution)/shard_map/ppermute | solution.py:127
  10.9 2.9 %collective-permute-done.2.refs_2_ = bf16[128,1152]{1,0:T(8,128)(2,1)S(1)} collective-permute-done((bf16[128,1152]{1,0:T(8,128)(2,1)}, bf16[128,1152]{1,0:T(8,128)(2,1)S(1)}, u32[]{:S(2)}, u32[]{:S(2)}) %collective-permute-start.2) | collective-permute-done | bytes 294944 | tf_op jit(solution)/shard_map/ppermute | solution.py:127
  13.8 4.7 %collective-permute-done.4.refs_4_ = bf16[128,1152]{1,0:T(8,128)(2,1)S(1)} collective-permute-done((bf16[128,1152]{1,0:T(8,128)(2,1)}, bf16[128,1152]{1,0:T(8,128)(2,1)S(1)}, u32[]{:S(2)}, u32[]{:S(2)}) %collective-permute-start.4) | collective-permute-done | bytes 294944 | tf_op jit(solution)/shard_map/ppermute | solution.py:127
  18.6 1.0 copy-done.1
  19.6 6.3 %project.2.refs_7_ = f32[128,2688]{1,0:T(8,128)S(1)} custom-call(s32[2]{0:T(128)S(1)} %pad_add_fusion.ids_ref, bf16[128,1152]{1,0:T(8,128)(2,1)S(1)} %copy-done.1, bf16[128,1152]{1,0:T(8,128)(2,1)S(1)} %collective-permute-done.6.refs_1_, bf16[9216,2688]{1,0:T(8,128)(2,1)} %refs_6_.1), custom_call_target="tpu_custom_call" | custom-call | flops 1585446912 | bytes 12386304 | tf_op jit(solution)/shard_map/project/pallas_call | solution.py:161
  25.9 1.1 copy-done
  27.0 15.2 %project.3 = f32[128,2688]{1,0:T(8,128)S(1)} custom-call(s32[6]{0:T(128)S(1)} %stack.69.ids_ref, bf16[128,1152]{1,0:T(8,128)(2,1)S(1)} %collective-permute-done.refs_0_, bf16[128,1152]{1,0:T(8,128)(2,1)S(1)} %collective-permute-done.1.refs_1_, bf16[128,1152]{1,0:T(8,128)(2,1)S(1)} %collective-permute-done.2.refs_2_, ...), custom_call_target="tpu_custom_call" | custom-call | flops 4756340736 | bytes 37158912 | tf_op jit(solution)/shard_map/project/pallas_call | solution.py:161
  42.4 2.8 %collective-permute-start.8 = (bf16[128,384]{1,0:T(8,128)(2,1)S(1)}, bf16[128,384]{1,0:T(8,128)(2,1)S(1)}, u32[]{:S(2)}, u32[]{:S(2)}) collective-permute-start(bf16[128,384]{1,0:T(8,128)(2,1)S(1)} %slice.215), channel_id=1, source_target_pairs={{0,8},{1,9},{2,10},{3,11},{4,12},{5,13},{6,14},{7,15},{8,0},{9,1},... | collective-permute-start | bytes 294920 | tf_op jit(solution)/shard_map/ppermute | solution.py:127
  45.5 2.7 %collective-permute-start.9 = (bf16[128,768]{1,0:T(8,128)(2,1)S(1)}, bf16[128,768]{1,0:T(8,128)(2,1)S(1)}, u32[]{:S(2)}, u32[]{:S(2)}) collective-permute-start(bf16[128,768]{1,0:T(8,128)(2,1)S(1)} %get-tuple-element.35), channel_id=1, source_target_pairs={{0,8},{1,9},{2,10},{3,11},{4,12},{5,13},{6,14},{7,15},{8,0},{9,1},... | collective-permute-start | bytes 589832 | tf_op jit(solution)/shard_map/ppermute | solution.py:127
  48.4 15.3 %collective-permute-done.8 = bf16[128,384]{1,0:T(8,128)(2,1)S(1)} collective-permute-done((bf16[128,384]{1,0:T(8,128)(2,1)S(1)}, bf16[128,384]{1,0:T(8,128)(2,1)S(1)}, u32[]{:S(2)}, u32[]{:S(2)}) %collective-permute-start.8) | collective-permute-done | bytes 98336 | tf_op jit(solution)/shard_map/ppermute | solution.py:127
  63.8 12.2 %collective-permute-done.10.partner_ref = bf16[128,768]{1,0:T(8,128)(2,1)S(1)} collective-permute-done((bf16[128,768]{1,0:T(8,128)(2,1)S(1)}, bf16[128,768]{1,0:T(8,128)(2,1)S(1)}, u32[]{:S(2)}, u32[]{:S(2)}) %collective-permute-start.10) | collective-permute-done | bytes 196640 | tf_op jit(solution)/shard_map/ppermute | solution.py:127
  76.0 13.4 %attend_and_mix.3.refs_0_ = f32[8,128,1152]{2,1,0:T(8,128)} custom-call(s32[8]{0:T(128)S(1)} %iota_xor_fusion.ids_ref, f32[128,768]{1,0:T(8,128)S(1)} %get-tuple-element.28.own_ref, bf16[128,768]{1,0:T(8,128)(2,1)S(1)} %collective-permute-done.10.partner_ref, bf16[128,192]{1,0:T(8,128)(2,1)S(1)} %get-tuple-element.47.key_ref, ...), custom_call_target="tpu_custom_call" | custom-call | flops 1811939328 | bytes 14155776 | tf_op jit(solution)/shard_map/attend_and_mix/pallas_call | solution.py:242
  89.4 14.8 %attend_and_mix.4.refs_0_ = f32[8,128,1152]{2,1,0:T(8,128)} custom-call(s32[8]{0:T(128)S(1)} %iota_xor_fusion.ids_ref, f32[128,768]{1,0:T(8,128)S(1)} %get-tuple-element.29.own_ref, bf16[128,768]{1,0:T(8,128)(2,1)S(1)} %collective-permute-done.9.partner_ref, bf16[128,192]{1,0:T(8,128)(2,1)S(1)} %get-tuple-element.47.key_ref, ...), custom_call_target="tpu_custom_call" | custom-call | flops 1811939328 | bytes 14155776 | tf_op jit(solution)/shard_map/attend_and_mix/pallas_call | solution.py:242
  104.2 13.4 %attend_and_mix.5 = (bf16[8,128,1152]{2,1,0:T(8,128)(2,1)S(1)}, f32[8,8,1152]{2,1,0:T(8,128)S(1)}) custom-call(s32[8]{0:T(128)S(1)} %iota_xor_fusion.ids_ref, f32[128,768]{1,0:T(8,128)S(1)} %get-tuple-element.30.own_ref, bf16[128,768]{1,0:T(8,128)(2,1)S(1)} %collective-permute-done.7.partner_ref, bf16[128,192]{1,0:T(8,128)(2,1)S(1)} %get-tuple-element.47.key_ref, ...), custom_call_target="tpu_custom_call" | custom-call | flops 1811939328 | bytes 14155776 | tf_op jit(solution)/shard_map/attend_and_mix/pallas_call | solution.py:242
  117.8 1.2 collective-permute-done.15
  119.1 1.8 %collective-permute-start.18 = (bf16[4,4,1152]{2,1,0:T(4,128)(2,1)S(1)}, bf16[4,4,1152]{2,1,0:T(4,128)(2,1)S(1)}, u32[]{:S(2)}, u32[]{:S(2)}) collective-permute-start(bf16[4,4,1152]{2,1,0:T(4,128)(2,1)S(1)} %pad_maximum_fusion.3), channel_id=1, source_target_pairs={{0,6},{1,7},{2,4},{3,5},{4,2},{5,3},{6,0},{7,1},{8,14},{9,15},{10,... | collective-permute-start | bytes 110600 | tf_op jit(solution)/shard_map/ppermute | solution.py:127
  120.8 1.3 collective-permute-start.17
  122.6 1.4 collective-permute-done.18
  124.8 1.3 collective-permute-done.16
  126.2 2.1 %collective-permute-start.19 = (bf16[4,4,1152]{2,1,0:T(4,128)(2,1)S(1)}, bf16[4,4,1152]{2,1,0:T(4,128)(2,1)S(1)}, u32[]{:S(2)}, u32[]{:S(2)}) collective-permute-start(bf16[4,4,1152]{2,1,0:T(4,128)(2,1)S(1)} %pad_maximum_fusion.4), channel_id=1, source_target_pairs={{0,8},{1,9},{2,10},{3,11},{4,12},{5,13},{6,14},{7,15},{8,0},{9,1},... | collective-permute-start | bytes 110600 | tf_op jit(solution)/shard_map/ppermute | solution.py:127
  128.3 2.8 %collective-permute-done.19 = bf16[4,4,1152]{2,1,0:T(4,128)(2,1)S(1)} collective-permute-done((bf16[4,4,1152]{2,1,0:T(4,128)(2,1)S(1)}, bf16[4,4,1152]{2,1,0:T(4,128)(2,1)S(1)}, u32[]{:S(2)}, u32[]{:S(2)}) %collective-permute-start.19) | collective-permute-done | bytes 36896 | tf_op jit(solution)/shard_map/ppermute | solution.py:127
  133.0 1.6 %collective-permute-done.11 = bf16[4,128,1152]{2,1,0:T(8,128)(2,1)S(1)} collective-permute-done((bf16[4,128,1152]{2,1,0:T(8,128)(2,1)S(1)}, bf16[4,128,1152]{2,1,0:T(8,128)(2,1)S(1)}, u32[]{:S(2)}, u32[]{:S(2)}) %collective-permute-start.11) | collective-permute-done | bytes 1179680 | tf_op jit(solution)/shard_map/ppermute | solution.py:127
  135.0 1.2 collective-permute-start.14
  136.2 0.8 collective-permute-start.13
  137.0 1.6 %collective-permute-start.12 = (bf16[128,1152]{1,0:T(8,128)(2,1)S(1)}, bf16[128,1152]{1,0:T(8,128)(2,1)S(1)}, u32[]{:S(2)}, u32[]{:S(2)}) collective-permute-start(bf16[128,1152]{1,0:T(8,128)(2,1)S(1)} %get-tuple-element.31), channel_id=1, source_target_pairs={{0,2},{1,3},{2,0},{3,1},{4,6},{5,7},{6,4},{7,5},{8,10},{9,11},{10,... | collective-permute-start | bytes 884744 | tf_op jit(solution)/shard_map/ppermute | solution.py:127
  138.6 0.9 convolution_convert_fusion
  139.5 6.4 %collective-permute-done.14 = bf16[128,1152]{1,0:T(8,128)(2,1)S(1)} collective-permute-done((bf16[128,1152]{1,0:T(8,128)(2,1)S(1)}, bf16[128,1152]{1,0:T(8,128)(2,1)S(1)}, u32[]{:S(2)}, u32[]{:S(2)}) %collective-permute-start.14) | collective-permute-done | bytes 294944 | tf_op jit(solution)/shard_map/ppermute | solution.py:127
  145.9 4.8 %collective-permute-done.13 = bf16[128,1152]{1,0:T(8,128)(2,1)S(1)} collective-permute-done((bf16[128,1152]{1,0:T(8,128)(2,1)S(1)}, bf16[128,1152]{1,0:T(8,128)(2,1)S(1)}, u32[]{:S(2)}, u32[]{:S(2)}) %collective-permute-start.13) | collective-permute-done | bytes 294944 | tf_op jit(solution)/shard_map/ppermute | solution.py:127
  150.6 0.9 collective-permute-done.12
  151.6 0.9 fusion.3
  (68 shorter events, 6.3 us)
Async XLA Ops:
  0.6 10.3 %collective-permute-start = (bf16[128,1152]{1,0:T(8,128)(2,1)}, bf16[128,1152]{1,0:T(8,128)(2,1)S(1)}, u32[]{:S(2)}, u32[]{:S(2)}) collective-permute-start(bf16[128,1152]{1,0:T(8,128)(2,1)} %refs_0_.1), channel_id=1, source_target_pairs={{0,2},{1,3},{2,0},{3,1},{4,6},{5,7},{6,4},{7,5},{8,10},{9,11},{10,... | collective-permute-start | bytes 884744 | tf_op jit(solution)/shard_map/ppermute | solution.py:127
  3.7 10.1 %collective-permute-start.2 = (bf16[128,1152]{1,0:T(8,128)(2,1)}, bf16[128,1152]{1,0:T(8,128)(2,1)S(1)}, u32[]{:S(2)}, u32[]{:S(2)}) collective-permute-start(bf16[128,1152]{1,0:T(8,128)(2,1)} %refs_0_.1), channel_id=1, source_target_pairs={{0,4},{1,5},{2,6},{3,7},{4,0},{5,1},{6,2},{7,3},{8,12},{9,13},{10,... | collective-permute-start | bytes 884744 | tf_op jit(solution)/shard_map/ppermute | solution.py:127
  5.2 13.2 %collective-permute-start.4 = (bf16[128,1152]{1,0:T(8,128)(2,1)}, bf16[128,1152]{1,0:T(8,128)(2,1)S(1)}, u32[]{:S(2)}, u32[]{:S(2)}) collective-permute-start(bf16[128,1152]{1,0:T(8,128)(2,1)} %refs_0_.1), channel_id=1, source_target_pairs={{0,6},{1,7},{2,4},{3,5},{4,2},{5,3},{6,0},{7,1},{8,14},{9,15},{10,... | collective-permute-start | bytes 884744 | tf_op jit(solution)/shard_map/ppermute | solution.py:127
  5.2 13.4 %collective-permute-start.6 = (bf16[128,1152]{1,0:T(8,128)(2,1)}, bf16[128,1152]{1,0:T(8,128)(2,1)S(1)}, u32[]{:S(2)}, u32[]{:S(2)}) collective-permute-start(bf16[128,1152]{1,0:T(8,128)(2,1)} %refs_0_.1), channel_id=1, source_target_pairs={{0,1},{1,0},{2,3},{3,2},{4,5},{5,4},{6,7},{7,6},{8,9},{9,8},{10,11... | collective-permute-start | bytes 884744 | tf_op jit(solution)/shard_map/ppermute | solution.py:127
  10.9 16.1 %collective-permute-start.1 = (bf16[128,1152]{1,0:T(8,128)(2,1)S(1)}, bf16[128,1152]{1,0:T(8,128)(2,1)S(1)}, u32[]{:S(2)}, u32[]{:S(2)}) collective-permute-start(bf16[128,1152]{1,0:T(8,128)(2,1)S(1)} %collective-permute-done.refs_0_), channel_id=1, source_target_pairs={{0,1},{1,0},{2,3},{3,2},{4,5},{5,4},{6,7},{7,6},{8,9},{9,8},{10,11... | collective-permute-start | bytes 884744 | tf_op jit(solution)/shard_map/ppermute | solution.py:127
  13.8 13.2 %collective-permute-start.3 = (bf16[128,1152]{1,0:T(8,128)(2,1)S(1)}, bf16[128,1152]{1,0:T(8,128)(2,1)S(1)}, u32[]{:S(2)}, u32[]{:S(2)}) collective-permute-start(bf16[128,1152]{1,0:T(8,128)(2,1)S(1)} %collective-permute-done.2.refs_2_), channel_id=1, source_target_pairs={{0,1},{1,0},{2,3},{3,2},{4,5},{5,4},{6,7},{7,6},{8,9},{9,8},{10,11... | collective-permute-start | bytes 884744 | tf_op jit(solution)/shard_map/ppermute | solution.py:127
  18.5 8.6 %collective-permute-start.5 = (bf16[128,1152]{1,0:T(8,128)(2,1)S(1)}, bf16[128,1152]{1,0:T(8,128)(2,1)S(1)}, u32[]{:S(2)}, u32[]{:S(2)}) collective-permute-start(bf16[128,1152]{1,0:T(8,128)(2,1)S(1)} %collective-permute-done.4.refs_4_), channel_id=1, source_target_pairs={{0,1},{1,0},{2,3},{3,2},{4,5},{5,4},{6,7},{7,6},{8,9},{9,8},{10,11... | collective-permute-start | bytes 884744 | tf_op jit(solution)/shard_map/ppermute | solution.py:127
  18.6 1.0 copy-start.1
  25.9 1.1 copy-start
  42.4 21.3 %collective-permute-start.8 = (bf16[128,384]{1,0:T(8,128)(2,1)S(1)}, bf16[128,384]{1,0:T(8,128)(2,1)S(1)}, u32[]{:S(2)}, u32[]{:S(2)}) collective-permute-start(bf16[128,384]{1,0:T(8,128)(2,1)S(1)} %slice.215), channel_id=1, source_target_pairs={{0,8},{1,9},{2,10},{3,11},{4,12},{5,13},{6,14},{7,15},{8,0},{9,1},... | collective-permute-start | bytes 294920 | tf_op jit(solution)/shard_map/ppermute | solution.py:127
  45.2 59.0 %collective-permute-start.7 = (bf16[128,768]{1,0:T(8,128)(2,1)S(1)}, bf16[128,768]{1,0:T(8,128)(2,1)S(1)}, u32[]{:S(2)}, u32[]{:S(2)}) collective-permute-start(bf16[128,768]{1,0:T(8,128)(2,1)S(1)} %get-tuple-element.36), channel_id=1, source_target_pairs={{0,8},{1,9},{2,10},{3,11},{4,12},{5,13},{6,14},{7,15},{8,0},{9,1},... | collective-permute-start | bytes 589832 | tf_op jit(solution)/shard_map/ppermute | solution.py:127
  45.5 43.9 %collective-permute-start.9 = (bf16[128,768]{1,0:T(8,128)(2,1)S(1)}, bf16[128,768]{1,0:T(8,128)(2,1)S(1)}, u32[]{:S(2)}, u32[]{:S(2)}) collective-permute-start(bf16[128,768]{1,0:T(8,128)(2,1)S(1)} %get-tuple-element.35), channel_id=1, source_target_pairs={{0,8},{1,9},{2,10},{3,11},{4,12},{5,13},{6,14},{7,15},{8,0},{9,1},... | collective-permute-start | bytes 589832 | tf_op jit(solution)/shard_map/ppermute | solution.py:127
  48.2 27.8 %collective-permute-start.10 = (bf16[128,768]{1,0:T(8,128)(2,1)S(1)}, bf16[128,768]{1,0:T(8,128)(2,1)S(1)}, u32[]{:S(2)}, u32[]{:S(2)}) collective-permute-start(bf16[128,768]{1,0:T(8,128)(2,1)S(1)} %get-tuple-element.34), channel_id=1, source_target_pairs={{0,8},{1,9},{2,10},{3,11},{4,12},{5,13},{6,14},{7,15},{8,0},{9,1},... | collective-permute-start | bytes 589832 | tf_op jit(solution)/shard_map/ppermute | solution.py:127
  104.2 24.1 %copy-start.2 = (s32[4]{0:T(128)S(1)}, s32[4]{0:T(128)}, u32[]{:S(2)}) copy-start(s32[4]{0:T(128)} %param.11) | copy-start | bytes 52
  117.7 1.3 collective-permute-start.15
  119.1 5.0 %collective-permute-start.18 = (bf16[4,4,1152]{2,1,0:T(4,128)(2,1)S(1)}, bf16[4,4,1152]{2,1,0:T(4,128)(2,1)S(1)}, u32[]{:S(2)}, u32[]{:S(2)}) collective-permute-start(bf16[4,4,1152]{2,1,0:T(4,128)(2,1)S(1)} %pad_maximum_fusion.3), channel_id=1, source_target_pairs={{0,6},{1,7},{2,4},{3,5},{4,2},{5,3},{6,0},{7,1},{8,14},{9,15},{10,... | collective-permute-start | bytes 110600 | tf_op jit(solution)/shard_map/ppermute | solution.py:127
  120.8 4.0 %collective-permute-start.17 = (bf16[4,4,1152]{2,1,0:T(4,128)(2,1)S(1)}, bf16[4,4,1152]{2,1,0:T(4,128)(2,1)S(1)}, u32[]{:S(2)}, u32[]{:S(2)}) collective-permute-start(bf16[4,4,1152]{2,1,0:T(4,128)(2,1)S(1)} %pad_maximum_fusion.3), channel_id=1, source_target_pairs={{0,4},{1,5},{2,6},{3,7},{4,0},{5,1},{6,2},{7,3},{8,12},{9,13},{10,... | collective-permute-start | bytes 110600 | tf_op jit(solution)/shard_map/ppermute | solution.py:127
  122.2 4.0 %collective-permute-start.16 = (bf16[4,4,1152]{2,1,0:T(4,128)(2,1)S(1)}, bf16[4,4,1152]{2,1,0:T(4,128)(2,1)S(1)}, u32[]{:S(2)}, u32[]{:S(2)}) collective-permute-start(bf16[4,4,1152]{2,1,0:T(4,128)(2,1)S(1)} %pad_maximum_fusion.3), channel_id=1, source_target_pairs={{0,2},{1,3},{2,0},{3,1},{4,6},{5,7},{6,4},{7,5},{8,10},{9,11},{10,... | collective-permute-start | bytes 110600 | tf_op jit(solution)/shard_map/ppermute | solution.py:127
  126.2 4.9 %collective-permute-start.19 = (bf16[4,4,1152]{2,1,0:T(4,128)(2,1)S(1)}, bf16[4,4,1152]{2,1,0:T(4,128)(2,1)S(1)}, u32[]{:S(2)}, u32[]{:S(2)}) collective-permute-start(bf16[4,4,1152]{2,1,0:T(4,128)(2,1)S(1)} %pad_maximum_fusion.4), channel_id=1, source_target_pairs={{0,8},{1,9},{2,10},{3,11},{4,12},{5,13},{6,14},{7,15},{8,0},{9,1},... | collective-permute-start | bytes 110600 | tf_op jit(solution)/shard_map/ppermute | solution.py:127
  131.2 1.3 collective-permute-start.20
  131.6 3.0 %collective-permute-start.11 = (bf16[4,128,1152]{2,1,0:T(8,128)(2,1)S(1)}, bf16[4,128,1152]{2,1,0:T(8,128)(2,1)S(1)}, u32[]{:S(2)}, u32[]{:S(2)}) collective-permute-start(bf16[4,128,1152]{2,1,0:T(8,128)(2,1)S(1)} %slice.173), channel_id=1, source_target_pairs={{0,1},{1,0},{2,3},{3,2},{4,5},{5,4},{6,7},{7,6},{8,9},{9,8},{10,11... | collective-permute-start | bytes 3538952 | tf_op jit(solution)/shard_map/ppermute | solution.py:127
  135.0 10.8 %collective-permute-start.14 = (bf16[128,1152]{1,0:T(8,128)(2,1)S(1)}, bf16[128,1152]{1,0:T(8,128)(2,1)S(1)}, u32[]{:S(2)}, u32[]{:S(2)}) collective-permute-start(bf16[128,1152]{1,0:T(8,128)(2,1)S(1)} %get-tuple-element.32), channel_id=1, source_target_pairs={{0,6},{1,7},{2,4},{3,5},{4,2},{5,3},{6,0},{7,1},{8,14},{9,15},{10,... | collective-permute-start | bytes 884744 | tf_op jit(solution)/shard_map/ppermute | solution.py:127
  136.2 14.5 %collective-permute-start.13 = (bf16[128,1152]{1,0:T(8,128)(2,1)S(1)}, bf16[128,1152]{1,0:T(8,128)(2,1)S(1)}, u32[]{:S(2)}, u32[]{:S(2)}) collective-permute-start(bf16[128,1152]{1,0:T(8,128)(2,1)S(1)} %get-tuple-element.33), channel_id=1, source_target_pairs={{0,4},{1,5},{2,6},{3,7},{4,0},{5,1},{6,2},{7,3},{8,12},{9,13},{10,... | collective-permute-start | bytes 884744 | tf_op jit(solution)/shard_map/ppermute | solution.py:127
  137.0 14.6 %collective-permute-start.12 = (bf16[128,1152]{1,0:T(8,128)(2,1)S(1)}, bf16[128,1152]{1,0:T(8,128)(2,1)S(1)}, u32[]{:S(2)}, u32[]{:S(2)}) collective-permute-start(bf16[128,1152]{1,0:T(8,128)(2,1)S(1)} %get-tuple-element.31), channel_id=1, source_target_pairs={{0,2},{1,3},{2,0},{3,1},{4,6},{5,7},{6,4},{7,5},{8,10},{9,11},{10,... | collective-permute-start | bytes 884744 | tf_op jit(solution)/shard_map/ppermute | solution.py:127

commit v2 on v0

--- a/solution.py
+++ b/solution.py
@@ -3,6 +3,8 @@
 import jax
 import jax.numpy as jnp
 from jax import lax
+from jax.experimental import pallas as pl
+from jax.experimental.pallas import tpu as pltpu
 from jax.sharding import PartitionSpec as P
 
 HD = 192
@@ -44,7 +46,7 @@
     )
 
 
-def per_device(hidden, w_qkv, w_out, segment_ids, end_positions, owners):
+def general_device(hidden, w_qkv, w_out, segment_ids, end_positions, owners):
     devices = lax.axis_size("gx")
     blocks = devices // KVG
     group_bits = KVG.bit_length() - 1
@@ -116,6 +118,371 @@
     return (mixed, reward_rows)
 
 
+LANES = 128
+ROW_PIECES = 3
+ROW_TILE = 16
+MIB = 1024 * 1024
+
+
+def xor_swap(block, distance):
+    count = lax.axis_size("gx")
+    return lax.ppermute(block, "gx", [(low, low ^ distance) for low in range(count)])
+
+
+def vmem():
+    return pl.BlockSpec(memory_space=pltpu.VMEM)
+
+
+def smem():
+    return pl.BlockSpec(memory_space=pltpu.SMEM)
+
+
+def anywhere():
+    return pl.BlockSpec(memory_space=pl.ANY)
+
+
+def project(features, distances, running, w_qkv, my_group, columns, first_column):
+    tokens, width = features[0].shape
+    count = len(features)
+    piece = width // ROW_PIECES
+    block_ids = jnp.stack([my_group ^ d for d in distances]).astype(jnp.int32)
+    operands = list(features) + [w_qkv]
+    if running is not None:
+        operands.append(running)
+    running_lanes = slice(0, columns)
+    if running is not None and running.shape[1] > columns:
+        running_lanes = slice(first_column, first_column + columns)
+
+    def kernel(ids_ref, *refs):
+        feature_refs = refs[:count]
+        w_ref = refs[count]
+        start_ref = refs[count + 1] if running is not None else None
+        out_ref, current, slabs, sems = refs[-4:]
+
+        def copy(block, part):
+            rows = pl.ds(ids_ref[block] * width + part * piece, piece)
+            return pltpu.make_async_copy(
+                w_ref.at[rows, pl.ds(first_column, columns)], slabs.at[block, part], sems.at[block, part]
+            )
+
+        for block in range(count):
+            for part in range(ROW_PIECES):
+                copy(block, part).start()
+        for block in range(count):
+            current[block] = feature_refs[block][...]
+        if start_ref is None:
+            out_ref[...] = jnp.zeros_like(out_ref)
+        else:
+            out_ref[...] = start_ref[:, running_lanes]
+
+        @pl.loop(0, count)
+        def _(block):
+            for part in range(ROW_PIECES):
+                copy(block, part).wait()
+                out_ref[...] += jnp.dot(
+                    current[block, :, part * piece : (part + 1) * piece],
+                    slabs[block, part],
+                    preferred_element_type=jnp.float32,
+                )
+
+    return pl.pallas_call(
+        kernel,
+        in_specs=[smem()] + [vmem()] * count + [anywhere()] + ([] if running is None else [vmem()]),
+        out_specs=vmem(),
+        out_shape=jax.ShapeDtypeStruct((tokens, columns), jnp.float32),
+        scratch_shapes=[
+            pltpu.VMEM((count, tokens, width), jnp.bfloat16),
+            pltpu.VMEM((count, ROW_PIECES, piece, columns), jnp.bfloat16),
+            pltpu.SemaphoreType.DMA((count, ROW_PIECES)),
+        ],
+        compiler_params=pltpu.CompilerParams(vmem_limit_bytes=40 * MIB),
+        cost_estimate=pl.CostEstimate(
+            flops=2 * count * tokens * width * columns,
+            bytes_accessed=2 * count * width * columns,
+            transcendentals=0,
+        ),
+        name="project",
+    )(block_ids, *operands)
+
+
+def packed_tiles(tokens):
+    blocks = tokens // ROW_TILE
+    places = []
+    for head in range(2):
+        places.append((head, head, blocks - 1, 0))
+        for low in range(blocks // 2 - 1):
+            tile = 2 + head * (blocks // 2 - 1) + low
+            places.append((tile, head, low, 0))
+            places.append((tile, head, blocks - 2 - low, (low + 1) * ROW_TILE))
+        places.append((blocks, head, blocks // 2 - 1, head * tokens // 2))
+    return places
+
+
+def partial_scores(queries, own_kv, partner_kv):
+    tokens = queries.shape[0]
+    blocks = tokens // ROW_TILE
+
+    def kernel(query_ref, own_ref, partner_ref, value_ref, score_ref, packed_ref):
+        pair = (own_ref[...] + partner_ref[...].astype(jnp.float32)).astype(jnp.bfloat16)
+        keys = pair[:, :HD]
+        value_ref[...] = pair[:, HD:]
+        lane = lax.broadcasted_iota(jnp.int32, (ROW_TILE, tokens), 1)
+        for first in range(0, HPG, 2):
+            tiles = [None] * (blocks + 1)
+            scores = []
+            for head in range(first, first + 2):
+                scores.append(
+                    contract_last(query_ref[:, head * HD : (head + 1) * HD].astype(jnp.bfloat16), keys)
+                )
+                score_ref[head] = scores[-1]
+            for tile, head, block, shift in packed_tiles(tokens):
+                rows = scores[head][block * ROW_TILE : (block + 1) * ROW_TILE]
+                if shift:
+                    rows = jnp.where(lane < shift, tiles[tile], pltpu.roll(rows, shift, 1))
+                tiles[tile] = rows
+            for tile, rows in enumerate(tiles):
+                packed_ref[first // 2, tile] = rows.astype(jnp.bfloat16)
+
+    return pl.pallas_call(
+        kernel,
+        out_shape=[
+            jax.ShapeDtypeStruct((tokens, HD), jnp.bfloat16),
+            jax.ShapeDtypeStruct((HPG, tokens, tokens), jnp.float32),
+            jax.ShapeDtypeStruct((HPG // 2, blocks + 1, ROW_TILE, tokens), jnp.bfloat16),
+        ],
+        compiler_params=pltpu.CompilerParams(vmem_limit_bytes=16 * MIB),
+        cost_estimate=pl.CostEstimate(
+            flops=2 * HPG * tokens * tokens * HD, bytes_accessed=2 * tokens * HPG * HD, transcendentals=0
+        ),
+        name="partial_scores",
+    )(queries, own_kv, partner_kv)
+
+
+def fetch_rows(block_ids, w_out, count):
+    rows, columns = w_out.shape[0] // KVG, w_out.shape[1]
+
+    def kernel(ids_ref, w_ref, *refs):
+        out_refs, sems = refs[:-1], refs[-1]
+        copies = [
+            pltpu.make_async_copy(
+                w_ref.at[pl.ds(ids_ref[block] * rows, rows)], out_refs[block // 2].at[block % 2], sems.at[block]
+            )
+            for block in range(count)
+        ]
+        for copy in copies:
+            copy.start()
+        for copy in copies:
+            copy.wait()
+
+    return pl.pallas_call(
+        kernel,
+        in_specs=[smem(), anywhere()],
+        out_specs=[vmem()] * (count // 2),
+        out_shape=[pltpu.VMEM((2, rows, columns), jnp.bfloat16)] * (count // 2),
+        scratch_shapes=[pltpu.SemaphoreType.DMA((count,))],
+        compiler_params=pltpu.CompilerParams(vmem_limit_bytes=2 * MIB),
+        cost_estimate=pl.CostEstimate(
+            flops=2 * count * LANES * rows * columns, bytes_accessed=2 * count * rows * columns, transcendentals=0
+        ),
+        name="fetch_rows",
+    )(block_ids, w_out)
+
+
+def mix_chip(attended, slab_ref, picker, even_ref, odd_ref, end_ref):
+    for core, out_ref in enumerate((even_ref, odd_ref)):
+        part = contract_last(attended[...], slab_ref[core]).astype(jnp.bfloat16)
+        out_ref[...] = part
+        end_ref[core] = jnp.dot(picker[...], part, preferred_element_type=jnp.float32)
+
+
+def chip_shapes(tokens, rows, picker):
+    part = jax.ShapeDtypeStruct((tokens, rows), jnp.bfloat16)
+    return [part, part, jax.ShapeDtypeStruct((2, picker.shape[0], rows), jnp.float32)]
+
+
+def attend_and_mix(own_scores, partner_scores, values, allowed, slabs, picker):
+    heads, tokens = own_scores.shape[:2]
+    blocks = tokens // ROW_TILE
+    count, rows, columns = slabs.shape
+    scale = 1.0 / math.sqrt(HD)
+
+    def kernel(
+        own_ref, partner_ref, value_ref, allowed_ref, slab_ref, picker_ref,
+        attended_ref, even_ref, odd_ref, end_ref,
+    ):
+        mask = allowed_ref[...] > 0.0
+        for two in range(heads // 2):
+            partner = [[None] * blocks, [None] * blocks]
+            for tile, head, block, shift in packed_tiles(tokens):
+                rows_of = partner_ref[two, tile].astype(jnp.float32)
+                partner[head][block] = pltpu.roll(rows_of, tokens - shift, 1) if shift else rows_of
+            for core in range(2):
+                head = 2 * two + core
+                scores = (own_ref[head] + jnp.concatenate(partner[core], 0)) * scale
+                row_max = jnp.max(jnp.where(mask, scores, -jnp.inf), axis=1, keepdims=True)
+                weights = jnp.where(mask, jnp.exp(scores - row_max), 0.0)
+                totals = jnp.sum(weights, axis=1, keepdims=True)
+                mixed_heads = jnp.dot(
+                    weights.astype(jnp.bfloat16), value_ref[...], preferred_element_type=jnp.float32
+                )
+                attended_ref[:, head * HD : (head + 1) * HD] = (mixed_heads / totals).astype(jnp.bfloat16)
+        mix_chip(attended_ref, slab_ref, picker_ref, even_ref, odd_ref, end_ref)
+
+    return pl.pallas_call(
+        kernel,
+        in_specs=[vmem()] * 6,
+        out_specs=[vmem()] * 4,
+        out_shape=[jax.ShapeDtypeStruct((tokens, columns), jnp.bfloat16)]
+        + chip_shapes(tokens, rows, picker),
+        compiler_params=pltpu.CompilerParams(vmem_limit_bytes=8 * MIB),
+        cost_estimate=pl.CostEstimate(
+            flops=4 * tokens * rows * columns,
+            bytes_accessed=4 * rows * columns,
+            transcendentals=heads * tokens * tokens,
+        ),
+        name="attend_and_mix",
+    )(own_scores, partner_scores, values, allowed, slabs, picker)
+
+
+def mix(attended, slabs, picker):
+    tokens = attended.shape[0]
+    rows, columns = slabs.shape[1:]
+
+    def kernel(attended_ref, slab_ref, picker_ref, even_ref, odd_ref, end_ref):
+        mix_chip(attended_ref, slab_ref, picker_ref, even_ref, odd_ref, end_ref)
+
+    return pl.pallas_call(
+        kernel,
+        in_specs=[vmem()] * 3,
+        out_specs=[vmem()] * 3,
+        out_shape=chip_shapes(tokens, rows, picker),
+        compiler_params=pltpu.CompilerParams(vmem_limit_bytes=8 * MIB),
+        cost_estimate=pl.CostEstimate(flops=tokens * rows, bytes_accessed=rows, transcendentals=0),
+        name="mix",
+    )(attended, slabs, picker)
+
+
+def add_rounded(left, right):
+    return (left.astype(jnp.float32) + right.astype(jnp.float32)).astype(jnp.bfloat16)
+
+
+def swap_blocks(blocks, distance):
+    return [blocks[j ^ distance] for j in range(len(blocks))]
+
+
+def natural_order(blocks, my_group):
+    distance = 1
+    while distance < len(blocks):
+        bit = (my_group & distance) != 0
+        swapped = swap_blocks(blocks, distance)
+        blocks = [jnp.where(bit, other, own) for own, other in zip(blocks, swapped)]
+        distance *= 2
+    return jnp.concatenate(blocks, axis=-1)
+
+
+def pair_device(hidden, w_qkv, w_out, segment_ids, end_positions, owners):
+    my_index = lax.axis_index("gx")
+    my_group = my_index % KVG
+    my_block = my_index // KVG
+    tokens = hidden.shape[0]
+    query_width = HPG * HD
+    together = lax.optimization_barrier
+    positions = jnp.arange(tokens, dtype=jnp.int32)
+    allowed = (
+        (segment_ids[:, None] == segment_ids[None, :]) & (positions[None, :] <= positions[:, None])
+    ).astype(jnp.float32)
+    completions = owners.shape[0]
+    end_rows = -(-completions // 8) * 8
+    picker = (
+        jnp.pad(end_positions, (0, end_rows - completions), constant_values=-1)[:, None] == positions[None, :]
+    ).astype(jnp.bfloat16)
+    same_owner = owners[:, None] == owners[None, :]
+    earlier = jnp.arange(completions)[None, :] < jnp.arange(completions)[:, None]
+    order_rank = jnp.sum((same_owner & earlier).astype(jnp.int32), axis=1)
+    chooser = (
+        (owners[None, :] == my_index)
+        & (order_rank[None, :] == jnp.arange(SLOTS, dtype=jnp.int32)[:, None])
+    ).astype(jnp.bfloat16)
+
+    columns = w_qkv.shape[1]
+    near_core = xor_swap(hidden, 1)
+    from_y, from_z = xor_swap(hidden, 2), xor_swap(hidden, 4)
+    early = project([hidden, near_core], (0, 1), None, w_qkv, my_group, columns, 0)
+    from_y, from_z, sent, early = together((from_y, from_z, hidden, early))
+    from_both = xor_swap(sent, 6)
+    from_y_core, from_z_core = xor_swap(from_y, 1), xor_swap(from_z, 1)
+    middle = project(
+        [from_y, from_z, from_y_core, from_z_core], (2, 4, 3, 5), early, w_qkv, my_group, columns, 0
+    )
+    from_both, middle = together((from_both, middle))
+    late = [from_both, xor_swap(from_both, 1)]
+    own_kv = project(late, (6, 7), middle, w_qkv, my_group, 2 * HD, query_width)
+    partner_kv = xor_swap(own_kv.astype(jnp.bfloat16), KVG)
+    middle, own_kv = together((middle, own_kv))
+    queries = project(late, (6, 7), middle, w_qkv, my_group, query_width, 0)
+
+    values, scores, packed = partial_scores(queries, own_kv, partner_kv)
+    block_ids = (my_group ^ jnp.arange(KVG, dtype=jnp.int32)).astype(jnp.int32)
+    packed, block_ids = together((packed, block_ids))
+    arrived = xor_swap(packed, KVG)
+    own_slabs, slabs_y, slabs_z, slabs_both = fetch_rows(block_ids, w_out, KVG)
+    arrived, slabs_both = together((arrived, slabs_both))
+    attended, even_both, odd_both, ends_both = attend_and_mix(
+        scores, arrived, values, allowed, slabs_both, picker
+    )
+    odd_both = xor_swap(odd_both, 1)
+    even_y, odd_y, ends_y = mix(attended, slabs_y, picker)
+    odd_both, even_y, odd_y = together((odd_both, even_y, odd_y))
+    odd_y = xor_swap(odd_y, 1)
+    near_both, attended = together((add_rounded(even_both, odd_both), attended))
+    sum_both = xor_swap(near_both, 6)
+    even_z, odd_z, ends_z = mix(attended, slabs_z, picker)
+    odd_y, even_z, odd_z = together((odd_y, even_z, odd_z))
+    odd_z = xor_swap(odd_z, 1)
+    near_y, attended = together((add_rounded(even_y, odd_y), attended))
+    sum_y = xor_swap(near_y, 2)
+    even_own, odd_own, ends_own = mix(attended, own_slabs, picker)
+    odd_z, even_own, odd_own, ends_own, sum_both = together((odd_z, even_own, odd_own, ends_own, sum_both))
+    sum_z = xor_swap(add_rounded(even_z, odd_z), 4)
+
+    end_parts = jnp.concatenate([ends_own, ends_y, ends_z, ends_both])[:, :completions]
+    end_far = xor_swap(end_parts[1::2].astype(jnp.bfloat16), 1)
+    ends = end_parts[0::2] + end_far.astype(jnp.float32)
+    got = xor_swap(ends.astype(jnp.bfloat16), 2).astype(jnp.float32)
+    odd_own = xor_swap(odd_own, 1)
+    ends = [ends[i] + got[i ^ 1] for i in range(KVG // 2)]
+    message = jnp.stack(ends).astype(jnp.bfloat16)
+    got = xor_swap(message, 4).astype(jnp.float32)
+    own_ends = jnp.stack([ends[i] + got[i ^ 2] for i in range(KVG // 2)]).astype(jnp.bfloat16)
+    got = [xor_swap(message, KVG).astype(jnp.float32), xor_swap(message, KVG ^ 4).astype(jnp.float32)]
+    other_ends = jnp.stack([got[0][i] + got[1][i ^ 2] for i in range(KVG // 2)]).astype(jnp.bfloat16)
+    both = jnp.stack([own_ends, other_ends])
+    both_far = xor_swap(both, 1)
+    halves = []
+    for half in range(2):
+        blocks = []
+        for i in range(KVG // 2):
+            blocks += [both[half, i], both_far[half, i]]
+        halves.append(natural_order(blocks, my_group))
+    end_full = jnp.concatenate(
+        [jnp.where(my_block == 0, halves[0], halves[1]), jnp.where(my_block == 0, halves[1], halves[0])], axis=-1
+    )
+    reward_rows = jnp.dot(chooser, end_full, preferred_element_type=jnp.float32).astype(jnp.bfloat16)
+
+    mixed = even_own.astype(jnp.float32)
+    for part in (odd_own, sum_y, sum_z, sum_both):
+        mixed += part.astype(jnp.float32)
+    return (mixed.astype(jnp.bfloat16), reward_rows)
+
+
+def per_device(hidden, w_qkv, w_out, segment_ids, end_positions, owners):
+    tokens, width = hidden.shape
+    blocks = lax.axis_size("gx") // KVG
+    if blocks == 2 and width % LANES == 0 and tokens == LANES:
+        return pair_device(hidden, w_qkv, w_out, segment_ids, end_positions, owners)
+    return general_device(hidden, w_qkv, w_out, segment_ids, end_positions, owners)
+
+
 def solution(mesh):
     placed = (
         P("groups", "gx"),

time: 251 us -> 98.5 us (0.39)
  waiting for transfers between devices: 168 us -> 15.2 us
  Pallas kernels: 0 us -> 54.4 us
  matrix products: 45.7 us -> 0.86 us
  blocking collectives: 20.8 us -> 0 us
  starting transfers between devices: 8.25 us -> 22.8 us
  other arithmetic: 5.69 us -> 2.49 us
    ppermute x9 -> x22, waiting for transfers between devices: 168 us -> 15.2 us  [xor_swap(): lax.ppermute(block, 'gx', [(low, low ^ distance) for low in range(count)])]
    pallas_call x0 -> x10, Pallas kernels: none -> 54.4 us  [the longest x4 23.2 us: project(): pl.pallas_call(kernel, in_specs=[smem()] + [vmem()] * count + [anywhere()...]
    dot_general x6 -> x1, matrix products: 45.7 us -> 0.86 us  [pair_device(): jnp.dot(chooser, end_full, preferred_element_type=jnp.float32)]
    all_gather x1 -> x0, blocking collectives: 20.8 us -> none  [per_device(): end_full = lax.all_gather(end_local, 'gx', axis=1, tiled=True)]
    ppermute x9 -> x22, starting transfers between devices: 8.25 us -> 22.8 us  [xor_swap(): lax.ppermute(block, 'gx', [(low, low ^ distance) for low in range(count)])]
    select_n x7 -> x1, other arithmetic: 4.61 us -> 0.06 us  [pair_device(): jnp.where(my_block == 0, halves[0], halves[1])]
  transfers between devices with their start and end apart: 9 -> 22, of which waited for: 9 -> 8; matrix products, arithmetic and copies ran while one was open for 0% -> 3% of each run, Pallas kernels for 0% -> 47%
where the time goes in v2:
time: 98.5 us; the launch traced here: 98.3 us
  Pallas kernels  54.4 us (55%)
  starting transfers between devices  22.8 us (23%)
  waiting for transfers between devices  15.2 us (15%)
  other arithmetic  2.49 us (3%)
  local copies, waits for them, and re-layouts  1.65 us (2%)
    pallas_call x4, Pallas kernels, project(): pl.pallas_call(kernel, in_specs=[smem()] + [vmem()] * count + [anywhere()...  23.2 us
    ppermute x22, starting transfers between devices, xor_swap(): lax.ppermute(block, 'gx', [(low, low ^ distance) for low in range(count)])  22.8 us
    ppermute x22, waiting for transfers between devices, xor_swap(): lax.ppermute(block, 'gx', [(low, low ^ distance) for low in range(count)])  15.2 us
    pallas_call x1, Pallas kernels, fetch_rows(): pl.pallas_call(kernel, in_specs=[smem(), anywhere()], out_specs=[vmem()]...  13.8 us
    pallas_call x3, Pallas kernels, mix(): pl.pallas_call(kernel, in_specs=[vmem()] * 3, out_specs=[vmem()] * 3, out...  11.5 us
    pallas_call x1, Pallas kernels, attend_and_mix(): pl.pallas_call(kernel, in_specs=[vmem()] * 6, out_specs=[vmem()] * 4, out...  5.46 us
  transfers between devices with their start and end apart: 22, of which 8 were waited for; matrix products, arithmetic and copies ran while one was open for 3% of the time, Pallas kernels for 47%

profile of v2, /device:TPU:0, one launch (start us, length us, event | category | flops | bytes accessed | tf_op | source)
XLA Modules:
  0.0 98.3 jit_solution(1491891883197861235)
XLA Ops:
  1.1 2.6 %collective-permute-start = (bf16[128,1152]{1,0:T(8,128)(2,1)}, bf16[128,1152]{1,0:T(8,128)(2,1)S(1)}, u32[]{:S(2)}, u32[]{:S(2)}) collective-permute-start(bf16[128,1152]{1,0:T(8,128)(2,1)} %refs_0_.1), channel_id=1, source_target_pairs={{0,2},{1,3},{2,0},{3,1},{4,6},{5,7},{6,4},{7,5},{8,10},{9,11},{10,... | collective-permute-start | bytes 884744 | tf_op jit(solution)/shard_map/ppermute | solution.py:129
  3.7 1.6 %collective-permute-start.1 = (bf16[128,1152]{1,0:T(8,128)(2,1)}, bf16[128,1152]{1,0:T(8,128)(2,1)S(1)}, u32[]{:S(2)}, u32[]{:S(2)}) collective-permute-start(bf16[128,1152]{1,0:T(8,128)(2,1)} %refs_0_.1), channel_id=1, source_target_pairs={{0,4},{1,5},{2,6},{3,7},{4,0},{5,1},{6,2},{7,3},{8,12},{9,13},{10,... | collective-permute-start | bytes 884744 | tf_op jit(solution)/shard_map/ppermute | solution.py:129
  5.3 0.7 pad.4
  6.1 1.0 copy-done
  7.0 5.8 %project.4.refs_5_ = f32[128,2688]{1,0:T(8,128)S(1)} custom-call(s32[2]{0:T(128)S(1)} %pad_add_fusion.1.ids_ref, bf16[128,1152]{1,0:T(8,128)(2,1)S(1)} %copy-done, bf16[128,1152]{1,0:T(8,128)(2,1)S(1)} %collective-permute-done.2.refs_1_, bf16[9216,2688]{1,0:T(8,128)(2,1)} %refs_2_.5), custom_call_target="tpu_custom_call" | custom-call | flops 1585446912 | bytes 12386304 | tf_op jit(solution)/shard_map/project/pallas_call | solution.py:188
  13.7 1.5 %collective-permute-start.3 = (bf16[128,1152]{1,0:T(8,128)(2,1)S(1)}, bf16[128,1152]{1,0:T(8,128)(2,1)S(1)}, u32[]{:S(2)}, u32[]{:S(2)}) collective-permute-start(bf16[128,1152]{1,0:T(8,128)(2,1)S(1)} %copy-done.1), channel_id=1, source_target_pairs={{0,6},{1,7},{2,4},{3,5},{4,2},{5,3},{6,0},{7,1},{8,14},{9,15},{10,... | collective-permute-start | bytes 884744 | tf_op jit(solution)/shard_map/ppermute | solution.py:129
  15.2 9.3 %project.5.refs_3_ = f32[128,2688]{1,0:T(8,128)S(1)} custom-call(s32[4]{0:T(128)S(1)} %pad_add_fusion.2.ids_ref, bf16[128,1152]{1,0:T(8,128)(2,1)S(1)} %collective-permute-done.refs_0_, bf16[128,1152]{1,0:T(8,128)(2,1)S(1)} %collective-permute-done.1.refs_1_, bf16[128,1152]{1,0:T(8,128)(2,1)S(1)} %collective-permute-done.4.refs_2_, ...), custom_call_target="tpu_custom_call" | custom-call | flops 3170893824 | bytes 24772608 | tf_op jit(solution)/shard_map/project/pallas_call | solution.py:188
  24.8 1.4 %collective-permute-done.6.refs_1_ = bf16[128,1152]{1,0:T(8,128)(2,1)S(1)} collective-permute-done((bf16[128,1152]{1,0:T(8,128)(2,1)S(1)}, bf16[128,1152]{1,0:T(8,128)(2,1)S(1)}, u32[]{:S(2)}, u32[]{:S(2)}) %collective-permute-start.6) | collective-permute-done | bytes 294944 | tf_op jit(solution)/shard_map/ppermute | solution.py:129
  26.2 2.8 %project.6.own_ref = f32[128,384]{1,0:T(8,128)S(1)} custom-call(s32[2]{0:T(128)S(1)} %pad_add_fusion.ids_ref, bf16[128,1152]{1,0:T(8,128)(2,1)S(1)} %collective-permute-done.3.refs_0_, bf16[128,1152]{1,0:T(8,128)(2,1)S(1)} %collective-permute-done.6.refs_1_, bf16[9216,2688]{1,0:T(8,128)(2,1)} %refs_2_.5, f32[128,2688]{1,0:T(8,128)S(1)} %project.5.refs_3_), custom_call_target="tpu_custom_call" | custom-call | flops 226492416 | bytes 1769472 | tf_op jit(solution)/shard_map/project/pallas_call | solution.py:188
  29.0 2.7 %collective-permute-start.7 = (bf16[128,384]{1,0:T(8,128)(2,1)S(1)}, bf16[128,384]{1,0:T(8,128)(2,1)S(1)}, u32[]{:S(2)}, u32[]{:S(2)}) collective-permute-start(bf16[128,384]{1,0:T(8,128)(2,1)S(1)} %convert_element_type.97), channel_id=1, source_target_pairs={{0,8},{1,9},{2,10},{3,11},{4,12},{5,13},{6,14},{7,15},{8,0},{9,1},... | collective-permute-start | bytes 294920 | tf_op jit(solution)/shard_map/ppermute | solution.py:129
  31.7 5.3 %project.7.query_ref = f32[128,2304]{1,0:T(8,128)S(1)} custom-call(s32[2]{0:T(128)S(1)} %pad_add_fusion.ids_ref, bf16[128,1152]{1,0:T(8,128)(2,1)S(1)} %collective-permute-done.3.refs_0_, bf16[128,1152]{1,0:T(8,128)(2,1)S(1)} %collective-permute-done.6.refs_1_, bf16[9216,2688]{1,0:T(8,128)(2,1)} %refs_2_.5, f32[128,2688]{1,0:T(8,128)S(1)} %project.5.refs_3_), custom_call_target="tpu_custom_call" | custom-call | flops 1358954496 | bytes 10616832 | tf_op jit(solution)/shard_map/project/pallas_call | solution.py:188
  37.5 0.5 collective-permute-start.8
  38.1 13.8 %fetch_rows.1 = (bf16[2,1152,2304]{2,1,0:T(8,128)(2,1)S(1)}, bf16[2,1152,2304]{2,1,0:T(8,128)(2,1)S(1)}, bf16[2,1152,2304]{2,1,0:T(8,128)(2,1)S(1)}, bf16[2,1152,2304]{2,1,0:T(8,128)(2,1)S(1)}) custom-call(s32[8]{0:T(128)S(1)} %iota_xor_fusion.ids_ref, bf16[9216,2304]{1,0:T(8,128)(2,1)} %w_ref.1), custom_call_target="tpu_custom_call" | custom-call | flops 5435817984 | bytes 42467328 | tf_op jit(solution)/shard_map/fetch_rows/pallas_call | solution.py:277
  51.8 5.5 %attend_and_mix.1 = (bf16[128,2304]{1,0:T(8,128)(2,1)S(1)}, bf16[128,1152]{1,0:T(8,128)(2,1)S(1)}, bf16[128,1152]{1,0:T(8,128)(2,1)S(1)}, f32[2,8,1152]{2,1,0:T(8,128)S(1)}) custom-call(f32[12,128,128]{2,1,0:T(8,128)S(1)} %get-tuple-element.57.own_ref, bf16[6,9,16,128]{3,2,1,0:T(8,128)(2,1)S(1)} %collective-permute-done.8.partner_ref, ...), custom_call_target="tpu_custom_call" | custom-call | flops 1358954496 | bytes 10616832 | tf_op jit(solution)/shard_map/attend_and_mix/pallas_call | solution.py:331
  57.3 3.8 %mix.3 = (bf16[128,1152]{1,0:T(8,128)(2,1)S(1)}, bf16[128,1152]{1,0:T(8,128)(2,1)S(1)}, f32[2,8,1152]{2,1,0:T(8,128)S(1)}) custom-call(bf16[128,2304]{1,0:T(8,128)(2,1)S(1)} %get-tuple-element.80.attended_ref, bf16[2,1152,2304]{2,1,0:T(8,128)(2,1)S(1)} %get-tuple-element.67.slab_ref, bf16[8,128]{1,0:T(8,128)(2,1)S(1)} %fusion.19.picker_ref), custom_call_target="tpu_custom_call" | custom-call | flops 147456 | bytes 1152 | tf_op jit(solution)/shard_map/mix/pallas_call | solution.py:354
  61.2 0.5 collective-permute-start.10
  61.8 3.5 %collective-permute-start.12 = (bf16[128,1152]{1,0:T(8,128)(2,1)S(1)}, bf16[128,1152]{1,0:T(8,128)(2,1)S(1)}, u32[]{:S(2)}, u32[]{:S(2)}) collective-permute-start(bf16[128,1152]{1,0:T(8,128)(2,1)S(1)} %add_convert_fusion.3), channel_id=1, source_target_pairs={{0,6},{1,7},{2,4},{3,5},{4,2},{5,3},{6,0},{7,1},{8,14},{9,15},{10,... | collective-permute-start | bytes 884744 | tf_op jit(solution)/shard_map/ppermute | solution.py:129
  65.2 3.8 %mix.4 = (bf16[128,1152]{1,0:T(8,128)(2,1)S(1)}, bf16[128,1152]{1,0:T(8,128)(2,1)S(1)}, f32[2,8,1152]{2,1,0:T(8,128)S(1)}) custom-call(bf16[128,2304]{1,0:T(8,128)(2,1)S(1)} %get-tuple-element.80.attended_ref, bf16[2,1152,2304]{2,1,0:T(8,128)(2,1)S(1)} %get-tuple-element.74.slab_ref, bf16[8,128]{1,0:T(8,128)(2,1)S(1)} %fusion.19.picker_ref), custom_call_target="tpu_custom_call" | custom-call | flops 147456 | bytes 1152 | tf_op jit(solution)/shard_map/mix/pallas_call | solution.py:354
  69.2 3.8 %mix.5 = (bf16[128,1152]{1,0:T(8,128)(2,1)S(1)}, bf16[128,1152]{1,0:T(8,128)(2,1)S(1)}, f32[2,8,1152]{2,1,0:T(8,128)S(1)}) custom-call(bf16[128,2304]{1,0:T(8,128)(2,1)S(1)} %get-tuple-element.80.attended_ref, bf16[2,1152,2304]{2,1,0:T(8,128)(2,1)S(1)} %get-tuple-element.81.slab_ref, bf16[8,128]{1,0:T(8,128)(2,1)S(1)} %fusion.19.picker_ref), custom_call_target="tpu_custom_call" | custom-call | flops 147456 | bytes 1152 | tf_op jit(solution)/shard_map/mix/pallas_call | solution.py:354
  73.1 0.6 collective-permute-start.16
  73.6 0.9 collective-permute-done.16
  74.5 1.6 %collective-permute-start.17 = (bf16[4,4,1152]{2,1,0:T(4,128)(2,1)S(1)}, bf16[4,4,1152]{2,1,0:T(4,128)(2,1)S(1)}, u32[]{:S(2)}, u32[]{:S(2)}) collective-permute-start(bf16[4,4,1152]{2,1,0:T(4,128)(2,1)S(1)} %get-tuple-element.116), channel_id=1, source_target_pairs={{0,2},{1,3},{2,0},{3,1},{4,6},{5,7},{6,4},{7,5},{8,10},{9,11},{10,... | collective-permute-start | bytes 110600 | tf_op jit(solution)/shard_map/ppermute | solution.py:129
  76.1 2.5 %collective-permute-done.17 = bf16[4,4,1152]{2,1,0:T(4,128)(2,1)S(1)} collective-permute-done((bf16[4,4,1152]{2,1,0:T(4,128)(2,1)S(1)}, bf16[4,4,1152]{2,1,0:T(4,128)(2,1)S(1)}, u32[]{:S(2)}, u32[]{:S(2)}) %collective-permute-start.17) | collective-permute-done | bytes 36896 | tf_op jit(solution)/shard_map/ppermute | solution.py:129
  78.6 2.0 %collective-permute-start.18 = (bf16[4,4,1152]{2,1,0:T(4,128)(2,1)S(1)}, bf16[4,4,1152]{2,1,0:T(4,128)(2,1)S(1)}, u32[]{:S(2)}, u32[]{:S(2)}) collective-permute-start(bf16[4,4,1152]{2,1,0:T(4,128)(2,1)S(1)} %pad_maximum_fusion.5), channel_id=1, source_target_pairs={{0,4},{1,5},{2,6},{3,7},{4,0},{5,1},{6,2},{7,3},{8,12},{9,13},{10,... | collective-permute-start | bytes 110600 | tf_op jit(solution)/shard_map/ppermute | solution.py:129
  80.8 0.6 collective-permute-start.14
  81.9 3.0 %collective-permute-start.20 = (bf16[4,4,1152]{2,1,0:T(4,128)(2,1)S(1)}, bf16[4,4,1152]{2,1,0:T(4,128)(2,1)S(1)}, u32[]{:S(2)}, u32[]{:S(2)}) collective-permute-start(bf16[4,4,1152]{2,1,0:T(4,128)(2,1)S(1)} %pad_maximum_fusion.5), channel_id=1, source_target_pairs={{0,12},{1,13},{2,14},{3,15},{4,8},{5,9},{6,10},{7,11},{8,4},{9,5},... | collective-permute-start | bytes 110600 | tf_op jit(solution)/shard_map/ppermute | solution.py:129
  84.9 1.4 %collective-permute-done.19 = bf16[4,4,1152]{2,1,0:T(4,128)(2,1)S(1)} collective-permute-done((bf16[4,4,1152]{2,1,0:T(4,128)(2,1)S(1)}, bf16[4,4,1152]{2,1,0:T(4,128)(2,1)S(1)}, u32[]{:S(2)}, u32[]{:S(2)}) %collective-permute-start.19) | collective-permute-done | bytes 36896 | tf_op jit(solution)/shard_map/ppermute | solution.py:129
  86.3 1.3 %collective-permute-done.20 = bf16[4,4,1152]{2,1,0:T(4,128)(2,1)S(1)} collective-permute-done((bf16[4,4,1152]{2,1,0:T(4,128)(2,1)S(1)}, bf16[4,4,1152]{2,1,0:T(4,128)(2,1)S(1)}, u32[]{:S(2)}, u32[]{:S(2)}) %collective-permute-start.20) | collective-permute-done | bytes 36896 | tf_op jit(solution)/shard_map/ppermute | solution.py:129
  88.5 0.5 collective-permute-done.21
  89.6 0.9 convolution_convert_fusion
  90.5 6.9 %collective-permute-done.15 = bf16[128,1152]{1,0:T(8,128)(2,1)S(1)} collective-permute-done((bf16[128,1152]{1,0:T(8,128)(2,1)S(1)}, bf16[128,1152]{1,0:T(8,128)(2,1)S(1)}, u32[]{:S(2)}, u32[]{:S(2)}) %collective-permute-start.15) | collective-permute-done | bytes 294944 | tf_op jit(solution)/shard_map/ppermute | solution.py:129
  97.4 0.9 add_convert_fusion
  (72 shorter events, 4.6 us)
Async XLA Ops:
  0.6 5.4 %collective-permute-start.2 = (bf16[128,1152]{1,0:T(8,128)(2,1)}, bf16[128,1152]{1,0:T(8,128)(2,1)S(1)}, u32[]{:S(2)}, u32[]{:S(2)}) collective-permute-start(bf16[128,1152]{1,0:T(8,128)(2,1)} %refs_0_.1), channel_id=1, source_target_pairs={{0,1},{1,0},{2,3},{3,2},{4,5},{5,4},{6,7},{7,6},{8,9},{9,8},{10,11... | collective-permute-start | bytes 884744 | tf_op jit(solution)/shard_map/ppermute | solution.py:129
  1.1 11.6 %collective-permute-start = (bf16[128,1152]{1,0:T(8,128)(2,1)}, bf16[128,1152]{1,0:T(8,128)(2,1)S(1)}, u32[]{:S(2)}, u32[]{:S(2)}) collective-permute-start(bf16[128,1152]{1,0:T(8,128)(2,1)} %refs_0_.1), channel_id=1, source_target_pairs={{0,2},{1,3},{2,0},{3,1},{4,6},{5,7},{6,4},{7,5},{8,10},{9,11},{10,... | collective-permute-start | bytes 884744 | tf_op jit(solution)/shard_map/ppermute | solution.py:129
  3.7 9.3 %collective-permute-start.1 = (bf16[128,1152]{1,0:T(8,128)(2,1)}, bf16[128,1152]{1,0:T(8,128)(2,1)S(1)}, u32[]{:S(2)}, u32[]{:S(2)}) collective-permute-start(bf16[128,1152]{1,0:T(8,128)(2,1)} %refs_0_.1), channel_id=1, source_target_pairs={{0,4},{1,5},{2,6},{3,7},{4,0},{5,1},{6,2},{7,3},{8,12},{9,13},{10,... | collective-permute-start | bytes 884744 | tf_op jit(solution)/shard_map/ppermute | solution.py:129
  6.1 1.0 copy-start
  7.0 6.7 %copy-start.1 = (bf16[128,1152]{1,0:T(8,128)(2,1)S(1)}, bf16[128,1152]{1,0:T(8,128)(2,1)}, u32[]{:S(2)}) copy-start(bf16[128,1152]{1,0:T(8,128)(2,1)} %refs_0_.1) | copy-start | bytes 884740
  13.0 2.2 %collective-permute-start.4 = (bf16[128,1152]{1,0:T(8,128)(2,1)S(1)}, bf16[128,1152]{1,0:T(8,128)(2,1)S(1)}, u32[]{:S(2)}, u32[]{:S(2)}) collective-permute-start(bf16[128,1152]{1,0:T(8,128)(2,1)S(1)} %collective-permute-done.refs_0_), channel_id=1, source_target_pairs={{0,1},{1,0},{2,3},{3,2},{4,5},{5,4},{6,7},{7,6},{8,9},{9,8},{10,11... | collective-permute-start | bytes 884744 | tf_op jit(solution)/shard_map/ppermute | solution.py:129
  13.0 2.2 %collective-permute-start.5 = (bf16[128,1152]{1,0:T(8,128)(2,1)S(1)}, bf16[128,1152]{1,0:T(8,128)(2,1)S(1)}, u32[]{:S(2)}, u32[]{:S(2)}) collective-permute-start(bf16[128,1152]{1,0:T(8,128)(2,1)S(1)} %collective-permute-done.1.refs_1_), channel_id=1, source_target_pairs={{0,1},{1,0},{2,3},{3,2},{4,5},{5,4},{6,7},{7,6},{8,9},{9,8},{10,11... | collective-permute-start | bytes 884744 | tf_op jit(solution)/shard_map/ppermute | solution.py:129
  13.7 11.1 %copy-start.2 = (s32[128]{0:T(128)S(1)}, s32[128]{0:T(128)}, u32[]{:S(2)}) copy-start(s32[128]{0:T(128)} %param.9) | copy-start | bytes 1540
  13.7 10.9 %collective-permute-start.3 = (bf16[128,1152]{1,0:T(8,128)(2,1)S(1)}, bf16[128,1152]{1,0:T(8,128)(2,1)S(1)}, u32[]{:S(2)}, u32[]{:S(2)}) collective-permute-start(bf16[128,1152]{1,0:T(8,128)(2,1)S(1)} %copy-done.1), channel_id=1, source_target_pairs={{0,6},{1,7},{2,4},{3,5},{4,2},{5,3},{6,0},{7,1},{8,14},{9,15},{10,... | collective-permute-start | bytes 884744 | tf_op jit(solution)/shard_map/ppermute | solution.py:129
  24.6 1.6 %collective-permute-start.6 = (bf16[128,1152]{1,0:T(8,128)(2,1)S(1)}, bf16[128,1152]{1,0:T(8,128)(2,1)S(1)}, u32[]{:S(2)}, u32[]{:S(2)}) collective-permute-start(bf16[128,1152]{1,0:T(8,128)(2,1)S(1)} %collective-permute-done.3.refs_0_), channel_id=1, source_target_pairs={{0,1},{1,0},{2,3},{3,2},{4,5},{5,4},{6,7},{7,6},{8,9},{9,8},{10,11... | collective-permute-start | bytes 884744 | tf_op jit(solution)/shard_map/ppermute | solution.py:129
  29.0 8.0 %collective-permute-start.7 = (bf16[128,384]{1,0:T(8,128)(2,1)S(1)}, bf16[128,384]{1,0:T(8,128)(2,1)S(1)}, u32[]{:S(2)}, u32[]{:S(2)}) collective-permute-start(bf16[128,384]{1,0:T(8,128)(2,1)S(1)} %convert_element_type.97), channel_id=1, source_target_pairs={{0,8},{1,9},{2,10},{3,11},{4,12},{5,13},{6,14},{7,15},{8,0},{9,1},... | collective-permute-start | bytes 294920 | tf_op jit(solution)/shard_map/ppermute | solution.py:129
  37.5 14.3 %collective-permute-start.8 = (bf16[6,9,16,128]{3,2,1,0:T(8,128)(2,1)S(1)}, bf16[6,9,16,128]{3,2,1,0:T(8,128)(2,1)S(1)}, u32[]{:S(2)}, u32[]{:S(2)}) collective-permute-start(bf16[6,9,16,128]{3,2,1,0:T(8,128)(2,1)S(1)} %get-tuple-element.59), channel_id=1, source_target_pairs={{0,8},{1,9},{2,10},{3,11},{4,12},{5,13},{6,14},{7,15},{8,0},{9,1},... | collective-permute-start | bytes 663560 | tf_op jit(solution)/shard_map/ppermute | solution.py:129
  57.3 3.8 %collective-permute-start.9 = (bf16[128,1152]{1,0:T(8,128)(2,1)S(1)}, bf16[128,1152]{1,0:T(8,128)(2,1)S(1)}, u32[]{:S(2)}, u32[]{:S(2)}) collective-permute-start(bf16[128,1152]{1,0:T(8,128)(2,1)S(1)} %get-tuple-element.65), channel_id=1, source_target_pairs={{0,1},{1,0},{2,3},{3,2},{4,5},{5,4},{6,7},{7,6},{8,9},{9,8},{10,11... | collective-permute-start | bytes 884744 | tf_op jit(solution)/shard_map/ppermute | solution.py:129
  61.2 7.9 %collective-permute-start.10 = (bf16[128,1152]{1,0:T(8,128)(2,1)S(1)}, bf16[128,1152]{1,0:T(8,128)(2,1)S(1)}, u32[]{:S(2)}, u32[]{:S(2)}) collective-permute-start(bf16[128,1152]{1,0:T(8,128)(2,1)S(1)} %get-tuple-element.70), channel_id=1, source_target_pairs={{0,1},{1,0},{2,3},{3,2},{4,5},{5,4},{6,7},{7,6},{8,9},{9,8},{10,11... | collective-permute-start | bytes 884744 | tf_op jit(solution)/shard_map/ppermute | solution.py:129
  61.8 11.2 %collective-permute-start.12 = (bf16[128,1152]{1,0:T(8,128)(2,1)S(1)}, bf16[128,1152]{1,0:T(8,128)(2,1)S(1)}, u32[]{:S(2)}, u32[]{:S(2)}) collective-permute-start(bf16[128,1152]{1,0:T(8,128)(2,1)S(1)} %add_convert_fusion.3), channel_id=1, source_target_pairs={{0,6},{1,7},{2,4},{3,5},{4,2},{5,3},{6,0},{7,1},{8,14},{9,15},{10,... | collective-permute-start | bytes 884744 | tf_op jit(solution)/shard_map/ppermute | solution.py:129
  65.2 10.9 %copy-start.3 = (s32[4]{0:T(128)S(1)}, s32[4]{0:T(128)}, u32[]{:S(2)}) copy-start(s32[4]{0:T(128)} %param.11) | copy-start | bytes 52
  69.1 3.9 %collective-permute-start.11 = (bf16[128,1152]{1,0:T(8,128)(2,1)S(1)}, bf16[128,1152]{1,0:T(8,128)(2,1)S(1)}, u32[]{:S(2)}, u32[]{:S(2)}) collective-permute-start(bf16[128,1152]{1,0:T(8,128)(2,1)S(1)} %get-tuple-element.77), channel_id=1, source_target_pairs={{0,1},{1,0},{2,3},{3,2},{4,5},{5,4},{6,7},{7,6},{8,9},{9,8},{10,11... | collective-permute-start | bytes 884744 | tf_op jit(solution)/shard_map/ppermute | solution.py:129
  73.1 1.4 %collective-permute-start.16 = (bf16[4,4,1152]{2,1,0:T(4,128)(2,1)S(1)}, bf16[4,4,1152]{2,1,0:T(4,128)(2,1)S(1)}, u32[]{:S(2)}, u32[]{:S(2)}) collective-permute-start(bf16[4,4,1152]{2,1,0:T(4,128)(2,1)S(1)} %slice.104), channel_id=1, source_target_pairs={{0,1},{1,0},{2,3},{3,2},{4,5},{5,4},{6,7},{7,6},{8,9},{9,8},{10,11... | collective-permute-start | bytes 110600 | tf_op jit(solution)/shard_map/ppermute | solution.py:129
  74.5 4.0 %collective-permute-start.17 = (bf16[4,4,1152]{2,1,0:T(4,128)(2,1)S(1)}, bf16[4,4,1152]{2,1,0:T(4,128)(2,1)S(1)}, u32[]{:S(2)}, u32[]{:S(2)}) collective-permute-start(bf16[4,4,1152]{2,1,0:T(4,128)(2,1)S(1)} %get-tuple-element.116), channel_id=1, source_target_pairs={{0,2},{1,3},{2,0},{3,1},{4,6},{5,7},{6,4},{7,5},{8,10},{9,11},{10,... | collective-permute-start | bytes 110600 | tf_op jit(solution)/shard_map/ppermute | solution.py:129
  78.6 6.2 %collective-permute-start.18 = (bf16[4,4,1152]{2,1,0:T(4,128)(2,1)S(1)}, bf16[4,4,1152]{2,1,0:T(4,128)(2,1)S(1)}, u32[]{:S(2)}, u32[]{:S(2)}) collective-permute-start(bf16[4,4,1152]{2,1,0:T(4,128)(2,1)S(1)} %pad_maximum_fusion.5), channel_id=1, source_target_pairs={{0,4},{1,5},{2,6},{3,7},{4,0},{5,1},{6,2},{7,3},{8,12},{9,13},{10,... | collective-permute-start | bytes 110600 | tf_op jit(solution)/shard_map/ppermute | solution.py:129
  80.8 9.7 %collective-permute-start.14 = (bf16[128,1152]{1,0:T(8,128)(2,1)S(1)}, bf16[128,1152]{1,0:T(8,128)(2,1)S(1)}, u32[]{:S(2)}, u32[]{:S(2)}) collective-permute-start(bf16[128,1152]{1,0:T(8,128)(2,1)S(1)} %add_convert_fusion.2), channel_id=1, source_target_pairs={{0,2},{1,3},{2,0},{3,1},{4,6},{5,7},{6,4},{7,5},{8,10},{9,11},{10,... | collective-permute-start | bytes 884744 | tf_op jit(solution)/shard_map/ppermute | solution.py:129
  81.4 4.9 %collective-permute-start.19 = (bf16[4,4,1152]{2,1,0:T(4,128)(2,1)S(1)}, bf16[4,4,1152]{2,1,0:T(4,128)(2,1)S(1)}, u32[]{:S(2)}, u32[]{:S(2)}) collective-permute-start(bf16[4,4,1152]{2,1,0:T(4,128)(2,1)S(1)} %pad_maximum_fusion.5), channel_id=1, source_target_pairs={{0,8},{1,9},{2,10},{3,11},{4,12},{5,13},{6,14},{7,15},{8,0},{9,1},... | collective-permute-start | bytes 110600 | tf_op jit(solution)/shard_map/ppermute | solution.py:129
  81.9 5.8 %collective-permute-start.20 = (bf16[4,4,1152]{2,1,0:T(4,128)(2,1)S(1)}, bf16[4,4,1152]{2,1,0:T(4,128)(2,1)S(1)}, u32[]{:S(2)}, u32[]{:S(2)}) collective-permute-start(bf16[4,4,1152]{2,1,0:T(4,128)(2,1)S(1)} %pad_maximum_fusion.5), channel_id=1, source_target_pairs={{0,12},{1,13},{2,14},{3,15},{4,8},{5,9},{6,10},{7,11},{8,4},{9,5},... | collective-permute-start | bytes 110600 | tf_op jit(solution)/shard_map/ppermute | solution.py:129
  87.7 1.3 %collective-permute-start.21 = (bf16[2,4,4,1152]{3,2,1,0:T(4,128)(2,1)S(1)}, bf16[2,4,4,1152]{3,2,1,0:T(4,128)(2,1)S(1)}, u32[]{:S(2)}, u32[]{:S(2)}) collective-permute-start(bf16[2,4,4,1152]{3,2,1,0:T(4,128)(2,1)S(1)} %maximum_maximum_fusion), channel_id=1, source_target_pairs={{0,1},{1,0},{2,3},{3,2},{4,5},{5,4},{6,7},{7,6},{8,9},{9,8},{10,11... | collective-permute-start | bytes 221192 | tf_op jit(solution)/shard_map/ppermute | solution.py:129
  87.9 9.5 %collective-permute-start.15 = (bf16[128,1152]{1,0:T(8,128)(2,1)S(1)}, bf16[128,1152]{1,0:T(8,128)(2,1)S(1)}, u32[]{:S(2)}, u32[]{:S(2)}) collective-permute-start(bf16[128,1152]{1,0:T(8,128)(2,1)S(1)} %add_convert_fusion.1), channel_id=1, source_target_pairs={{0,4},{1,5},{2,6},{3,7},{4,0},{5,1},{6,2},{7,3},{8,12},{9,13},{10,... | collective-permute-start | bytes 884744 | tf_op jit(solution)/shard_map/ppermute | solution.py:129
  88.1 9.3 %collective-permute-start.13 = (bf16[128,1152]{1,0:T(8,128)(2,1)S(1)}, bf16[128,1152]{1,0:T(8,128)(2,1)S(1)}, u32[]{:S(2)}, u32[]{:S(2)}) collective-permute-start(bf16[128,1152]{1,0:T(8,128)(2,1)S(1)} %get-tuple-element.87), channel_id=1, source_target_pairs={{0,1},{1,0},{2,3},{3,2},{4,5},{5,4},{6,7},{7,6},{8,9},{9,8},{10,11... | collective-permute-start | bytes 884744 | tf_op jit(solution)/shard_map/ppermute | solution.py:129

commit v3 on v2

--- a/solution.py
+++ b/solution.py
@@ -119,7 +119,7 @@
 
 
 LANES = 128
-ROW_PIECES = 3
+ROW_CUTS = (0, 384, 768, 1152)
 ROW_TILE = 16
 MIB = 1024 * 1024
 
@@ -144,7 +144,8 @@
 def project(features, distances, running, w_qkv, my_group, columns, first_column):
     tokens, width = features[0].shape
     count = len(features)
-    piece = width // ROW_PIECES
+    cuts = [cut * width // ROW_CUTS[-1] for cut in ROW_CUTS]
+    pieces = list(zip(cuts, cuts[1:]))
     block_ids = jnp.stack([my_group ^ d for d in distances]).astype(jnp.int32)
     operands = list(features) + [w_qkv]
     if running is not None:
@@ -160,13 +161,16 @@
         out_ref, current, slabs, sems = refs[-4:]
 
         def copy(block, part):
-            rows = pl.ds(ids_ref[block] * width + part * piece, piece)
+            low, high = pieces[part]
+            rows = pl.ds(ids_ref[block] * width + low, high - low)
             return pltpu.make_async_copy(
-                w_ref.at[rows, pl.ds(first_column, columns)], slabs.at[block, part], sems.at[block, part]
+                w_ref.at[rows, pl.ds(first_column, columns)],
+                slabs.at[block, pl.ds(low, high - low)],
+                sems.at[block, part],
             )
 
         for block in range(count):
-            for part in range(ROW_PIECES):
+            for part in range(len(pieces)):
                 copy(block, part).start()
         for block in range(count):
             current[block] = feature_refs[block][...]
@@ -177,25 +181,30 @@
 
         @pl.loop(0, count)
         def _(block):
-            for part in range(ROW_PIECES):
+            for part in range(len(pieces)):
                 copy(block, part).wait()
                 out_ref[...] += jnp.dot(
-                    current[block, :, part * piece : (part + 1) * piece],
-                    slabs[block, part],
+                    current[block, :, pieces[part][0] : pieces[part][1]],
+                    slabs[block, pieces[part][0] : pieces[part][1]],
                     preferred_element_type=jnp.float32,
                 )
 
     return pl.pallas_call(
         kernel,
-        in_specs=[smem()] + [vmem()] * count + [anywhere()] + ([] if running is None else [vmem()]),
+        in_specs=[smem()]
+        + [vmem()] * count
+        + [anywhere()]
+        + ([] if running is None else [vmem()]),
         out_specs=vmem(),
         out_shape=jax.ShapeDtypeStruct((tokens, columns), jnp.float32),
         scratch_shapes=[
             pltpu.VMEM((count, tokens, width), jnp.bfloat16),
-            pltpu.VMEM((count, ROW_PIECES, piece, columns), jnp.bfloat16),
-            pltpu.SemaphoreType.DMA((count, ROW_PIECES)),
+            pltpu.VMEM((count, width, columns), jnp.bfloat16),
+            pltpu.SemaphoreType.DMA((count, len(pieces))),
         ],
-        compiler_params=pltpu.CompilerParams(vmem_limit_bytes=40 * MIB),
+        compiler_params=pltpu.CompilerParams(
+            vmem_limit_bytes=2 * count * width * (tokens + columns) + 2 * MIB
+        ),
         cost_estimate=pl.CostEstimate(
             flops=2 * count * tokens * width * columns,
             bytes_accessed=2 * count * width * columns,
@@ -203,6 +212,75 @@
         ),
         name="project",
     )(block_ids, *operands)
+
+
+def fetch_kv(block_ids, w_qkv, query_width):
+    count, rows = block_ids.shape[0], w_qkv.shape[0] // KVG
+    kv_width = w_qkv.shape[1] - query_width
+    pieces = len(ROW_CUTS) - 1
+    piece = rows // pieces
+
+    def kernel(ids_ref, w_ref, kv_ref, sems):
+        copies = [
+            pltpu.make_async_copy(
+                w_ref.at[pl.ds(ids_ref[block] * rows + part * piece, piece), pl.ds(query_width, kv_width)],
+                kv_ref.at[block, pl.ds(part * piece, piece)],
+                sems.at[block, part],
+            )
+            for block in range(count)
+            for part in range(pieces)
+        ]
+        for copy in copies:
+            copy.start()
+        for copy in copies:
+            copy.wait()
+
+    return pl.pallas_call(
+        kernel,
+        in_specs=[smem(), anywhere()],
+        out_specs=vmem(),
+        out_shape=pltpu.VMEM((count, rows, kv_width), jnp.bfloat16),
+        scratch_shapes=[pltpu.SemaphoreType.DMA((count, pieces))],
+        compiler_params=pltpu.CompilerParams(vmem_limit_bytes=32 * MIB),
+        cost_estimate=pl.CostEstimate(flops=rows, bytes_accessed=2 * rows * kv_width, transcendentals=0),
+        name="fetch_kv",
+    )(block_ids, w_qkv)
+
+
+def fold_tokens(rows):
+    half = rows.shape[0] // 2
+    return jnp.concatenate([rows[:half], rows[half:]], 1)
+
+
+def unfold_tokens(folded):
+    width = folded.shape[1] // 2
+    return jnp.concatenate([folded[:, :width], folded[:, width:]], 0)
+
+
+def finish_kv(features, running, w_kv):
+    tokens = running.shape[0]
+    columns = w_kv.shape[2]
+    first = running.shape[1] - columns
+
+    def kernel(*refs):
+        running_ref, w_ref, out_ref, key_ref = refs[-4:]
+        total = running_ref[:, first:]
+        for i, feature_ref in enumerate(refs[:-4]):
+            total += jnp.dot(feature_ref[...], w_ref[i], preferred_element_type=jnp.float32)
+        out_ref[...] = total
+        key_ref[...] = fold_tokens(total[:, :HD]).astype(jnp.bfloat16)
+
+    return pl.pallas_call(
+        kernel,
+        in_specs=[vmem()] * (len(features) + 2),
+        out_specs=[vmem()] * 2,
+        out_shape=[
+            jax.ShapeDtypeStruct((tokens, columns), jnp.float32),
+            jax.ShapeDtypeStruct((tokens // 2, columns), jnp.bfloat16),
+        ],
+        compiler_params=pltpu.CompilerParams(vmem_limit_bytes=8 * MIB),
+        name="finish_kv",
+    )(*features, running, w_kv)
 
 
 def packed_tiles(tokens):
@@ -218,14 +296,21 @@
     return places
 
 
-def partial_scores(queries, own_kv, partner_kv):
+def value_tiles(tokens):
+    return [
+        (slice(row, row + ROW_TILE), slice(lane, lane + LANES))
+        for row in range(0, tokens // 2, ROW_TILE)
+        for lane in range(0, 2 * HD, LANES)
+    ]
+
+
+def partial_scores(queries, own_kv, partner_keys):
     tokens = queries.shape[0]
     blocks = tokens // ROW_TILE
 
-    def kernel(query_ref, own_ref, partner_ref, value_ref, score_ref, packed_ref):
-        pair = (own_ref[...] + partner_ref[...].astype(jnp.float32)).astype(jnp.bfloat16)
-        keys = pair[:, :HD]
-        value_ref[...] = pair[:, HD:]
+    def kernel(query_ref, own_ref, partner_ref, score_ref, packed_ref):
+        partner_keys = unfold_tokens(partner_ref[...].astype(jnp.float32))
+        keys = (own_ref[:, :HD] + partner_keys).astype(jnp.bfloat16)
         lane = lax.broadcasted_iota(jnp.int32, (ROW_TILE, tokens), 1)
         for first in range(0, HPG, 2):
             tiles = [None] * (blocks + 1)
@@ -241,21 +326,25 @@
                     rows = jnp.where(lane < shift, tiles[tile], pltpu.roll(rows, shift, 1))
                 tiles[tile] = rows
             for tile, rows in enumerate(tiles):
-                packed_ref[first // 2, tile] = rows.astype(jnp.bfloat16)
+                packed_ref[first // 2 * (blocks + 1) + tile] = rows.astype(jnp.bfloat16)
+        folded = fold_tokens(own_ref[:, HD:])
+        for tile, place in enumerate(value_tiles(tokens)):
+            packed_ref[HPG // 2 * (blocks + 1) + tile] = folded[place].astype(jnp.bfloat16)
 
     return pl.pallas_call(
         kernel,
         out_shape=[
-            jax.ShapeDtypeStruct((tokens, HD), jnp.bfloat16),
             jax.ShapeDtypeStruct((HPG, tokens, tokens), jnp.float32),
-            jax.ShapeDtypeStruct((HPG // 2, blocks + 1, ROW_TILE, tokens), jnp.bfloat16),
+            jax.ShapeDtypeStruct(
+                (HPG // 2 * (blocks + 1) + len(value_tiles(tokens)), ROW_TILE, tokens), jnp.bfloat16
+            ),
         ],
         compiler_params=pltpu.CompilerParams(vmem_limit_bytes=16 * MIB),
         cost_estimate=pl.CostEstimate(
             flops=2 * HPG * tokens * tokens * HD, bytes_accessed=2 * tokens * HPG * HD, transcendentals=0
         ),
         name="partial_scores",
-    )(queries, own_kv, partner_kv)
+    )(queries, own_kv, partner_keys)
 
 
 def fetch_rows(block_ids, w_out, count):
@@ -288,33 +377,41 @@
     )(block_ids, w_out)
 
 
-def mix_chip(attended, slab_ref, picker, even_ref, odd_ref, end_ref):
+def mix_chip(attended, slab_ref, even_ref, odd_ref, end_ref):
+    tokens, end_rows = even_ref.shape[0], end_ref.shape[1]
     for core, out_ref in enumerate((even_ref, odd_ref)):
-        part = contract_last(attended[...], slab_ref[core]).astype(jnp.bfloat16)
-        out_ref[...] = part
-        end_ref[core] = jnp.dot(picker[...], part, preferred_element_type=jnp.float32)
-
-
-def chip_shapes(tokens, rows, picker):
+        part = contract_last(attended[...], slab_ref[core])
+        out_ref[...] = part[:tokens].astype(jnp.bfloat16)
+        end_ref[core] = part[tokens : tokens + end_rows]
+
+
+def chip_shapes(tokens, rows, end_rows):
     part = jax.ShapeDtypeStruct((tokens, rows), jnp.bfloat16)
-    return [part, part, jax.ShapeDtypeStruct((2, picker.shape[0], rows), jnp.float32)]
-
-
-def attend_and_mix(own_scores, partner_scores, values, allowed, slabs, picker):
+    return [part, part, jax.ShapeDtypeStruct((2, end_rows, rows), jnp.float32)]
+
+
+def attend_and_mix(own_scores, partner_scores, own_kv, allowed, slabs, picker, end_rows):
     heads, tokens = own_scores.shape[:2]
     blocks = tokens // ROW_TILE
     count, rows, columns = slabs.shape
     scale = 1.0 / math.sqrt(HD)
 
     def kernel(
-        own_ref, partner_ref, value_ref, allowed_ref, slab_ref, picker_ref,
+        own_ref, partner_ref, own_kv_ref, allowed_ref, slab_ref, picker_ref,
         attended_ref, even_ref, odd_ref, end_ref,
     ):
         mask = allowed_ref[...] > 0.0
+        first_tile = heads // 2 * (blocks + 1)
+        tiles = [partner_ref[first_tile + tile].astype(jnp.float32) for tile in range(len(value_tiles(tokens)))]
+        across = 2 * HD // LANES
+        folded = jnp.concatenate(
+            [jnp.concatenate(tiles[i : i + across], 1) for i in range(0, len(tiles), across)], 0
+        )
+        value = (own_kv_ref[:, HD:] + unfold_tokens(folded)).astype(jnp.bfloat16)
         for two in range(heads // 2):
             partner = [[None] * blocks, [None] * blocks]
             for tile, head, block, shift in packed_tiles(tokens):
-                rows_of = partner_ref[two, tile].astype(jnp.float32)
+                rows_of = partner_ref[two * (blocks + 1) + tile].astype(jnp.float32)
                 partner[head][block] = pltpu.roll(rows_of, tokens - shift, 1) if shift else rows_of
             for core in range(2):
                 head = 2 * two + core
@@ -323,17 +420,20 @@
                 weights = jnp.where(mask, jnp.exp(scores - row_max), 0.0)
                 totals = jnp.sum(weights, axis=1, keepdims=True)
                 mixed_heads = jnp.dot(
-                    weights.astype(jnp.bfloat16), value_ref[...], preferred_element_type=jnp.float32
+                    weights.astype(jnp.bfloat16), value, preferred_element_type=jnp.float32
                 )
-                attended_ref[:, head * HD : (head + 1) * HD] = (mixed_heads / totals).astype(jnp.bfloat16)
-        mix_chip(attended_ref, slab_ref, picker_ref, even_ref, odd_ref, end_ref)
+                attended_ref[:tokens, head * HD : (head + 1) * HD] = (mixed_heads / totals).astype(jnp.bfloat16)
+        attended_ref[tokens:] = jnp.dot(
+            picker_ref[...], attended_ref[:tokens], preferred_element_type=jnp.float32
+        ).astype(jnp.bfloat16)
+        mix_chip(attended_ref, slab_ref, even_ref, odd_ref, end_ref)
 
     return pl.pallas_call(
         kernel,
         in_specs=[vmem()] * 6,
         out_specs=[vmem()] * 4,
-        out_shape=[jax.ShapeDtypeStruct((tokens, columns), jnp.bfloat16)]
-        + chip_shapes(tokens, rows, picker),
+        out_shape=[jax.ShapeDtypeStruct((tokens + picker.shape[0], columns), jnp.bfloat16)]
+        + chip_shapes(tokens, rows, end_rows),
         compiler_params=pltpu.CompilerParams(vmem_limit_bytes=8 * MIB),
         cost_estimate=pl.CostEstimate(
             flops=4 * tokens * rows * columns,
@@ -341,25 +441,24 @@
             transcendentals=heads * tokens * tokens,
         ),
         name="attend_and_mix",
-    )(own_scores, partner_scores, values, allowed, slabs, picker)
-
-
-def mix(attended, slabs, picker):
-    tokens = attended.shape[0]
+    )(own_scores, partner_scores, own_kv, allowed, slabs, picker)
+
+
+def mix(attended, slabs, tokens, end_rows):
     rows, columns = slabs.shape[1:]
 
-    def kernel(attended_ref, slab_ref, picker_ref, even_ref, odd_ref, end_ref):
-        mix_chip(attended_ref, slab_ref, picker_ref, even_ref, odd_ref, end_ref)
+    def kernel(attended_ref, slab_ref, even_ref, odd_ref, end_ref):
+        mix_chip(attended_ref, slab_ref, even_ref, odd_ref, end_ref)
 
     return pl.pallas_call(
         kernel,
-        in_specs=[vmem()] * 3,
+        in_specs=[vmem()] * 2,
         out_specs=[vmem()] * 3,
-        out_shape=chip_shapes(tokens, rows, picker),
+        out_shape=chip_shapes(tokens, rows, end_rows),
         compiler_params=pltpu.CompilerParams(vmem_limit_bytes=8 * MIB),
         cost_estimate=pl.CostEstimate(flops=tokens * rows, bytes_accessed=rows, transcendentals=0),
         name="mix",
-    )(attended, slabs, picker)
+    )(attended, slabs)
 
 
 def add_rounded(left, right):
@@ -387,15 +486,7 @@
     tokens = hidden.shape[0]
     query_width = HPG * HD
     together = lax.optimization_barrier
-    positions = jnp.arange(tokens, dtype=jnp.int32)
-    allowed = (
-        (segment_ids[:, None] == segment_ids[None, :]) & (positions[None, :] <= positions[:, None])
-    ).astype(jnp.float32)
     completions = owners.shape[0]
-    end_rows = -(-completions // 8) * 8
-    picker = (
-        jnp.pad(end_positions, (0, end_rows - completions), constant_values=-1)[:, None] == positions[None, :]
-    ).astype(jnp.bfloat16)
     same_owner = owners[:, None] == owners[None, :]
     earlier = jnp.arange(completions)[None, :] < jnp.arange(completions)[:, None]
     order_rank = jnp.sum((same_owner & earlier).astype(jnp.int32), axis=1)
@@ -408,55 +499,67 @@
     near_core = xor_swap(hidden, 1)
     from_y, from_z = xor_swap(hidden, 2), xor_swap(hidden, 4)
     early = project([hidden, near_core], (0, 1), None, w_qkv, my_group, columns, 0)
+    block_ids = (my_group ^ jnp.arange(KVG, dtype=jnp.int32)).astype(jnp.int32)
     from_y, from_z, sent, early = together((from_y, from_z, hidden, early))
     from_both = xor_swap(sent, 6)
     from_y_core, from_z_core = xor_swap(from_y, 1), xor_swap(from_z, 1)
     middle = project(
         [from_y, from_z, from_y_core, from_z_core], (2, 4, 3, 5), early, w_qkv, my_group, columns, 0
     )
-    from_both, middle = together((from_both, middle))
+    from_both, middle, block_ids, segment_ids, end_positions = together(
+        (from_both, middle, block_ids, segment_ids, end_positions)
+    )
+    w_kv = fetch_kv(block_ids[KVG - 2 :], w_qkv, query_width)
+    positions = jnp.arange(tokens, dtype=jnp.int32)
+    allowed = (
+        (segment_ids[:, None] == segment_ids[None, :]) & (positions[None, :] <= positions[:, None])
+    ).astype(jnp.float32)
+    end_rows = -(-completions // 8) * 8
+    picked_rows = -(-completions // ROW_TILE) * ROW_TILE
+    picker = (
+        jnp.pad(end_positions, (0, picked_rows - completions), constant_values=-1)[:, None] == positions[None, :]
+    ).astype(jnp.bfloat16)
     late = [from_both, xor_swap(from_both, 1)]
-    own_kv = project(late, (6, 7), middle, w_qkv, my_group, 2 * HD, query_width)
-    partner_kv = xor_swap(own_kv.astype(jnp.bfloat16), KVG)
+    own_kv, folded_keys = finish_kv(late, middle, w_kv)
+    partner_keys = xor_swap(folded_keys, KVG)
     middle, own_kv = together((middle, own_kv))
     queries = project(late, (6, 7), middle, w_qkv, my_group, query_width, 0)
 
-    values, scores, packed = partial_scores(queries, own_kv, partner_kv)
-    block_ids = (my_group ^ jnp.arange(KVG, dtype=jnp.int32)).astype(jnp.int32)
+    scores, packed = partial_scores(queries, own_kv, partner_keys)
     packed, block_ids = together((packed, block_ids))
     arrived = xor_swap(packed, KVG)
     own_slabs, slabs_y, slabs_z, slabs_both = fetch_rows(block_ids, w_out, KVG)
     arrived, slabs_both = together((arrived, slabs_both))
     attended, even_both, odd_both, ends_both = attend_and_mix(
-        scores, arrived, values, allowed, slabs_both, picker
+        scores, arrived, own_kv, allowed, slabs_both, picker, end_rows
     )
     odd_both = xor_swap(odd_both, 1)
-    even_y, odd_y, ends_y = mix(attended, slabs_y, picker)
+    even_y, odd_y, ends_y = mix(attended, slabs_y, tokens, end_rows)
     odd_both, even_y, odd_y = together((odd_both, even_y, odd_y))
     odd_y = xor_swap(odd_y, 1)
     near_both, attended = together((add_rounded(even_both, odd_both), attended))
     sum_both = xor_swap(near_both, 6)
-    even_z, odd_z, ends_z = mix(attended, slabs_z, picker)
+    even_z, odd_z, ends_z = mix(attended, slabs_z, tokens, end_rows)
     odd_y, even_z, odd_z = together((odd_y, even_z, odd_z))
     odd_z = xor_swap(odd_z, 1)
     near_y, attended = together((add_rounded(even_y, odd_y), attended))
-    sum_y = xor_swap(near_y, 2)
-    even_own, odd_own, ends_own = mix(attended, own_slabs, picker)
+    even_own, odd_own, ends_own = mix(attended, own_slabs, tokens, end_rows)
     odd_z, even_own, odd_own, ends_own, sum_both = together((odd_z, even_own, odd_own, ends_own, sum_both))
-    sum_z = xor_swap(add_rounded(even_z, odd_z), 4)
+    near_z = add_rounded(even_z, odd_z)
 
     end_parts = jnp.concatenate([ends_own, ends_y, ends_z, ends_both])[:, :completions]
     end_far = xor_swap(end_parts[1::2].astype(jnp.bfloat16), 1)
     ends = end_parts[0::2] + end_far.astype(jnp.float32)
-    got = xor_swap(ends.astype(jnp.bfloat16), 2).astype(jnp.float32)
-    odd_own = xor_swap(odd_own, 1)
-    ends = [ends[i] + got[i ^ 1] for i in range(KVG // 2)]
-    message = jnp.stack(ends).astype(jnp.bfloat16)
-    got = xor_swap(message, 4).astype(jnp.float32)
-    own_ends = jnp.stack([ends[i] + got[i ^ 2] for i in range(KVG // 2)]).astype(jnp.bfloat16)
-    got = [xor_swap(message, KVG).astype(jnp.float32), xor_swap(message, KVG ^ 4).astype(jnp.float32)]
-    other_ends = jnp.stack([got[0][i] + got[1][i ^ 2] for i in range(KVG // 2)]).astype(jnp.bfloat16)
-    both = jnp.stack([own_ends, other_ends])
+    ends, odd_own, near_y, near_z = together((ends, xor_swap(odd_own, 1), near_y, near_z))
+    message = ends.astype(jnp.bfloat16)
+    ends = [ends[i] for i in range(KVG // 2)]
+    for distance in range(2, KVG, 2):
+        got = xor_swap(message, distance).astype(jnp.float32)
+        ends = [ends[i] + got[i ^ distance // 2] for i in range(KVG // 2)]
+    sum_y, sum_z = xor_swap(near_y, 2), xor_swap(near_z, 4)
+    ends = jnp.stack(ends).astype(jnp.bfloat16)
+    both = jnp.stack([ends, xor_swap(ends, KVG)])
+    both, sum_y, sum_z = together((both, sum_y, sum_z))
     both_far = xor_swap(both, 1)
     halves = []
     for half in range(2):

time: 98.5 us -> 89.2 us (0.906)
  starting transfers between devices: 22.8 us -> 18.5 us
  waiting for transfers between devices: 15.2 us -> 13.1 us
  local copies, waits for them, and re-layouts: 1.65 us -> 0.1 us
  Pallas kernels: 54.4 us -> 53.2 us
    ppermute x22, starting transfers between devices: 22.8 us -> 18.5 us  [xor_swap(): lax.ppermute(block, 'gx', [(low, low ^ distance) for low in range(count)])]
    pallas_call x4 -> x3, Pallas kernels: 23.2 us -> 20.9 us  [project(): pl.pallas_call(kernel, in_specs=[smem()] + [vmem()] * count + [anywhere()...]
    ppermute x22, waiting for transfers between devices: 15.2 us -> 13.1 us  [xor_swap(): lax.ppermute(block, 'gx', [(low, low ^ distance) for low in range(count)])]
    pallas_call x4 -> x6, Pallas kernels: 12 us -> 13.4 us  [the longest x3 10.4 us: mix(): pl.pallas_call(kernel, in_specs=[vmem()] * 2, out_specs=[vmem()] * 3, out...]
  transfers between devices with their start and end apart: 22 -> 22, of which waited for: 8 -> 11; matrix products, arithmetic and copies ran while one was open for 3% -> 2% of each run, Pallas kernels for 47% -> 53%
where the time goes in v3:
time: 89.2 us; the launch traced here: 89 us
  Pallas kernels  53.2 us (60%)
  starting transfers between devices  18.5 us (21%)
  waiting for transfers between devices  13.1 us (15%)
  other arithmetic  2.41 us (3%)
  between operations  0.96 us (1%)
    pallas_call x3, Pallas kernels, project(): pl.pallas_call(kernel, in_specs=[smem()] + [vmem()] * count + [anywhere()...  20.9 us
    ppermute x22, starting transfers between devices, xor_swap(): lax.ppermute(block, 'gx', [(low, low ^ distance) for low in range(count)])  18.5 us
    pallas_call x1, Pallas kernels, fetch_rows(): pl.pallas_call(kernel, in_specs=[smem(), anywhere()], out_specs=[vmem()]...  13.8 us
    ppermute x22, waiting for transfers between devices, xor_swap(): lax.ppermute(block, 'gx', [(low, low ^ distance) for low in range(count)])  13.1 us
    pallas_call x3, Pallas kernels, mix(): pl.pallas_call(kernel, in_specs=[vmem()] * 2, out_specs=[vmem()] * 3, out...  10.4 us
    pallas_call x1, Pallas kernels, attend_and_mix(): pl.pallas_call(kernel, in_specs=[vmem()] * 6, out_specs=[vmem()] * 4, out...  5.08 us
    pallas_call x1, Pallas kernels, fetch_kv(): pl.pallas_call(kernel, in_specs=[smem(), anywhere()], out_specs=vmem(), o...  2.02 us
  transfers between devices with their start and end apart: 22, of which 11 were waited for; matrix products, arithmetic and copies ran while one was open for 2% of the time, Pallas kernels for 53%

profile of v3, /device:TPU:0, one launch (start us, length us, event | category | flops | bytes accessed | tf_op | source)
XLA Modules:
  0.0 89.0 jit_solution(15046498032125857898)
XLA Ops:
  0.6 0.5 collective-permute-start.2
  1.1 2.6 %collective-permute-start = (bf16[128,1152]{1,0:T(8,128)(2,1)}, bf16[128,1152]{1,0:T(8,128)(2,1)S(1)}, u32[]{:S(2)}, u32[]{:S(2)}) collective-permute-start(bf16[128,1152]{1,0:T(8,128)(2,1)} %refs_0_.1), channel_id=1, source_target_pairs={{0,2},{1,3},{2,0},{3,1},{4,6},{5,7},{6,4},{7,5},{8,10},{9,11},{10,... | collective-permute-start | bytes 884744 | tf_op jit(solution)/shard_map/ppermute | solution.py:129
  3.7 1.6 %collective-permute-start.1 = (bf16[128,1152]{1,0:T(8,128)(2,1)}, bf16[128,1152]{1,0:T(8,128)(2,1)S(1)}, u32[]{:S(2)}, u32[]{:S(2)}) collective-permute-start(bf16[128,1152]{1,0:T(8,128)(2,1)} %refs_0_.1), channel_id=1, source_target_pairs={{0,4},{1,5},{2,6},{3,7},{4,0},{5,1},{6,2},{7,3},{8,12},{9,13},{10,... | collective-permute-start | bytes 884744 | tf_op jit(solution)/shard_map/ppermute | solution.py:129
  5.4 6.2 %project.3.refs_5_ = f32[128,2688]{1,0:T(8,128)S(1)} custom-call(s32[2]{0:T(128)S(1)} %pad_add_fusion.1.ids_ref, bf16[128,1152]{1,0:T(8,128)(2,1)} %refs_0_.1, bf16[128,1152]{1,0:T(8,128)(2,1)S(1)} %collective-permute-done.2.refs_1_, bf16[9216,2688]{1,0:T(8,128)(2,1)} %refs_2_.3), custom_call_target="tpu_custom_call" | custom-call | flops 1585446912 | bytes 12386304 | tf_op jit(solution)/shard_map/project/pallas_call | solution.py:192
  11.6 1.4 %collective-permute-done.1.refs_1_ = bf16[128,1152]{1,0:T(8,128)(2,1)S(1)} collective-permute-done((bf16[128,1152]{1,0:T(8,128)(2,1)}, bf16[128,1152]{1,0:T(8,128)(2,1)S(1)}, u32[]{:S(2)}, u32[]{:S(2)}) %collective-permute-start.1) | collective-permute-done | bytes 294944 | tf_op jit(solution)/shard_map/ppermute | solution.py:129
  13.0 0.5 collective-permute-start.5
  13.7 1.5 %collective-permute-start.3 = (bf16[128,1152]{1,0:T(8,128)(2,1)}, bf16[128,1152]{1,0:T(8,128)(2,1)S(1)}, u32[]{:S(2)}, u32[]{:S(2)}) collective-permute-start(bf16[128,1152]{1,0:T(8,128)(2,1)} %refs_0_.1), channel_id=1, source_target_pairs={{0,6},{1,7},{2,4},{3,5},{4,2},{5,3},{6,0},{7,1},{8,14},{9,15},{10,... | collective-permute-start | bytes 884744 | tf_op jit(solution)/shard_map/ppermute | solution.py:129
  15.2 9.4 %project.4.refs_2_.refs_3_ = f32[128,2688]{1,0:T(8,128)S(1)} custom-call(s32[4]{0:T(128)S(1)} %pad_add_fusion.2.ids_ref, bf16[128,1152]{1,0:T(8,128)(2,1)S(1)} %collective-permute-done.refs_0_, bf16[128,1152]{1,0:T(8,128)(2,1)S(1)} %collective-permute-done.1.refs_1_, bf16[128,1152]{1,0:T(8,128)(2,1)S(1)} %collective-permute-done.4.refs_2_, ...), custom_call_target="tpu_custom_call" | custom-call | flops 3170893824 | bytes 24772608 | tf_op jit(solution)/shard_map/project/pallas_call | solution.py:192
  24.8 2.0 %fetch_kv.1.refs_3_ = bf16[2,1152,384]{2,1,0:T(8,128)(2,1)S(1)} custom-call(s32[2]{0:T(128)S(1)} %slice.109.ids_ref, bf16[9216,2688]{1,0:T(8,128)(2,1)} %refs_2_.3), custom_call_target="tpu_custom_call" | custom-call | flops 1152 | bytes 884736 | tf_op jit(solution)/shard_map/fetch_kv/pallas_call | solution.py:238
  26.9 0.5 finish_kv.1
  27.5 2.7 %collective-permute-start.7 = (bf16[64,384]{1,0:T(8,128)(2,1)S(1)}, bf16[64,384]{1,0:T(8,128)(2,1)S(1)}, u32[]{:S(2)}, u32[]{:S(2)}) collective-permute-start(bf16[64,384]{1,0:T(8,128)(2,1)S(1)} %get-tuple-element.70), channel_id=1, source_target_pairs={{0,8},{1,9},{2,10},{3,11},{4,12},{5,13},{6,14},{7,15},{8,0},{9,1},... | collective-permute-start | bytes 147464 | tf_op jit(solution)/shard_map/ppermute | solution.py:129
  30.1 5.3 %project.5.query_ref = f32[128,2304]{1,0:T(8,128)S(1)} custom-call(s32[2]{0:T(128)S(1)} %pad_add_fusion.ids_ref, bf16[128,1152]{1,0:T(8,128)(2,1)S(1)} %collective-permute-done.3.refs_0_, bf16[128,1152]{1,0:T(8,128)(2,1)S(1)} %collective-permute-done.6.refs_1_, bf16[9216,2688]{1,0:T(8,128)(2,1)} %refs_2_.3, f32[128,2688]{1,0:T(8,128)S(1)} %project.4.refs_2_.refs_3_), custom_call_target="tpu_custom_call" | custom-call | flops 1358954496 | bytes 10616832 | tf_op jit(solution)/shard_map/project/pallas_call | solution.py:192
  35.5 0.5 partial_scores.1
  36.4 13.8 %fetch_rows.1 = (bf16[2,1152,2304]{2,1,0:T(8,128)(2,1)S(1)}, bf16[2,1152,2304]{2,1,0:T(8,128)(2,1)S(1)}, bf16[2,1152,2304]{2,1,0:T(8,128)(2,1)S(1)}, bf16[2,1152,2304]{2,1,0:T(8,128)(2,1)S(1)}) custom-call(s32[8]{0:T(128)S(1)} %iota_xor_fusion.ids_ref, bf16[9216,2304]{1,0:T(8,128)(2,1)} %w_ref.3), custom_call_target="tpu_custom_call" | custom-call | flops 5435817984 | bytes 42467328 | tf_op jit(solution)/shard_map/fetch_rows/pallas_call | solution.py:366
  50.2 1.2 %collective-permute-done.8.partner_ref = bf16[66,16,128]{2,1,0:T(8,128)(2,1)S(1)} collective-permute-done((bf16[66,16,128]{2,1,0:T(8,128)(2,1)S(1)}, bf16[66,16,128]{2,1,0:T(8,128)(2,1)S(1)}, u32[]{:S(2)}, u32[]{:S(2)}) %collective-permute-start.8) | collective-permute-done | bytes 270368 | tf_op jit(solution)/shard_map/ppermute | solution.py:129
  51.4 5.1 %attend_and_mix.1 = (bf16[144,2304]{1,0:T(8,128)(2,1)S(1)}, bf16[128,1152]{1,0:T(8,128)(2,1)S(1)}, bf16[128,1152]{1,0:T(8,128)(2,1)S(1)}, f32[2,8,1152]{2,1,0:T(8,128)S(1)}) custom-call(f32[12,128,128]{2,1,0:T(8,128)S(1)} %get-tuple-element.71.own_ref, bf16[66,16,128]{2,1,0:T(8,128)(2,1)S(1)} %collective-permute-done.8.partner_ref, ...), custom_call_target="tpu_custom_call" | custom-call | flops 1358954496 | bytes 10616832 | tf_op jit(solution)/shard_map/attend_and_mix/pallas_call | solution.py:431
  56.5 3.5 %mix.3 = (bf16[128,1152]{1,0:T(8,128)(2,1)S(1)}, bf16[128,1152]{1,0:T(8,128)(2,1)S(1)}, f32[2,8,1152]{2,1,0:T(8,128)S(1)}) custom-call(bf16[144,2304]{1,0:T(8,128)(2,1)S(1)} %get-tuple-element.95.attended_ref, bf16[2,1152,2304]{2,1,0:T(8,128)(2,1)S(1)} %get-tuple-element.82.slab_ref), custom_call_target="tpu_custom_call" | custom-call | flops 147456 | bytes 1152 | tf_op jit(solution)/shard_map/mix/pallas_call | solution.py:453
  60.0 0.6 collective-permute-start.10
  61.0 3.5 %mix.4 = (bf16[128,1152]{1,0:T(8,128)(2,1)S(1)}, bf16[128,1152]{1,0:T(8,128)(2,1)S(1)}, f32[2,8,1152]{2,1,0:T(8,128)S(1)}) custom-call(bf16[144,2304]{1,0:T(8,128)(2,1)S(1)} %get-tuple-element.95.attended_ref, bf16[2,1152,2304]{2,1,0:T(8,128)(2,1)S(1)} %get-tuple-element.89.slab_ref), custom_call_target="tpu_custom_call" | custom-call | flops 147456 | bytes 1152 | tf_op jit(solution)/shard_map/mix/pallas_call | solution.py:453
  64.6 3.5 %mix.5 = (bf16[128,1152]{1,0:T(8,128)(2,1)S(1)}, bf16[128,1152]{1,0:T(8,128)(2,1)S(1)}, f32[2,8,1152]{2,1,0:T(8,128)S(1)}) custom-call(bf16[144,2304]{1,0:T(8,128)(2,1)S(1)} %get-tuple-element.95.attended_ref, bf16[2,1152,2304]{2,1,0:T(8,128)(2,1)S(1)} %get-tuple-element.96.slab_ref), custom_call_target="tpu_custom_call" | custom-call | flops 147456 | bytes 1152 | tf_op jit(solution)/shard_map/mix/pallas_call | solution.py:453
  68.1 2.5 %collective-permute-done.12 = bf16[128,1152]{1,0:T(8,128)(2,1)S(1)} collective-permute-done((bf16[128,1152]{1,0:T(8,128)(2,1)S(1)}, bf16[128,1152]{1,0:T(8,128)(2,1)S(1)}, u32[]{:S(2)}, u32[]{:S(2)}) %collective-permute-start.12) | collective-permute-done | bytes 294944 | tf_op jit(solution)/shard_map/ppermute | solution.py:129
  70.7 0.5 collective-permute-start.14
  71.3 0.6 collective-permute-done.13
  72.4 1.5 %collective-permute-start.15 = (bf16[4,4,1152]{2,1,0:T(4,128)(2,1)S(1)}, bf16[4,4,1152]{2,1,0:T(4,128)(2,1)S(1)}, u32[]{:S(2)}, u32[]{:S(2)}) collective-permute-start(bf16[4,4,1152]{2,1,0:T(4,128)(2,1)S(1)} %convert_element_type.96), channel_id=1, source_target_pairs={{0,2},{1,3},{2,0},{3,1},{4,6},{5,7},{6,4},{7,5},{8,10},{9,11},{10,... | collective-permute-start | bytes 110600 | tf_op jit(solution)/shard_map/ppermute | solution.py:129
  73.9 2.1 %collective-permute-start.17 = (bf16[4,4,1152]{2,1,0:T(4,128)(2,1)S(1)}, bf16[4,4,1152]{2,1,0:T(4,128)(2,1)S(1)}, u32[]{:S(2)}, u32[]{:S(2)}) collective-permute-start(bf16[4,4,1152]{2,1,0:T(4,128)(2,1)S(1)} %convert_element_type.96), channel_id=1, source_target_pairs={{0,6},{1,7},{2,4},{3,5},{4,2},{5,3},{6,0},{7,1},{8,14},{9,15},{10,... | collective-permute-start | bytes 110600 | tf_op jit(solution)/shard_map/ppermute | solution.py:129
  76.0 1.4 %collective-permute-start.19 = (bf16[128,1152]{1,0:T(8,128)(2,1)S(1)}, bf16[128,1152]{1,0:T(8,128)(2,1)S(1)}, u32[]{:S(2)}, u32[]{:S(2)}) collective-permute-start(bf16[128,1152]{1,0:T(8,128)(2,1)S(1)} %add_convert_fusion.2), channel_id=1, source_target_pairs={{0,2},{1,3},{2,0},{3,1},{4,6},{5,7},{6,4},{7,5},{8,10},{9,11},{10,... | collective-permute-start | bytes 884744 | tf_op jit(solution)/shard_map/ppermute | solution.py:129
  77.9 1.0 %collective-permute-done.17 = bf16[4,4,1152]{2,1,0:T(4,128)(2,1)S(1)} collective-permute-done((bf16[4,4,1152]{2,1,0:T(4,128)(2,1)S(1)}, bf16[4,4,1152]{2,1,0:T(4,128)(2,1)S(1)}, u32[]{:S(2)}, u32[]{:S(2)}) %collective-permute-start.17) | collective-permute-done | bytes 36896 | tf_op jit(solution)/shard_map/ppermute | solution.py:129
  79.0 2.1 %collective-permute-start.18 = (bf16[4,4,1152]{2,1,0:T(4,128)(2,1)S(1)}, bf16[4,4,1152]{2,1,0:T(4,128)(2,1)S(1)}, u32[]{:S(2)}, u32[]{:S(2)}) collective-permute-start(bf16[4,4,1152]{2,1,0:T(4,128)(2,1)S(1)} %pad_maximum_fusion.6), channel_id=1, source_target_pairs={{0,8},{1,9},{2,10},{3,11},{4,12},{5,13},{6,14},{7,15},{8,0},{9,1},... | collective-permute-start | bytes 110600 | tf_op jit(solution)/shard_map/ppermute | solution.py:129
  81.2 3.3 %collective-permute-done.18 = bf16[4,4,1152]{2,1,0:T(4,128)(2,1)S(1)} collective-permute-done((bf16[4,4,1152]{2,1,0:T(4,128)(2,1)S(1)}, bf16[4,4,1152]{2,1,0:T(4,128)(2,1)S(1)}, u32[]{:S(2)}, u32[]{:S(2)}) %collective-permute-start.18) | collective-permute-done | bytes 36896 | tf_op jit(solution)/shard_map/ppermute | solution.py:129
  84.9 1.5 %collective-permute-done.20 = bf16[128,1152]{1,0:T(8,128)(2,1)S(1)} collective-permute-done((bf16[128,1152]{1,0:T(8,128)(2,1)S(1)}, bf16[128,1152]{1,0:T(8,128)(2,1)S(1)}, u32[]{:S(2)}, u32[]{:S(2)}) %collective-permute-start.20) | collective-permute-done | bytes 294944 | tf_op jit(solution)/shard_map/ppermute | solution.py:129
  86.4 0.9 %add_convert_fusion = bf16[128,1152]{1,0:T(8,128)(2,1)} fusion(bf16[128,1152]{1,0:T(8,128)(2,1)S(1)} %collective-permute-done.12, bf16[128,1152]{1,0:T(8,128)(2,1)S(1)} %collective-permute-done.20, bf16[128,1152]{1,0:T(8,128)(2,1)S(1)} %collective-permute-done.19, bf16[128,1152]{1,0:T(8,128)(2,1)S(1)} %collective-permute-done.14, ...), kind=kLoop, calls=%fused_computation.1 | loop fusion | flops 1474560 | bytes 1769472 | tf_op jit(solution)/shard_map/convert_element_type | solution.py:578
  88.2 0.9 convolution_convert_fusion
  (69 shorter events, 4.2 us)
Async XLA Ops:
  0.6 4.8 %collective-permute-start.2 = (bf16[128,1152]{1,0:T(8,128)(2,1)}, bf16[128,1152]{1,0:T(8,128)(2,1)S(1)}, u32[]{:S(2)}, u32[]{:S(2)}) collective-permute-start(bf16[128,1152]{1,0:T(8,128)(2,1)} %refs_0_.1), channel_id=1, source_target_pairs={{0,1},{1,0},{2,3},{3,2},{4,5},{5,4},{6,7},{7,6},{8,9},{9,8},{10,11... | collective-permute-start | bytes 884744 | tf_op jit(solution)/shard_map/ppermute | solution.py:129
  1.1 10.4 %collective-permute-start = (bf16[128,1152]{1,0:T(8,128)(2,1)}, bf16[128,1152]{1,0:T(8,128)(2,1)S(1)}, u32[]{:S(2)}, u32[]{:S(2)}) collective-permute-start(bf16[128,1152]{1,0:T(8,128)(2,1)} %refs_0_.1), channel_id=1, source_target_pairs={{0,2},{1,3},{2,0},{3,1},{4,6},{5,7},{6,4},{7,5},{8,10},{9,11},{10,... | collective-permute-start | bytes 884744 | tf_op jit(solution)/shard_map/ppermute | solution.py:129
  3.7 9.3 %collective-permute-start.1 = (bf16[128,1152]{1,0:T(8,128)(2,1)}, bf16[128,1152]{1,0:T(8,128)(2,1)S(1)}, u32[]{:S(2)}, u32[]{:S(2)}) collective-permute-start(bf16[128,1152]{1,0:T(8,128)(2,1)} %refs_0_.1), channel_id=1, source_target_pairs={{0,4},{1,5},{2,6},{3,7},{4,0},{5,1},{6,2},{7,3},{8,12},{9,13},{10,... | collective-permute-start | bytes 884744 | tf_op jit(solution)/shard_map/ppermute | solution.py:129
  13.0 2.2 %collective-permute-start.4 = (bf16[128,1152]{1,0:T(8,128)(2,1)S(1)}, bf16[128,1152]{1,0:T(8,128)(2,1)S(1)}, u32[]{:S(2)}, u32[]{:S(2)}) collective-permute-start(bf16[128,1152]{1,0:T(8,128)(2,1)S(1)} %collective-permute-done.refs_0_), channel_id=1, source_target_pairs={{0,1},{1,0},{2,3},{3,2},{4,5},{5,4},{6,7},{7,6},{8,9},{9,8},{10,11... | collective-permute-start | bytes 884744 | tf_op jit(solution)/shard_map/ppermute | solution.py:129
  13.0 2.2 %collective-permute-start.5 = (bf16[128,1152]{1,0:T(8,128)(2,1)S(1)}, bf16[128,1152]{1,0:T(8,128)(2,1)S(1)}, u32[]{:S(2)}, u32[]{:S(2)}) collective-permute-start(bf16[128,1152]{1,0:T(8,128)(2,1)S(1)} %collective-permute-done.1.refs_1_), channel_id=1, source_target_pairs={{0,1},{1,0},{2,3},{3,2},{4,5},{5,4},{6,7},{7,6},{8,9},{9,8},{10,11... | collective-permute-start | bytes 884744 | tf_op jit(solution)/shard_map/ppermute | solution.py:129
  13.7 11.0 %copy-start.1 = (s32[4]{0:T(128)S(1)}, s32[4]{0:T(128)}, u32[]{:S(2)}) copy-start(s32[4]{0:T(128)} %param.10) | copy-start | bytes 52
  13.7 10.9 %collective-permute-start.3 = (bf16[128,1152]{1,0:T(8,128)(2,1)}, bf16[128,1152]{1,0:T(8,128)(2,1)S(1)}, u32[]{:S(2)}, u32[]{:S(2)}) collective-permute-start(bf16[128,1152]{1,0:T(8,128)(2,1)} %refs_0_.1), channel_id=1, source_target_pairs={{0,6},{1,7},{2,4},{3,5},{4,2},{5,3},{6,0},{7,1},{8,14},{9,15},{10,... | collective-permute-start | bytes 884744 | tf_op jit(solution)/shard_map/ppermute | solution.py:129
  24.7 2.2 %collective-permute-start.6 = (bf16[128,1152]{1,0:T(8,128)(2,1)S(1)}, bf16[128,1152]{1,0:T(8,128)(2,1)S(1)}, u32[]{:S(2)}, u32[]{:S(2)}) collective-permute-start(bf16[128,1152]{1,0:T(8,128)(2,1)S(1)} %collective-permute-done.3.refs_0_), channel_id=1, source_target_pairs={{0,1},{1,0},{2,3},{3,2},{4,5},{5,4},{6,7},{7,6},{8,9},{9,8},{10,11... | collective-permute-start | bytes 884744 | tf_op jit(solution)/shard_map/ppermute | solution.py:129
  24.8 2.0 %copy-start = (s32[128]{0:T(128)S(1)}, s32[128]{0:T(128)}, u32[]{:S(2)}) copy-start(s32[128]{0:T(128)} %param.9) | copy-start | bytes 1540
  27.5 8.0 %collective-permute-start.7 = (bf16[64,384]{1,0:T(8,128)(2,1)S(1)}, bf16[64,384]{1,0:T(8,128)(2,1)S(1)}, u32[]{:S(2)}, u32[]{:S(2)}) collective-permute-start(bf16[64,384]{1,0:T(8,128)(2,1)S(1)} %get-tuple-element.70), channel_id=1, source_target_pairs={{0,8},{1,9},{2,10},{3,11},{4,12},{5,13},{6,14},{7,15},{8,0},{9,1},... | collective-permute-start | bytes 147464 | tf_op jit(solution)/shard_map/ppermute | solution.py:129
  36.0 15.4 %collective-permute-start.8 = (bf16[66,16,128]{2,1,0:T(8,128)(2,1)S(1)}, bf16[66,16,128]{2,1,0:T(8,128)(2,1)S(1)}, u32[]{:S(2)}, u32[]{:S(2)}) collective-permute-start(bf16[66,16,128]{2,1,0:T(8,128)(2,1)S(1)} %get-tuple-element.73), channel_id=1, source_target_pairs={{0,8},{1,9},{2,10},{3,11},{4,12},{5,13},{6,14},{7,15},{8,0},{9,1},... | collective-permute-start | bytes 811016 | tf_op jit(solution)/shard_map/ppermute | solution.py:129
  56.4 3.5 %collective-permute-start.9 = (bf16[128,1152]{1,0:T(8,128)(2,1)S(1)}, bf16[128,1152]{1,0:T(8,128)(2,1)S(1)}, u32[]{:S(2)}, u32[]{:S(2)}) collective-permute-start(bf16[128,1152]{1,0:T(8,128)(2,1)S(1)} %get-tuple-element.80), channel_id=1, source_target_pairs={{0,1},{1,0},{2,3},{3,2},{4,5},{5,4},{6,7},{7,6},{8,9},{9,8},{10,11... | collective-permute-start | bytes 884744 | tf_op jit(solution)/shard_map/ppermute | solution.py:129
  60.0 4.4 %collective-permute-start.10 = (bf16[128,1152]{1,0:T(8,128)(2,1)S(1)}, bf16[128,1152]{1,0:T(8,128)(2,1)S(1)}, u32[]{:S(2)}, u32[]{:S(2)}) collective-permute-start(bf16[128,1152]{1,0:T(8,128)(2,1)S(1)} %get-tuple-element.85), channel_id=1, source_target_pairs={{0,1},{1,0},{2,3},{3,2},{4,5},{5,4},{6,7},{7,6},{8,9},{9,8},{10,11... | collective-permute-start | bytes 884744 | tf_op jit(solution)/shard_map/ppermute | solution.py:129
  60.7 9.9 %collective-permute-start.12 = (bf16[128,1152]{1,0:T(8,128)(2,1)S(1)}, bf16[128,1152]{1,0:T(8,128)(2,1)S(1)}, u32[]{:S(2)}, u32[]{:S(2)}) collective-permute-start(bf16[128,1152]{1,0:T(8,128)(2,1)S(1)} %add_convert_fusion.3), channel_id=1, source_target_pairs={{0,6},{1,7},{2,4},{3,5},{4,2},{5,3},{6,0},{7,1},{8,14},{9,15},{10,... | collective-permute-start | bytes 884744 | tf_op jit(solution)/shard_map/ppermute | solution.py:129
  61.0 15.0 %copy-start.2 = (s32[4]{0:T(128)S(1)}, s32[4]{0:T(128)}, u32[]{:S(2)}) copy-start(s32[4]{0:T(128)} %param.11) | copy-start | bytes 52
  64.5 6.1 %collective-permute-start.11 = (bf16[128,1152]{1,0:T(8,128)(2,1)S(1)}, bf16[128,1152]{1,0:T(8,128)(2,1)S(1)}, u32[]{:S(2)}, u32[]{:S(2)}) collective-permute-start(bf16[128,1152]{1,0:T(8,128)(2,1)S(1)} %get-tuple-element.92), channel_id=1, source_target_pairs={{0,1},{1,0},{2,3},{3,2},{4,5},{5,4},{6,7},{7,6},{8,9},{9,8},{10,11... | collective-permute-start | bytes 884744 | tf_op jit(solution)/shard_map/ppermute | solution.py:129
  70.6 1.3 %collective-permute-start.13 = (bf16[4,4,1152]{2,1,0:T(4,128)(2,1)S(1)}, bf16[4,4,1152]{2,1,0:T(4,128)(2,1)S(1)}, u32[]{:S(2)}, u32[]{:S(2)}) collective-permute-start(bf16[4,4,1152]{2,1,0:T(4,128)(2,1)S(1)} %slice.112), channel_id=1, source_target_pairs={{0,1},{1,0},{2,3},{3,2},{4,5},{5,4},{6,7},{7,6},{8,9},{9,8},{10,11... | collective-permute-start | bytes 110600 | tf_op jit(solution)/shard_map/ppermute | solution.py:129
  70.7 1.7 %collective-permute-start.14 = (bf16[128,1152]{1,0:T(8,128)(2,1)S(1)}, bf16[128,1152]{1,0:T(8,128)(2,1)S(1)}, u32[]{:S(2)}, u32[]{:S(2)}) collective-permute-start(bf16[128,1152]{1,0:T(8,128)(2,1)S(1)} %get-tuple-element.106), channel_id=1, source_target_pairs={{0,1},{1,0},{2,3},{3,2},{4,5},{5,4},{6,7},{7,6},{8,9},{9,8},{10,11... | collective-permute-start | bytes 884744 | tf_op jit(solution)/shard_map/ppermute | solution.py:129
  72.4 5.0 %collective-permute-start.15 = (bf16[4,4,1152]{2,1,0:T(4,128)(2,1)S(1)}, bf16[4,4,1152]{2,1,0:T(4,128)(2,1)S(1)}, u32[]{:S(2)}, u32[]{:S(2)}) collective-permute-start(bf16[4,4,1152]{2,1,0:T(4,128)(2,1)S(1)} %convert_element_type.96), channel_id=1, source_target_pairs={{0,2},{1,3},{2,0},{3,1},{4,6},{5,7},{6,4},{7,5},{8,10},{9,11},{10,... | collective-permute-start | bytes 110600 | tf_op jit(solution)/shard_map/ppermute | solution.py:129
  73.9 4.0 %collective-permute-start.16 = (bf16[4,4,1152]{2,1,0:T(4,128)(2,1)S(1)}, bf16[4,4,1152]{2,1,0:T(4,128)(2,1)S(1)}, u32[]{:S(2)}, u32[]{:S(2)}) collective-permute-start(bf16[4,4,1152]{2,1,0:T(4,128)(2,1)S(1)} %convert_element_type.96), channel_id=1, source_target_pairs={{0,4},{1,5},{2,6},{3,7},{4,0},{5,1},{6,2},{7,3},{8,12},{9,13},{10,... | collective-permute-start | bytes 110600 | tf_op jit(solution)/shard_map/ppermute | solution.py:129
  73.9 5.0 %collective-permute-start.17 = (bf16[4,4,1152]{2,1,0:T(4,128)(2,1)S(1)}, bf16[4,4,1152]{2,1,0:T(4,128)(2,1)S(1)}, u32[]{:S(2)}, u32[]{:S(2)}) collective-permute-start(bf16[4,4,1152]{2,1,0:T(4,128)(2,1)S(1)} %convert_element_type.96), channel_id=1, source_target_pairs={{0,6},{1,7},{2,4},{3,5},{4,2},{5,3},{6,0},{7,1},{8,14},{9,15},{10,... | collective-permute-start | bytes 110600 | tf_op jit(solution)/shard_map/ppermute | solution.py:129
  76.0 8.9 %collective-permute-start.19 = (bf16[128,1152]{1,0:T(8,128)(2,1)S(1)}, bf16[128,1152]{1,0:T(8,128)(2,1)S(1)}, u32[]{:S(2)}, u32[]{:S(2)}) collective-permute-start(bf16[128,1152]{1,0:T(8,128)(2,1)S(1)} %add_convert_fusion.2), channel_id=1, source_target_pairs={{0,2},{1,3},{2,0},{3,1},{4,6},{5,7},{6,4},{7,5},{8,10},{9,11},{10,... | collective-permute-start | bytes 884744 | tf_op jit(solution)/shard_map/ppermute | solution.py:129
  77.4 8.9 %collective-permute-start.20 = (bf16[128,1152]{1,0:T(8,128)(2,1)S(1)}, bf16[128,1152]{1,0:T(8,128)(2,1)S(1)}, u32[]{:S(2)}, u32[]{:S(2)}) collective-permute-start(bf16[128,1152]{1,0:T(8,128)(2,1)S(1)} %add_convert_fusion.1), channel_id=1, source_target_pairs={{0,4},{1,5},{2,6},{3,7},{4,0},{5,1},{6,2},{7,3},{8,12},{9,13},{10,... | collective-permute-start | bytes 884744 | tf_op jit(solution)/shard_map/ppermute | solution.py:129
  79.0 5.6 %collective-permute-start.18 = (bf16[4,4,1152]{2,1,0:T(4,128)(2,1)S(1)}, bf16[4,4,1152]{2,1,0:T(4,128)(2,1)S(1)}, u32[]{:S(2)}, u32[]{:S(2)}) collective-permute-start(bf16[4,4,1152]{2,1,0:T(4,128)(2,1)S(1)} %pad_maximum_fusion.6), channel_id=1, source_target_pairs={{0,8},{1,9},{2,10},{3,11},{4,12},{5,13},{6,14},{7,15},{8,0},{9,1},... | collective-permute-start | bytes 110600 | tf_op jit(solution)/shard_map/ppermute | solution.py:129
  86.4 1.3 %collective-permute-start.21 = (bf16[2,4,4,1152]{3,2,1,0:T(4,128)(2,1)S(1)}, bf16[2,4,4,1152]{3,2,1,0:T(4,128)(2,1)S(1)}, u32[]{:S(2)}, u32[]{:S(2)}) collective-permute-start(bf16[2,4,4,1152]{3,2,1,0:T(4,128)(2,1)S(1)} %pad_maximum_fusion.5), channel_id=1, source_target_pairs={{0,1},{1,0},{2,3},{3,2},{4,5},{5,4},{6,7},{7,6},{8,9},{9,8},{10,11... | collective-permute-start | bytes 221192 | tf_op jit(solution)/shard_map/ppermute | solution.py:129

commit v4 on v3

--- a/solution.py
+++ b/solution.py
@@ -377,20 +377,12 @@
     )(block_ids, w_out)
 
 
-def mix_chip(attended, slab_ref, even_ref, odd_ref, end_ref):
-    tokens, end_rows = even_ref.shape[0], end_ref.shape[1]
+def mix_chip(attended, slab_ref, even_ref, odd_ref):
     for core, out_ref in enumerate((even_ref, odd_ref)):
-        part = contract_last(attended[...], slab_ref[core])
-        out_ref[...] = part[:tokens].astype(jnp.bfloat16)
-        end_ref[core] = part[tokens : tokens + end_rows]
-
-
-def chip_shapes(tokens, rows, end_rows):
-    part = jax.ShapeDtypeStruct((tokens, rows), jnp.bfloat16)
-    return [part, part, jax.ShapeDtypeStruct((2, end_rows, rows), jnp.float32)]
-
-
-def attend_and_mix(own_scores, partner_scores, own_kv, allowed, slabs, picker, end_rows):
+        out_ref[...] = contract_last(attended[...], slab_ref[core]).astype(jnp.bfloat16)
+
+
+def attend_and_mix(own_scores, partner_scores, own_kv, allowed, slabs, picker):
     heads, tokens = own_scores.shape[:2]
     blocks = tokens // ROW_TILE
     count, rows, columns = slabs.shape
@@ -398,7 +390,7 @@
 
     def kernel(
         own_ref, partner_ref, own_kv_ref, allowed_ref, slab_ref, picker_ref,
-        attended_ref, even_ref, odd_ref, end_ref,
+        attended_ref, even_ref, odd_ref,
     ):
         mask = allowed_ref[...] > 0.0
         first_tile = heads // 2 * (blocks + 1)
@@ -426,14 +418,15 @@
         attended_ref[tokens:] = jnp.dot(
             picker_ref[...], attended_ref[:tokens], preferred_element_type=jnp.float32
         ).astype(jnp.bfloat16)
-        mix_chip(attended_ref, slab_ref, even_ref, odd_ref, end_ref)
-
+        mix_chip(attended_ref, slab_ref, even_ref, odd_ref)
+
+    out_rows = tokens + picker.shape[0]
     return pl.pallas_call(
         kernel,
         in_specs=[vmem()] * 6,
-        out_specs=[vmem()] * 4,
-        out_shape=[jax.ShapeDtypeStruct((tokens + picker.shape[0], columns), jnp.bfloat16)]
-        + chip_shapes(tokens, rows, end_rows),
+        out_specs=[vmem()] * 3,
+        out_shape=[jax.ShapeDtypeStruct((out_rows, columns), jnp.bfloat16)]
+        + [jax.ShapeDtypeStruct((out_rows, rows), jnp.bfloat16)] * 2,
         compiler_params=pltpu.CompilerParams(vmem_limit_bytes=8 * MIB),
         cost_estimate=pl.CostEstimate(
             flops=4 * tokens * rows * columns,
@@ -444,45 +437,59 @@
     )(own_scores, partner_scores, own_kv, allowed, slabs, picker)
 
 
-def mix(attended, slabs, tokens, end_rows):
-    rows, columns = slabs.shape[1:]
-
-    def kernel(attended_ref, slab_ref, even_ref, odd_ref, end_ref):
-        mix_chip(attended_ref, slab_ref, even_ref, odd_ref, end_ref)
+def mix(attended, slabs):
+    out_rows = attended.shape[0]
+    rows = slabs.shape[1]
+
+    def kernel(attended_ref, slab_ref, even_ref, odd_ref):
+        mix_chip(attended_ref, slab_ref, even_ref, odd_ref)
 
     return pl.pallas_call(
         kernel,
         in_specs=[vmem()] * 2,
-        out_specs=[vmem()] * 3,
-        out_shape=chip_shapes(tokens, rows, end_rows),
+        out_specs=[vmem()] * 2,
+        out_shape=[jax.ShapeDtypeStruct((out_rows, rows), jnp.bfloat16)] * 2,
         compiler_params=pltpu.CompilerParams(vmem_limit_bytes=8 * MIB),
-        cost_estimate=pl.CostEstimate(flops=tokens * rows, bytes_accessed=rows, transcendentals=0),
+        cost_estimate=pl.CostEstimate(flops=out_rows * rows, bytes_accessed=rows, transcendentals=0),
         name="mix",
     )(attended, slabs)
 
 
+def place_rewards(chooser, positions, blocks):
+    slots = SLOTS
+    places = chooser.shape[0] // slots
+    features = blocks[0].shape[1]
+
+    def kernel(chooser_ref, position_ref, *refs):
+        out_ref = refs[-1]
+        for i, block_ref in enumerate(refs[:-1]):
+            chosen = jnp.dot(chooser_ref[...], block_ref[...], preferred_element_type=jnp.float32)
+            for place in range(places):
+                lanes = pl.ds(pl.multiple_of(position_ref[i * places + place] * features, LANES), features)
+                out_ref[:, lanes] = chosen[place * slots : (place + 1) * slots].astype(jnp.bfloat16)
+
+    return pl.pallas_call(
+        kernel,
+        in_specs=[vmem(), smem()] + [vmem()] * len(blocks),
+        out_specs=vmem(),
+        out_shape=jax.ShapeDtypeStruct((slots, len(blocks) * places * features), jnp.bfloat16),
+        compiler_params=pltpu.CompilerParams(vmem_limit_bytes=8 * MIB),
+        name="place_rewards",
+    )(chooser, positions, *blocks)
+
+
+def swap_groups(rows, groups, distance):
+    size = rows.shape[0] // groups
+    return jnp.concatenate([rows[(j ^ distance) * size : ((j ^ distance) + 1) * size] for j in range(groups)], 0)
+
+
 def add_rounded(left, right):
     return (left.astype(jnp.float32) + right.astype(jnp.float32)).astype(jnp.bfloat16)
-
-
-def swap_blocks(blocks, distance):
-    return [blocks[j ^ distance] for j in range(len(blocks))]
-
-
-def natural_order(blocks, my_group):
-    distance = 1
-    while distance < len(blocks):
-        bit = (my_group & distance) != 0
-        swapped = swap_blocks(blocks, distance)
-        blocks = [jnp.where(bit, other, own) for own, other in zip(blocks, swapped)]
-        distance *= 2
-    return jnp.concatenate(blocks, axis=-1)
 
 
 def pair_device(hidden, w_qkv, w_out, segment_ids, end_positions, owners):
     my_index = lax.axis_index("gx")
     my_group = my_index % KVG
-    my_block = my_index // KVG
     tokens = hidden.shape[0]
     query_width = HPG * HD
     together = lax.optimization_barrier
@@ -514,7 +521,6 @@
     allowed = (
         (segment_ids[:, None] == segment_ids[None, :]) & (positions[None, :] <= positions[:, None])
     ).astype(jnp.float32)
-    end_rows = -(-completions // 8) * 8
     picked_rows = -(-completions // ROW_TILE) * ROW_TILE
     picker = (
         jnp.pad(end_positions, (0, picked_rows - completions), constant_values=-1)[:, None] == positions[None, :]
@@ -530,50 +536,47 @@
     arrived = xor_swap(packed, KVG)
     own_slabs, slabs_y, slabs_z, slabs_both = fetch_rows(block_ids, w_out, KVG)
     arrived, slabs_both = together((arrived, slabs_both))
-    attended, even_both, odd_both, ends_both = attend_and_mix(
-        scores, arrived, own_kv, allowed, slabs_both, picker, end_rows
-    )
+    attended, even_both, odd_both = attend_and_mix(scores, arrived, own_kv, allowed, slabs_both, picker)
     odd_both = xor_swap(odd_both, 1)
-    even_y, odd_y, ends_y = mix(attended, slabs_y, tokens, end_rows)
+    even_y, odd_y = mix(attended, slabs_y)
     odd_both, even_y, odd_y = together((odd_both, even_y, odd_y))
     odd_y = xor_swap(odd_y, 1)
-    near_both, attended = together((add_rounded(even_both, odd_both), attended))
+    near_both, attended = together((add_rounded(even_both[:tokens], odd_both[:tokens]), attended))
     sum_both = xor_swap(near_both, 6)
-    even_z, odd_z, ends_z = mix(attended, slabs_z, tokens, end_rows)
+    even_z, odd_z = mix(attended, slabs_z)
     odd_y, even_z, odd_z = together((odd_y, even_z, odd_z))
     odd_z = xor_swap(odd_z, 1)
-    near_y, attended = together((add_rounded(even_y, odd_y), attended))
-    even_own, odd_own, ends_own = mix(attended, own_slabs, tokens, end_rows)
-    odd_z, even_own, odd_own, ends_own, sum_both = together((odd_z, even_own, odd_own, ends_own, sum_both))
-    near_z = add_rounded(even_z, odd_z)
-
-    end_parts = jnp.concatenate([ends_own, ends_y, ends_z, ends_both])[:, :completions]
-    end_far = xor_swap(end_parts[1::2].astype(jnp.bfloat16), 1)
-    ends = end_parts[0::2] + end_far.astype(jnp.float32)
-    ends, odd_own, near_y, near_z = together((ends, xor_swap(odd_own, 1), near_y, near_z))
+    near_y, attended = together((add_rounded(even_y[:tokens], odd_y[:tokens]), attended))
+    even_own, odd_own = mix(attended, own_slabs)
+    odd_z, even_own, odd_own = together((odd_z, even_own, odd_own))
+    odd_own = xor_swap(odd_own, 1)
+    near_z = add_rounded(even_z[:tokens], odd_z[:tokens])
+
+    ends = jnp.concatenate(
+        [
+            even[tokens : tokens + completions].astype(jnp.float32)
+            + odd[tokens : tokens + completions].astype(jnp.float32)
+            for even, odd in ((even_own, odd_own), (even_y, odd_y), (even_z, odd_z), (even_both, odd_both))
+        ]
+    )
+    ends, near_y, near_z, sum_both = together((ends, near_y, near_z, sum_both))
     message = ends.astype(jnp.bfloat16)
-    ends = [ends[i] for i in range(KVG // 2)]
     for distance in range(2, KVG, 2):
         got = xor_swap(message, distance).astype(jnp.float32)
-        ends = [ends[i] + got[i ^ distance // 2] for i in range(KVG // 2)]
-    sum_y, sum_z = xor_swap(near_y, 2), xor_swap(near_z, 4)
-    ends = jnp.stack(ends).astype(jnp.bfloat16)
-    both = jnp.stack([ends, xor_swap(ends, KVG)])
-    both, sum_y, sum_z = together((both, sum_y, sum_z))
+        ends += swap_groups(got, KVG // 2, distance // 2)
+    sum_z, sum_y = xor_swap(near_z, 4), xor_swap(near_y, 2)
+    ends = ends.astype(jnp.bfloat16)
+    other_ends = xor_swap(ends, KVG)
+    both, sum_z, sum_y = together((jnp.concatenate([ends, other_ends]), sum_z, sum_y))
     both_far = xor_swap(both, 1)
-    halves = []
-    for half in range(2):
-        blocks = []
-        for i in range(KVG // 2):
-            blocks += [both[half, i], both_far[half, i]]
-        halves.append(natural_order(blocks, my_group))
-    end_full = jnp.concatenate(
-        [jnp.where(my_block == 0, halves[0], halves[1]), jnp.where(my_block == 0, halves[1], halves[0])], axis=-1
-    )
-    reward_rows = jnp.dot(chooser, end_full, preferred_element_type=jnp.float32).astype(jnp.bfloat16)
-
-    mixed = even_own.astype(jnp.float32)
-    for part in (odd_own, sum_y, sum_z, sum_both):
+    chips = 2 * jnp.arange(KVG // 2, dtype=jnp.int32)
+    halves = KVG * jnp.arange(2, dtype=jnp.int32)
+    distances = (halves[:, None] + chips[None, :]).reshape(-1)
+    places = my_index ^ jnp.concatenate([distances, distances + 1])
+    reward_rows = place_rewards(jnp.kron(jnp.eye(KVG, dtype=jnp.bfloat16), chooser), places.astype(jnp.int32), [both, both_far])
+
+    mixed = even_own[:tokens].astype(jnp.float32)
+    for part in (odd_own[:tokens], sum_y, sum_z, sum_both):
         mixed += part.astype(jnp.float32)
     return (mixed.astype(jnp.bfloat16), reward_rows)
 

time: 89.2 us -> 87.3 us (0.979)
  waiting for transfers between devices: 13.1 us -> 7.8 us
  starting transfers between devices: 18.5 us -> 20.2 us
  Pallas kernels: 53.2 us -> 54.5 us
  other arithmetic: 2.41 us -> 3.48 us
    ppermute x22 -> x21, waiting for transfers between devices: 13.1 us -> 7.8 us  [xor_swap(): lax.ppermute(block, 'gx', [(low, low ^ distance) for low in range(count)])]
    ppermute x22 -> x21, starting transfers between devices: 18.5 us -> 20.2 us  [xor_swap(): lax.ppermute(block, 'gx', [(low, low ^ distance) for low in range(count)])]
    pallas_call x4 -> x5, Pallas kernels: 15.5 us -> 16.8 us  [the longest x3 10.4 us: mix(): pl.pallas_call(kernel, in_specs=[vmem()] * 2, out_specs=[vmem()] * 2, out...]
  transfers between devices with their start and end apart: 22 -> 21, of which waited for: 11 -> 10; matrix products, arithmetic and copies ran while one was open for 2% -> 4% of each run, Pallas kernels for 53% -> 54%
where the time goes in v4:
time: 87.3 us; the launch traced here: 87.2 us
  Pallas kernels  54.5 us (62%)
  starting transfers between devices  20.2 us (23%)
  waiting for transfers between devices  7.8 us (9%)
  other arithmetic  3.48 us (4%)
  between operations  0.9 us (1%)
    pallas_call x3, Pallas kernels, project(): pl.pallas_call(kernel, in_specs=[smem()] + [vmem()] * count + [anywhere()...  20.9 us
    ppermute x21, starting transfers between devices, xor_swap(): lax.ppermute(block, 'gx', [(low, low ^ distance) for low in range(count)])  20.2 us
    pallas_call x1, Pallas kernels, fetch_rows(): pl.pallas_call(kernel, in_specs=[smem(), anywhere()], out_specs=[vmem()]...  13.8 us
    pallas_call x3, Pallas kernels, mix(): pl.pallas_call(kernel, in_specs=[vmem()] * 2, out_specs=[vmem()] * 2, out...  10.4 us
    ppermute x21, waiting for transfers between devices, xor_swap(): lax.ppermute(block, 'gx', [(low, low ^ distance) for low in range(count)])  7.8 us
    pallas_call x1, Pallas kernels, attend_and_mix(): pl.pallas_call(kernel, in_specs=[vmem()] * 6, out_specs=[vmem()] * 3, out...  5.13 us
    pallas_call x1, Pallas kernels, fetch_kv(): pl.pallas_call(kernel, in_specs=[smem(), anywhere()], out_specs=vmem(), o...  2.02 us
  transfers between devices with their start and end apart: 21, of which 10 were waited for; matrix products, arithmetic and copies ran while one was open for 4% of the time, Pallas kernels for 54%

profile of v4, /device:TPU:0, one launch (start us, length us, event | category | flops | bytes accessed | tf_op | source)
XLA Modules:
  0.0 87.2 jit_solution(17094766210045823014)
XLA Ops:
  0.6 0.5 collective-permute-start.2
  1.1 2.6 %collective-permute-start = (bf16[128,1152]{1,0:T(8,128)(2,1)}, bf16[128,1152]{1,0:T(8,128)(2,1)S(1)}, u32[]{:S(2)}, u32[]{:S(2)}) collective-permute-start(bf16[128,1152]{1,0:T(8,128)(2,1)} %refs_0_.1), channel_id=1, source_target_pairs={{0,2},{1,3},{2,0},{3,1},{4,6},{5,7},{6,4},{7,5},{8,10},{9,11},{10,... | collective-permute-start | bytes 884744 | tf_op jit(solution)/shard_map/ppermute | solution.py:129
  3.7 1.6 %collective-permute-start.1 = (bf16[128,1152]{1,0:T(8,128)(2,1)}, bf16[128,1152]{1,0:T(8,128)(2,1)S(1)}, u32[]{:S(2)}, u32[]{:S(2)}) collective-permute-start(bf16[128,1152]{1,0:T(8,128)(2,1)} %refs_0_.1), channel_id=1, source_target_pairs={{0,4},{1,5},{2,6},{3,7},{4,0},{5,1},{6,2},{7,3},{8,12},{9,13},{10,... | collective-permute-start | bytes 884744 | tf_op jit(solution)/shard_map/ppermute | solution.py:129
  5.3 0.7 broadcast_compare_fusion
  6.3 0.9 %convert_reduce_fusion = s32[4]{0:T(128)S(1)} fusion(s32[4]{0:T(128)} %param.11), kind=kLoop, calls=%fused_computation.22 | loop fusion | flops 76 | bytes 32 | tf_op jit(solution)/shard_map/reduce_sum | solution.py:499
  7.2 6.2 %project.3.refs_5_ = f32[128,2688]{1,0:T(8,128)S(1)} custom-call(s32[2]{0:T(128)S(1)} %pad_add_fusion.1.ids_ref, bf16[128,1152]{1,0:T(8,128)(2,1)} %refs_0_.1, bf16[128,1152]{1,0:T(8,128)(2,1)S(1)} %collective-permute-done.2.refs_1_, bf16[9216,2688]{1,0:T(8,128)(2,1)} %refs_2_.3), custom_call_target="tpu_custom_call" | custom-call | flops 1585446912 | bytes 12386304 | tf_op jit(solution)/shard_map/project/pallas_call | solution.py:192
  14.1 1.1 %collective-permute-start.3 = (bf16[128,1152]{1,0:T(8,128)(2,1)}, bf16[128,1152]{1,0:T(8,128)(2,1)S(1)}, u32[]{:S(2)}, u32[]{:S(2)}) collective-permute-start(bf16[128,1152]{1,0:T(8,128)(2,1)} %refs_0_.1), channel_id=1, source_target_pairs={{0,6},{1,7},{2,4},{3,5},{4,2},{5,3},{6,0},{7,1},{8,14},{9,15},{10,... | collective-permute-start | bytes 884744 | tf_op jit(solution)/shard_map/ppermute | solution.py:129
  15.5 9.3 %project.4.refs_2_.refs_3_ = f32[128,2688]{1,0:T(8,128)S(1)} custom-call(s32[4]{0:T(128)S(1)} %pad_add_fusion.2.ids_ref, bf16[128,1152]{1,0:T(8,128)(2,1)S(1)} %collective-permute-done.refs_0_, bf16[128,1152]{1,0:T(8,128)(2,1)S(1)} %collective-permute-done.1.refs_1_, bf16[128,1152]{1,0:T(8,128)(2,1)S(1)} %collective-permute-done.4.refs_2_, ...), custom_call_target="tpu_custom_call" | custom-call | flops 3170893824 | bytes 24772608 | tf_op jit(solution)/shard_map/project/pallas_call | solution.py:192
  25.2 2.0 %fetch_kv.1.refs_3_ = bf16[2,1152,384]{2,1,0:T(8,128)(2,1)S(1)} custom-call(s32[2]{0:T(128)S(1)} %slice.85.ids_ref, bf16[9216,2688]{1,0:T(8,128)(2,1)} %refs_2_.3), custom_call_target="tpu_custom_call" | custom-call | flops 1152 | bytes 884736 | tf_op jit(solution)/shard_map/fetch_kv/pallas_call | solution.py:238
  27.3 0.5 finish_kv.1
  27.9 2.7 %collective-permute-start.7 = (bf16[64,384]{1,0:T(8,128)(2,1)S(1)}, bf16[64,384]{1,0:T(8,128)(2,1)S(1)}, u32[]{:S(2)}, u32[]{:S(2)}) collective-permute-start(bf16[64,384]{1,0:T(8,128)(2,1)S(1)} %get-tuple-element.64), channel_id=1, source_target_pairs={{0,8},{1,9},{2,10},{3,11},{4,12},{5,13},{6,14},{7,15},{8,0},{9,1},... | collective-permute-start | bytes 147464 | tf_op jit(solution)/shard_map/ppermute | solution.py:129
  30.5 5.3 %project.5.query_ref = f32[128,2304]{1,0:T(8,128)S(1)} custom-call(s32[2]{0:T(128)S(1)} %pad_add_fusion.ids_ref, bf16[128,1152]{1,0:T(8,128)(2,1)S(1)} %collective-permute-done.3.refs_0_, bf16[128,1152]{1,0:T(8,128)(2,1)S(1)} %collective-permute-done.6.refs_1_, bf16[9216,2688]{1,0:T(8,128)(2,1)} %refs_2_.3, f32[128,2688]{1,0:T(8,128)S(1)} %project.4.refs_2_.refs_3_), custom_call_target="tpu_custom_call" | custom-call | flops 1358954496 | bytes 10616832 | tf_op jit(solution)/shard_map/project/pallas_call | solution.py:192
  36.8 13.8 %fetch_rows.1 = (bf16[2,1152,2304]{2,1,0:T(8,128)(2,1)S(1)}, bf16[2,1152,2304]{2,1,0:T(8,128)(2,1)S(1)}, bf16[2,1152,2304]{2,1,0:T(8,128)(2,1)S(1)}, bf16[2,1152,2304]{2,1,0:T(8,128)(2,1)S(1)}) custom-call(s32[8]{0:T(128)S(1)} %iota_xor_fusion.ids_ref, bf16[9216,2304]{1,0:T(8,128)(2,1)} %w_ref.3), custom_call_target="tpu_custom_call" | custom-call | flops 5435817984 | bytes 42467328 | tf_op jit(solution)/shard_map/fetch_rows/pallas_call | solution.py:366
  50.6 1.1 %collective-permute-done.8.partner_ref = bf16[66,16,128]{2,1,0:T(8,128)(2,1)S(1)} collective-permute-done((bf16[66,16,128]{2,1,0:T(8,128)(2,1)S(1)}, bf16[66,16,128]{2,1,0:T(8,128)(2,1)S(1)}, u32[]{:S(2)}, u32[]{:S(2)}) %collective-permute-start.8) | collective-permute-done | bytes 270368 | tf_op jit(solution)/shard_map/ppermute | solution.py:129
  51.6 5.1 %attend_and_mix.1 = (bf16[144,2304]{1,0:T(8,128)(2,1)S(1)}, bf16[144,1152]{1,0:T(8,128)(2,1)S(1)}, bf16[144,1152]{1,0:T(8,128)(2,1)S(1)}) custom-call(f32[12,128,128]{2,1,0:T(8,128)S(1)} %get-tuple-element.65.own_ref, bf16[66,16,128]{2,1,0:T(8,128)(2,1)S(1)} %collective-permute-done.8.partner_ref, f32[128,384]{1,0:T(8,128)S(1)} %get-tuple-element.63.own_ref.own_kv_ref, ...), custom_call_target="tpu_custom_call" | custom-call | flops 1358954496 | bytes 10616832 | tf_op jit(solution)/shard_map/attend_and_mix/pallas_call | solution.py:424
  56.9 3.5 %mix.3 = (bf16[144,1152]{1,0:T(8,128)(2,1)S(1)}, bf16[144,1152]{1,0:T(8,128)(2,1)S(1)}) custom-call(bf16[144,2304]{1,0:T(8,128)(2,1)S(1)} %get-tuple-element.89.attended_ref, bf16[2,1152,2304]{2,1,0:T(8,128)(2,1)S(1)} %get-tuple-element.76.slab_ref), custom_call_target="tpu_custom_call" | custom-call | flops 165888 | bytes 1152 | tf_op jit(solution)/shard_map/mix/pallas_call | solution.py:447
  60.5 0.6 collective-permute-start.10
  61.1 0.8 collective-permute-start.13
  61.9 3.5 %mix.4 = (bf16[144,1152]{1,0:T(8,128)(2,1)S(1)}, bf16[144,1152]{1,0:T(8,128)(2,1)S(1)}) custom-call(bf16[144,2304]{1,0:T(8,128)(2,1)S(1)} %get-tuple-element.89.attended_ref, bf16[2,1152,2304]{2,1,0:T(8,128)(2,1)S(1)} %get-tuple-element.83.slab_ref), custom_call_target="tpu_custom_call" | custom-call | flops 165888 | bytes 1152 | tf_op jit(solution)/shard_map/mix/pallas_call | solution.py:447
  65.5 3.5 %mix.5 = (bf16[144,1152]{1,0:T(8,128)(2,1)S(1)}, bf16[144,1152]{1,0:T(8,128)(2,1)S(1)}) custom-call(bf16[144,2304]{1,0:T(8,128)(2,1)S(1)} %get-tuple-element.89.attended_ref, bf16[2,1152,2304]{2,1,0:T(8,128)(2,1)S(1)} %get-tuple-element.90.slab_ref), custom_call_target="tpu_custom_call" | custom-call | flops 165888 | bytes 1152 | tf_op jit(solution)/shard_map/mix/pallas_call | solution.py:447
  69.0 0.6 collective-permute-start.12
  69.7 1.2 %collective-permute-done.12 = bf16[144,1152]{1,0:T(8,128)(2,1)S(1)} collective-permute-done((bf16[144,1152]{1,0:T(8,128)(2,1)S(1)}, bf16[144,1152]{1,0:T(8,128)(2,1)S(1)}, u32[]{:S(2)}, u32[]{:S(2)}) %collective-permute-start.12) | collective-permute-done | bytes 331808 | tf_op jit(solution)/shard_map/ppermute | solution.py:129
  71.0 2.2 %collective-permute-start.16 = (bf16[16,1152]{1,0:T(8,128)(2,1)S(1)}, bf16[16,1152]{1,0:T(8,128)(2,1)S(1)}, u32[]{:S(2)}, u32[]{:S(2)}) collective-permute-start(bf16[16,1152]{1,0:T(8,128)(2,1)S(1)} %convert_element_type.128), channel_id=1, source_target_pairs={{0,6},{1,7},{2,4},{3,5},{4,2},{5,3},{6,0},{7,1},{8,14},{9,15},{10,... | collective-permute-start | bytes 110600 | tf_op jit(solution)/shard_map/ppermute | solution.py:129
  73.1 0.6 collective-permute-start.15
  73.7 0.8 collective-permute-start.14
  74.5 1.9 %collective-permute-start.18 = (bf16[128,1152]{1,0:T(8,128)(2,1)S(1)}, bf16[128,1152]{1,0:T(8,128)(2,1)S(1)}, u32[]{:S(2)}, u32[]{:S(2)}) collective-permute-start(bf16[128,1152]{1,0:T(8,128)(2,1)S(1)} %add_convert_fusion.1), channel_id=1, source_target_pairs={{0,4},{1,5},{2,6},{3,7},{4,0},{5,1},{6,2},{7,3},{8,12},{9,13},{10,... | collective-permute-start | bytes 884744 | tf_op jit(solution)/shard_map/ppermute | solution.py:129
  76.4 0.7 collective-permute-start.19
  77.7 2.3 %collective-permute-start.17 = (bf16[16,1152]{1,0:T(8,128)(2,1)S(1)}, bf16[16,1152]{1,0:T(8,128)(2,1)S(1)}, u32[]{:S(2)}, u32[]{:S(2)}) collective-permute-start(bf16[16,1152]{1,0:T(8,128)(2,1)S(1)} %fusion.2), channel_id=1, source_target_pairs={{0,8},{1,9},{2,10},{3,11},{4,12},{5,13},{6,14},{7,15},{8,0},{9,1},... | collective-permute-start | bytes 110600 | tf_op jit(solution)/shard_map/ppermute | solution.py:129
  80.1 3.0 %collective-permute-done.17 = bf16[16,1152]{1,0:T(8,128)(2,1)S(1)} collective-permute-done((bf16[16,1152]{1,0:T(8,128)(2,1)S(1)}, bf16[16,1152]{1,0:T(8,128)(2,1)S(1)}, u32[]{:S(2)}, u32[]{:S(2)}) %collective-permute-start.17) | collective-permute-done | bytes 36896 | tf_op jit(solution)/shard_map/ppermute | solution.py:129
  83.1 1.0 %collective-permute-done.18 = bf16[128,1152]{1,0:T(8,128)(2,1)S(1)} collective-permute-done((bf16[128,1152]{1,0:T(8,128)(2,1)S(1)}, bf16[128,1152]{1,0:T(8,128)(2,1)S(1)}, u32[]{:S(2)}, u32[]{:S(2)}) %collective-permute-start.18) | collective-permute-done | bytes 294944 | tf_op jit(solution)/shard_map/ppermute | solution.py:129
  84.6 0.9 %add_convert_fusion = bf16[128,1152]{1,0:T(8,128)(2,1)} fusion(bf16[128,1152]{1,0:T(8,128)(2,1)S(1)} %collective-permute-done.13, bf16[128,1152]{1,0:T(8,128)(2,1)S(1)} %collective-permute-done.18, bf16[128,1152]{1,0:T(8,128)(2,1)S(1)} %collective-permute-done.19, bf16[144,1152]{1,0:T(8,128)(2,1)S(1)} %collective-permute-done.12, ...), kind=kLoop, calls=%fused_computation | loop fusion | flops 1474560 | bytes 1769472 | tf_op jit(solution)/shard_map/convert_element_type | solution.py:581
  85.8 1.3 %place_rewards.1 = bf16[2,18432]{1,0:T(2,128)(2,1)} custom-call(bf16[16,32]{1,0:T(8,128)(2,1)S(1)} %mul.45.chooser_ref, s32[16]{0:T(128)S(1)} %add_xor_fusion.position_ref, bf16[32,1152]{1,0:T(8,128)(2,1)S(1)} %pad_maximum_fusion.1.refs_0_, bf16[32,1152]{1,0:T(8,128)(2,1)S(1)} %collective-permute-done.20.refs_1_), custom_call_target="tpu_custom_call" | custom-call | tf_op jit(solution)/shard_map/place_rewards/pallas_call | solution.py:471
  (61 shorter events, 4.6 us)
Async XLA Ops:
  0.6 6.6 %collective-permute-start.2 = (bf16[128,1152]{1,0:T(8,128)(2,1)}, bf16[128,1152]{1,0:T(8,128)(2,1)S(1)}, u32[]{:S(2)}, u32[]{:S(2)}) collective-permute-start(bf16[128,1152]{1,0:T(8,128)(2,1)} %refs_0_.1), channel_id=1, source_target_pairs={{0,1},{1,0},{2,3},{3,2},{4,5},{5,4},{6,7},{7,6},{8,9},{9,8},{10,11... | collective-permute-start | bytes 884744 | tf_op jit(solution)/shard_map/ppermute | solution.py:129
  1.1 12.3 %collective-permute-start = (bf16[128,1152]{1,0:T(8,128)(2,1)}, bf16[128,1152]{1,0:T(8,128)(2,1)S(1)}, u32[]{:S(2)}, u32[]{:S(2)}) collective-permute-start(bf16[128,1152]{1,0:T(8,128)(2,1)} %refs_0_.1), channel_id=1, source_target_pairs={{0,2},{1,3},{2,0},{3,1},{4,6},{5,7},{6,4},{7,5},{8,10},{9,11},{10,... | collective-permute-start | bytes 884744 | tf_op jit(solution)/shard_map/ppermute | solution.py:129
  3.7 9.7 %collective-permute-start.1 = (bf16[128,1152]{1,0:T(8,128)(2,1)}, bf16[128,1152]{1,0:T(8,128)(2,1)S(1)}, u32[]{:S(2)}, u32[]{:S(2)}) collective-permute-start(bf16[128,1152]{1,0:T(8,128)(2,1)} %refs_0_.1), channel_id=1, source_target_pairs={{0,4},{1,5},{2,6},{3,7},{4,0},{5,1},{6,2},{7,3},{8,12},{9,13},{10,... | collective-permute-start | bytes 884744 | tf_op jit(solution)/shard_map/ppermute | solution.py:129
  13.4 1.8 %collective-permute-start.4 = (bf16[128,1152]{1,0:T(8,128)(2,1)S(1)}, bf16[128,1152]{1,0:T(8,128)(2,1)S(1)}, u32[]{:S(2)}, u32[]{:S(2)}) collective-permute-start(bf16[128,1152]{1,0:T(8,128)(2,1)S(1)} %collective-permute-done.refs_0_), channel_id=1, source_target_pairs={{0,1},{1,0},{2,3},{3,2},{4,5},{5,4},{6,7},{7,6},{8,9},{9,8},{10,11... | collective-permute-start | bytes 884744 | tf_op jit(solution)/shard_map/ppermute | solution.py:129
  13.5 2.0 %collective-permute-start.5 = (bf16[128,1152]{1,0:T(8,128)(2,1)S(1)}, bf16[128,1152]{1,0:T(8,128)(2,1)S(1)}, u32[]{:S(2)}, u32[]{:S(2)}) collective-permute-start(bf16[128,1152]{1,0:T(8,128)(2,1)S(1)} %collective-permute-done.1.refs_1_), channel_id=1, source_target_pairs={{0,1},{1,0},{2,3},{3,2},{4,5},{5,4},{6,7},{7,6},{8,9},{9,8},{10,11... | collective-permute-start | bytes 884744 | tf_op jit(solution)/shard_map/ppermute | solution.py:129
  14.1 11.0 %copy-start.1 = (s32[4]{0:T(128)S(1)}, s32[4]{0:T(128)}, u32[]{:S(2)}) copy-start(s32[4]{0:T(128)} %param.10) | copy-start | bytes 52
  14.1 10.8 %collective-permute-start.3 = (bf16[128,1152]{1,0:T(8,128)(2,1)}, bf16[128,1152]{1,0:T(8,128)(2,1)S(1)}, u32[]{:S(2)}, u32[]{:S(2)}) collective-permute-start(bf16[128,1152]{1,0:T(8,128)(2,1)} %refs_0_.1), channel_id=1, source_target_pairs={{0,6},{1,7},{2,4},{3,5},{4,2},{5,3},{6,0},{7,1},{8,14},{9,15},{10,... | collective-permute-start | bytes 884744 | tf_op jit(solution)/shard_map/ppermute | solution.py:129
  24.9 2.4 %collective-permute-start.6 = (bf16[128,1152]{1,0:T(8,128)(2,1)S(1)}, bf16[128,1152]{1,0:T(8,128)(2,1)S(1)}, u32[]{:S(2)}, u32[]{:S(2)}) collective-permute-start(bf16[128,1152]{1,0:T(8,128)(2,1)S(1)} %collective-permute-done.3.refs_0_), channel_id=1, source_target_pairs={{0,1},{1,0},{2,3},{3,2},{4,5},{5,4},{6,7},{7,6},{8,9},{9,8},{10,11... | collective-permute-start | bytes 884744 | tf_op jit(solution)/shard_map/ppermute | solution.py:129
  25.2 2.0 %copy-start = (s32[128]{0:T(128)S(1)}, s32[128]{0:T(128)}, u32[]{:S(2)}) copy-start(s32[128]{0:T(128)} %param.9) | copy-start | bytes 1540
  27.9 8.0 %collective-permute-start.7 = (bf16[64,384]{1,0:T(8,128)(2,1)S(1)}, bf16[64,384]{1,0:T(8,128)(2,1)S(1)}, u32[]{:S(2)}, u32[]{:S(2)}) collective-permute-start(bf16[64,384]{1,0:T(8,128)(2,1)S(1)} %get-tuple-element.64), channel_id=1, source_target_pairs={{0,8},{1,9},{2,10},{3,11},{4,12},{5,13},{6,14},{7,15},{8,0},{9,1},... | collective-permute-start | bytes 147464 | tf_op jit(solution)/shard_map/ppermute | solution.py:129
  36.4 15.2 %collective-permute-start.8 = (bf16[66,16,128]{2,1,0:T(8,128)(2,1)S(1)}, bf16[66,16,128]{2,1,0:T(8,128)(2,1)S(1)}, u32[]{:S(2)}, u32[]{:S(2)}) collective-permute-start(bf16[66,16,128]{2,1,0:T(8,128)(2,1)S(1)} %get-tuple-element.67), channel_id=1, source_target_pairs={{0,8},{1,9},{2,10},{3,11},{4,12},{5,13},{6,14},{7,15},{8,0},{9,1},... | collective-permute-start | bytes 811016 | tf_op jit(solution)/shard_map/ppermute | solution.py:129
  56.8 3.6 %collective-permute-start.9 = (bf16[144,1152]{1,0:T(8,128)(2,1)S(1)}, bf16[144,1152]{1,0:T(8,128)(2,1)S(1)}, u32[]{:S(2)}, u32[]{:S(2)}) collective-permute-start(bf16[144,1152]{1,0:T(8,128)(2,1)S(1)} %get-tuple-element.74), channel_id=1, source_target_pairs={{0,1},{1,0},{2,3},{3,2},{4,5},{5,4},{6,7},{7,6},{8,9},{9,8},{10,11... | collective-permute-start | bytes 995336 | tf_op jit(solution)/shard_map/ppermute | solution.py:129
  60.5 4.9 %collective-permute-start.10 = (bf16[144,1152]{1,0:T(8,128)(2,1)S(1)}, bf16[144,1152]{1,0:T(8,128)(2,1)S(1)}, u32[]{:S(2)}, u32[]{:S(2)}) collective-permute-start(bf16[144,1152]{1,0:T(8,128)(2,1)S(1)} %get-tuple-element.79), channel_id=1, source_target_pairs={{0,1},{1,0},{2,3},{3,2},{4,5},{5,4},{6,7},{7,6},{8,9},{9,8},{10,11... | collective-permute-start | bytes 995336 | tf_op jit(solution)/shard_map/ppermute | solution.py:129
  61.1 9.9 %collective-permute-start.13 = (bf16[128,1152]{1,0:T(8,128)(2,1)S(1)}, bf16[128,1152]{1,0:T(8,128)(2,1)S(1)}, u32[]{:S(2)}, u32[]{:S(2)}) collective-permute-start(bf16[128,1152]{1,0:T(8,128)(2,1)S(1)} %add_convert_fusion.3), channel_id=1, source_target_pairs={{0,6},{1,7},{2,4},{3,5},{4,2},{5,3},{6,0},{7,1},{8,14},{9,15},{10,... | collective-permute-start | bytes 884744 | tf_op jit(solution)/shard_map/ppermute | solution.py:129
  65.5 3.6 %collective-permute-start.11 = (bf16[144,1152]{1,0:T(8,128)(2,1)S(1)}, bf16[144,1152]{1,0:T(8,128)(2,1)S(1)}, u32[]{:S(2)}, u32[]{:S(2)}) collective-permute-start(bf16[144,1152]{1,0:T(8,128)(2,1)S(1)} %get-tuple-element.86), channel_id=1, source_target_pairs={{0,1},{1,0},{2,3},{3,2},{4,5},{5,4},{6,7},{7,6},{8,9},{9,8},{10,11... | collective-permute-start | bytes 995336 | tf_op jit(solution)/shard_map/ppermute | solution.py:129
  69.0 1.8 %collective-permute-start.12 = (bf16[144,1152]{1,0:T(8,128)(2,1)S(1)}, bf16[144,1152]{1,0:T(8,128)(2,1)S(1)}, u32[]{:S(2)}, u32[]{:S(2)}) collective-permute-start(bf16[144,1152]{1,0:T(8,128)(2,1)S(1)} %get-tuple-element.94), channel_id=1, source_target_pairs={{0,1},{1,0},{2,3},{3,2},{4,5},{5,4},{6,7},{7,6},{8,9},{9,8},{10,11... | collective-permute-start | bytes 995336 | tf_op jit(solution)/shard_map/ppermute | solution.py:129
  71.0 6.2 %collective-permute-start.16 = (bf16[16,1152]{1,0:T(8,128)(2,1)S(1)}, bf16[16,1152]{1,0:T(8,128)(2,1)S(1)}, u32[]{:S(2)}, u32[]{:S(2)}) collective-permute-start(bf16[16,1152]{1,0:T(8,128)(2,1)S(1)} %convert_element_type.128), channel_id=1, source_target_pairs={{0,6},{1,7},{2,4},{3,5},{4,2},{5,3},{6,0},{7,1},{8,14},{9,15},{10,... | collective-permute-start | bytes 110600 | tf_op jit(solution)/shard_map/ppermute | solution.py:129
  73.1 4.2 %collective-permute-start.15 = (bf16[16,1152]{1,0:T(8,128)(2,1)S(1)}, bf16[16,1152]{1,0:T(8,128)(2,1)S(1)}, u32[]{:S(2)}, u32[]{:S(2)}) collective-permute-start(bf16[16,1152]{1,0:T(8,128)(2,1)S(1)} %convert_element_type.128), channel_id=1, source_target_pairs={{0,4},{1,5},{2,6},{3,7},{4,0},{5,1},{6,2},{7,3},{8,12},{9,13},{10,... | collective-permute-start | bytes 110600 | tf_op jit(solution)/shard_map/ppermute | solution.py:129
  73.7 4.0 %collective-permute-start.14 = (bf16[16,1152]{1,0:T(8,128)(2,1)S(1)}, bf16[16,1152]{1,0:T(8,128)(2,1)S(1)}, u32[]{:S(2)}, u32[]{:S(2)}) collective-permute-start(bf16[16,1152]{1,0:T(8,128)(2,1)S(1)} %convert_element_type.128), channel_id=1, source_target_pairs={{0,2},{1,3},{2,0},{3,1},{4,6},{5,7},{6,4},{7,5},{8,10},{9,11},{10,... | collective-permute-start | bytes 110600 | tf_op jit(solution)/shard_map/ppermute | solution.py:129
  74.5 9.7 %collective-permute-start.18 = (bf16[128,1152]{1,0:T(8,128)(2,1)S(1)}, bf16[128,1152]{1,0:T(8,128)(2,1)S(1)}, u32[]{:S(2)}, u32[]{:S(2)}) collective-permute-start(bf16[128,1152]{1,0:T(8,128)(2,1)S(1)} %add_convert_fusion.1), channel_id=1, source_target_pairs={{0,4},{1,5},{2,6},{3,7},{4,0},{5,1},{6,2},{7,3},{8,12},{9,13},{10,... | collective-permute-start | bytes 884744 | tf_op jit(solution)/shard_map/ppermute | solution.py:129
  76.4 8.1 %collective-permute-start.19 = (bf16[128,1152]{1,0:T(8,128)(2,1)S(1)}, bf16[128,1152]{1,0:T(8,128)(2,1)S(1)}, u32[]{:S(2)}, u32[]{:S(2)}) collective-permute-start(bf16[128,1152]{1,0:T(8,128)(2,1)S(1)} %add_convert_fusion.2), channel_id=1, source_target_pairs={{0,2},{1,3},{2,0},{3,1},{4,6},{5,7},{6,4},{7,5},{8,10},{9,11},{10,... | collective-permute-start | bytes 884744 | tf_op jit(solution)/shard_map/ppermute | solution.py:129
  77.7 5.4 %collective-permute-start.17 = (bf16[16,1152]{1,0:T(8,128)(2,1)S(1)}, bf16[16,1152]{1,0:T(8,128)(2,1)S(1)}, u32[]{:S(2)}, u32[]{:S(2)}) collective-permute-start(bf16[16,1152]{1,0:T(8,128)(2,1)S(1)} %fusion.2), channel_id=1, source_target_pairs={{0,8},{1,9},{2,10},{3,11},{4,12},{5,13},{6,14},{7,15},{8,0},{9,1},... | collective-permute-start | bytes 110600 | tf_op jit(solution)/shard_map/ppermute | solution.py:129
  84.6 1.3 %collective-permute-start.20 = (bf16[32,1152]{1,0:T(8,128)(2,1)S(1)}, bf16[32,1152]{1,0:T(8,128)(2,1)S(1)}, u32[]{:S(2)}, u32[]{:S(2)}) collective-permute-start(bf16[32,1152]{1,0:T(8,128)(2,1)S(1)} %pad_maximum_fusion.1.refs_0_), channel_id=1, source_target_pairs={{0,1},{1,0},{2,3},{3,2},{4,5},{5,4},{6,7},{7,6},{8,9},{9,8},{10,11... | collective-permute-start | bytes 221192 | tf_op jit(solution)/shard_map/ppermute | solution.py:129
